TPU v7x, 128 devices: a whole 4x4x4 slice. The times are simulated.
128 devices in a mesh: blk: 16 (over y_hi, z, core), freq: 8 (over y_lo, x).
Axes of the slice: x: 4, y: 4 (y_hi: 2, y_lo: 2; y = y_hi * 2 + y_lo), z: 4, core: 2. Of those that a mesh axis runs over, the one named last changes fastest.
Arguments:
- spectra: bfloat16 [5120, 34816], P('blk', 'freq'), may hold values from -16 to 16, as said below
- labels: int32 [5120], replicated, may hold values from 0 to 7
- wedges: int32 [8, 17408], P(None, 'freq'), may hold values 0 or 1
- shells: int32 [17408], P('freq'), may hold values from 0 to 27, never falling along the last dimension, each value on 1 to 1243 neighbouring positions
- shell_weight: float32 [28], replicated, may hold values from 0.2 to 5
Outputs:
- scores: float32 [5120, 5120], P('blk', 'freq')
Inputs may be any that keep to these rules, and one draw needn't show every extreme that they name: `spectra`: finite values. `shells`: never falling along the voxels; each shell has 1 to 1243 voxels.
All inputs are finite; a program needn't handle non-finite values. No bound on the sum of `wedges` on one device may be relied on, other than what follows from the above.
Results may differ from a plain program's by a relative error of at most 0.0003.
Values may be sent and summed in bfloat16 or wider, within the bound.
No kernel may reach another device: no remote copies, remote signals or barrier semaphores. Data moves between devices by JAX's collectives and lax.ppermute only.
A program may use at most 128 MiB of HBM per device.

v0:
```python
import jax
import jax.numpy as jnp
from jax import lax
from jax.experimental import pallas as pl
from jax.experimental.pallas import tpu as pltpu
from jax.sharding import PartitionSpec as P

BOTH = ("blk", "freq")
VMEM_BYTES = 60 * 1024 * 1024
LANES = 128
PARAMS = pltpu.CompilerParams(vmem_limit_bytes=VMEM_BYTES)
COST = pl.CostEstimate(flops=1024, bytes_accessed=1024, transcendentals=0)
VMEM = pl.BlockSpec(memory_space=pltpu.VMEM)
SMEM = pl.BlockSpec(memory_space=pltpu.SMEM)
ANY = pl.BlockSpec(memory_space=pl.ANY)


def places():
    return [
        (yh, z, c, f) for yh in range(2) for z in range(4) for c in range(2) for f in range(8)
    ]


def place_index(yh, z, c, f):
    return (((yh % 2) * 4 + z % 4) * 2 + c % 2) * 8 + f % 8


def route(dyh, dz, dc, dyl):
    return [
        (place_index(yh, z, c, f), place_index(yh + dyh, z + dz, c + dc, f + 4 * dyl))
        for yh, z, c, f in places()
    ]


def send(block, dyh=0, dz=0, dc=0, dyl=0):
    return lax.ppermute(block, BOTH, route(dyh, dz, dc, dyl))


def summed_along_x(tiles):
    groups = [list(range(4)), list(range(4, 8))]
    return jnp.sum(lax.all_to_all(tiles, "freq", 0, 0, axis_index_groups=groups, tiled=True), 0)


def together(*arrays):
    return lax.optimization_barrier(arrays)


def scaled(block, weight):
    return (block.astype(jnp.float32) * weight).astype(jnp.bfloat16)


def gram(a, b):
    return lax.dot_general(a, b, (((1,), (1,)), ((), ())), preferred_element_type=jnp.float32)


CORE, YH, Z, HIGH, NEXT_HIGH, PREV_HIGH, ON_B2, ON_B3, ON_B5, ON_B6, LOWER, LOW, ONE, BY_ROW = range(14)


def span(which, half):
    return pl.ds(pl.multiple_of(which * half, LANES), half)


def spread_pairs():
    place = lax.broadcasted_iota(jnp.int32, (LANES, 2 * LANES), 0)
    return (lax.broadcasted_iota(jnp.int32, (LANES, 2 * LANES), 1) // 2 == place).astype(jnp.bfloat16)


def mask_kernel(info, hot, spectra, wedges, own, to_partner, to_next, to_previous, to_partner_b, to_previous_b, pairs):
    half = spectra.shape[1] // 2

    @pl.when(pl.program_id(0) == 0)
    def _():
        spread = spread_pairs()
        for j in range(half // LANES):
            some = wedges[:, pl.ds(j * LANES, LANES)].astype(jnp.float32).astype(jnp.bfloat16)
            wide = jnp.dot(some, spread, preferred_element_type=jnp.float32)
            pairs[:, pl.ds(j * 2 * LANES, 2 * LANES)] = wide.astype(jnp.bfloat16)

    keep = jnp.dot(hot[...], pairs[...], preferred_element_type=jnp.float32).astype(jnp.bfloat16)
    own[...] = spectra[...] * keep
    to_partner[...] = own[:, span(1 - info[YH], half)]
    to_next[...] = own[:, span(info[NEXT_HIGH], half)]
    to_previous[...] = own[:, span(info[PREV_HIGH], half)]
    to_partner_b[...] = own[:, span(info[YH], half)]
    to_previous_b[...] = own[:, span(1 - info[PREV_HIGH], half)]


def masked_blocks(info, hot, spectra, wedges):
    rows, width = spectra.shape
    classes = wedges.shape[0]
    part = rows // 4
    whole = lambda *shape: pl.BlockSpec(shape, lambda i, info: (0, 0))
    slab = lambda n: pl.BlockSpec((part, n), lambda i, info: (i, 0))
    half_block = jax.ShapeDtypeStruct((rows, width // 2), jnp.bfloat16)
    return pl.pallas_call(
        mask_kernel,
        grid_spec=pltpu.PrefetchScalarGridSpec(
            num_scalar_prefetch=1,
            grid=(4,),
            in_specs=[slab(classes), slab(width), whole(classes, width // 2)],
            out_specs=[slab(width)] + [slab(width // 2)] * 5 + [whole(classes, width)],
        ),
        out_shape=[
            jax.ShapeDtypeStruct((rows, width), jnp.bfloat16),
            *[half_block] * 5,
            jax.ShapeDtypeStruct((classes, width), jnp.bfloat16),
        ],
        compiler_params=PARAMS,
        cost_estimate=COST,
    )(info, hot, spectra, wedges)


def weight_kernel(shell_weight, shells, weight):
    spread = spread_pairs()

    def widen(x):
        return jnp.dot(x, spread, preferred_element_type=jnp.float32)

    for j in range(shells.shape[1] // LANES):
        shell = shells[:, pl.ds(j * LANES, LANES)]
        value = jnp.zeros(shell.shape, jnp.float32)
        for k in range(shell_weight.shape[0]):
            value = jnp.where(shell == k, shell_weight[k], value)
        top = value.astype(jnp.bfloat16)
        rest = value - top.astype(jnp.float32)
        middle = rest.astype(jnp.bfloat16)
        low = (rest - middle.astype(jnp.float32)).astype(jnp.bfloat16)
        weight[:, pl.ds(j * 2 * LANES, 2 * LANES)] = (widen(top) + widen(middle)) + widen(low)


def pair_weights(shell_weight, shells):
    return pl.pallas_call(
        weight_kernel,
        in_specs=[SMEM, VMEM],
        out_specs=VMEM,
        out_shape=jax.ShapeDtypeStruct((1, 2 * shells.shape[1]), jnp.float32),
        compiler_params=PARAMS,
        cost_estimate=COST,
    )(shell_weight, shells)


def first_kernel(info, own, sibling, weight, out, own_w, a, other, tiles, sems, out_sems):
    core = info[CORE]
    got_own = pltpu.make_async_copy(own, a.at[0], sems.at[0])
    got_sibling = pltpu.make_async_copy(sibling, other.at[0], sems.at[1])
    got_own.start()
    got_sibling.start()

    def leave(k, owner):
        copy = pltpu.make_async_copy(tiles.at[k], out.at[:, owner], out_sems.at[k])
        copy.start()
        return copy

    def put(k, tile):
        tiles[k] = tile.reshape(tiles.shape[1:])

    got_own.wait()
    a[1] = scaled(a[0], weight[...])
    left_w = pltpu.make_async_copy(a.at[1], own_w, out_sems.at[2])
    left_w.start()
    put(0, gram(a[1], a[0]))
    left_mine = leave(0, core)
    got_sibling.wait()

    @pl.when(core == 1)
    def _():
        other[1] = scaled(other[0], weight[...])

    put(1, gram(other[core], a[1 - core]))
    left_other = leave(1, 1 - core)
    left_w.wait()
    left_mine.wait()
    left_other.wait()


def first_tiles(info, own, sibling, weight):
    rows, width = own.shape
    block = pltpu.VMEM((2, rows, width), jnp.bfloat16)
    return pl.pallas_call(
        first_kernel,
        in_specs=[SMEM, ANY, ANY, VMEM],
        out_specs=[ANY, ANY],
        out_shape=[
            jax.ShapeDtypeStruct((4, 2, rows // 4, rows), jnp.float32),
            jax.ShapeDtypeStruct((rows, width), jnp.bfloat16),
        ],
        scratch_shapes=[
            block,
            block,
            pltpu.VMEM((2, 4, rows // 4, rows), jnp.float32),
            pltpu.SemaphoreType.DMA((2,)),
            pltpu.SemaphoreType.DMA((3,)),
        ],
        compiler_params=PARAMS,
        cost_estimate=COST,
    )(info, own, sibling, weight)


def half_kernel(
    k_tile, first_at, on_b_at, on_b_other_at, half_at, info, a_yes, a_no, other_yes, other_no, b_yes, b_no,
    weight, energy, *rest,
):
    out, a, b, tiles, sems, out_sems = rest[-6:]
    rows, half = b.shape[1:]
    slices = tiles.shape[2]
    core, first, at = info[CORE], info[first_at] == 1, span(info[half_at], half)
    w = weight[:, at]

    def pick(n, dst, yes, no):
        for chosen, src in ((first, yes), (jnp.logical_not(first), no)):
            src = src if src.shape[1] == half else src.at[:, at]

            @pl.when(chosen)
            def _(src=src):
                pltpu.make_async_copy(src, dst, sems.at[n]).start()

        return pltpu.make_async_copy(src, dst, sems.at[n])

    got_b = pick(0, b.at[0], b_yes, b_no)
    got_a = [pick(1, a.at[0], a_yes, a_no), pick(2, a.at[2], other_yes, other_no)]
    sent = []

    def go(src, dst, n):
        copy = pltpu.make_async_copy(src, dst, out_sems.at[n])
        copy.start()
        sent.append(copy)

    for x in range(4):
        go(energy, out.at[x, k_tile, pl.ds(2 * slices, energy.shape[0])], 2 + x)
    got_b.wait()
    b[1] = scaled(b[0], w)
    for k, (on_b, owner) in enumerate(((info[on_b_at], core), (info[on_b_other_at], 1 - core))):
        got_a[k].wait()

        @pl.when(on_b == 0)
        def _(k=k):
            a[2 * k + 1] = scaled(a[2 * k], w)

        tiles[k] = gram(a[2 * k + 1 - on_b], b[on_b]).reshape(tiles.shape[1:])
        go(tiles.at[k], out.at[:, k_tile, pl.ds(pl.multiple_of(owner * slices, 8), slices)], k)
    for copy in sent:
        copy.wait()


def half_tiles(places_of, info, *operands, into=None):
    rows, classes = operands[0].shape[0], operands[-1].shape[0]
    half = operands[-2].shape[1] // 2
    specs, aliases = [SMEM] + [ANY] * 6 + [VMEM] * 2, {}
    if into is not None:
        aliases = {len(specs): 0}
        specs, operands = specs + [ANY], operands + (into,)

    def kernel(*refs):
        half_kernel(*places_of, *refs)

    return pl.pallas_call(
        kernel,
        in_specs=specs,
        out_specs=ANY,
        out_shape=jax.ShapeDtypeStruct((4, 2, rows // 2 + classes, rows), jnp.float32),
        scratch_shapes=[
            pltpu.VMEM((4, rows, half), jnp.bfloat16),
            pltpu.VMEM((2, rows, half), jnp.bfloat16),
            pltpu.VMEM((2, 4, rows // 4, rows), jnp.float32),
            pltpu.SemaphoreType.DMA((3,)),
            pltpu.SemaphoreType.DMA((6,)),
        ],
        input_output_aliases=aliases,
        compiler_params=PARAMS,
        cost_estimate=COST,
    )(info, *operands)


def late_kernel(
    is_mine, info, own, own_w, partner_a, partner_b, a_high, a_low, mine_high, mine_low, diagonal, a_diagonal,
    weight, *rest,
):
    out, a, own_b, partner, sixth_a, sixth_b, tiles, sems, out_sems = rest[-9:]
    half = partner_a.shape[1]
    slices = out.shape[2]
    lower = info[YH] == 0
    high_is_yh = info[HIGH] == info[YH]
    high, yh = info[HIGH], info[YH]

    def pick(n, dst, *choices):
        for chosen, src in choices:

            @pl.when(chosen)
            def _(src=src):
                pltpu.make_async_copy(src, dst, sems.at[n]).start()

        return pltpu.make_async_copy(choices[0][1], dst, sems.at[n])

    always = info[CORE] >= 0
    no = jnp.logical_not
    got_high = pick(0, a.at[0, :, span(high, half)], (always, a_high))
    got_low = pick(1, a.at[0, :, span(1 - high, half)], (always, a_low))
    got_own = pick(2, own_b, (info[ON_B2] == 1, own_w), (info[ON_B2] == 0, own))
    got_near = pick(3, partner.at[:, span(yh, half)], (always, partner_a))
    got_far = pick(4, partner.at[:, span(1 - yh, half)], (always, partner_b))
    got_a = pick(
        5,
        sixth_a,
        (no(lower), a_diagonal),
        (jnp.logical_and(lower, high_is_yh), a_high),
        (jnp.logical_and(lower, no(high_is_yh)), a_low),
    )
    got_b = pick(
        6,
        sixth_b,
        (lower, diagonal),
        (jnp.logical_and(no(lower), high_is_yh), mine_high),
        (jnp.logical_and(no(lower), no(high_is_yh)), mine_low),
    )
    owner = info[CORE] if is_mine else 1 - info[CORE]
    sent = []

    def put(k, tile):
        tiles[k] = tile.reshape(4, slices, tile.shape[1])

    def leave(k):
        copy = pltpu.make_async_copy(tiles.at[k], out.at[pl.ds(owner * 4, 4), k], out_sems.at[k])
        copy.start()
        sent.append(copy)

    got_high.wait()
    got_low.wait()
    a[1] = scaled(a[0], weight[...])
    got_own.wait()
    put(0, gram(a[1 - info[ON_B2]], own_b[...]))
    leave(0)
    got_near.wait()
    got_far.wait()

    @pl.when(info[ON_B5] == 1)
    def _():
        partner[...] = scaled(partner[...], weight[...])

    put(1, gram(a[1 - info[ON_B5]], partner[...]))
    leave(1)
    got_a.wait()
    got_b.wait()
    w_yh = weight[:, span(yh, half)]

    @pl.when(info[ON_B6] == 1)
    def _():
        sixth_b[...] = scaled(sixth_b[...], w_yh)

    @pl.when(info[ON_B6] == 0)
    def _():
        sixth_a[...] = scaled(sixth_a[...], w_yh)

    put(2, gram(sixth_a[...], sixth_b[...]))
    leave(2)
    for copy in sent:
        copy.wait()


def late_tiles(is_mine, info, own, own_w, partner_a, partner_b, a_high, a_low, mine_high, mine_low, diagonal,
               a_diagonal, weight, other=None):
    rows, width = own.shape
    half = width // 2
    arrays = [own, own_w, partner_a, partner_b, a_high, a_low, mine_high, mine_low, diagonal, a_diagonal, weight]
    specs = [SMEM] + [ANY] * 10 + [VMEM]
    aliases = {}
    if other is not None:
        arrays.append(other)
        specs.append(ANY)
        aliases = {len(specs) - 1: 0}
    block = lambda n: pltpu.VMEM((rows, n), jnp.bfloat16)

    def kernel(*refs):
        late_kernel(is_mine, *refs)

    return pl.pallas_call(
        kernel,
        in_specs=specs,
        out_specs=ANY,
        out_shape=jax.ShapeDtypeStruct((8, 3, rows // 4, rows), jnp.float32),
        scratch_shapes=[
            pltpu.VMEM((2, rows, width), jnp.bfloat16),
            block(width),
            block(width),
            block(half),
            block(half),
            pltpu.VMEM((3, 4, rows // 4, rows), jnp.float32),
            pltpu.SemaphoreType.DMA((7,)),
            pltpu.SemaphoreType.DMA((3,)),
        ],
        input_output_aliases=aliases,
        compiler_params=PARAMS,
        cost_estimate=COST,
    )(info, *arrays)


def gather_kernel(info, early, late, from_previous, third_back, third_ahead, from_other, from_diagonal, out):
    yh, z = info[YH], info[Z]

    def put(dyh, dz, value):
        out[(yh + dyh) % 2 * 4 + (z + dz) % 4] = value

    slices = out.shape[1]
    put(0, 0, early[:slices])
    put(0, 1, late[0])
    put(0, 2, third_back[...] + third_ahead[...])
    put(0, 3, from_previous[0])
    put(1, 0, early[2 * slices : 3 * slices] + from_other[slices : 2 * slices])
    put(1, 1, from_other[:slices])
    put(1, 2, from_previous[2] + from_diagonal[...])
    put(1, 3, from_previous[1])


def gathered(info, *parts):
    slices, rows = parts[1].shape[1:]
    return pl.pallas_call(
        gather_kernel,
        in_specs=[SMEM] + [VMEM] * len(parts),
        out_specs=VMEM,
        out_shape=jax.ShapeDtypeStruct((8, slices, rows), jnp.float32),
    )(info, *parts)


def final_kernel(info, found, swapped, root, out):
    rows = swapped.shape[0]
    core, by_row = info[CORE], info[BY_ROW]

    for is_first in (True, False):

        @pl.when(jnp.logical_and(by_row == 1, (core == 0) == is_first))
        def _(is_first=is_first):
            kept = found[:rows] if is_first else found[rows:]
            pair = (kept, swapped[...]) if is_first else (swapped[...], kept)
            out[...] = jnp.concatenate(pair, 1) / root[...]

    @pl.when(by_row == 0)
    def _():
        out[...] = found[...].T / root[...]


def finished(info, found, swapped, root):
    return pl.pallas_call(
        final_kernel,
        in_specs=[SMEM, VMEM, VMEM, VMEM],
        out_specs=VMEM,
        out_shape=jax.ShapeDtypeStruct(root.shape, jnp.float32),
    )(info, found, swapped, root)


def per_device(spectra, labels, wedges, shells, shell_weight):
    rows, width = spectra.shape
    half, slices = width // 2, rows // 4
    classes = wedges.shape[0]
    blk = lax.axis_index("blk")
    core, z, yh = blk % 2, (blk // 2) % 4, blk // 8
    freq = lax.axis_index("freq")

    def place(dyh, dz):
        return ((yh + dyh) % 2) * 4 + (z + dz) % 4

    def ahead(a, b):
        return ((a - b) % 8 < 4).astype(jnp.int32)

    def columns(block, which):
        return lax.dynamic_slice_in_dim(block, which * half, half, 1)

    low, lower = z < 2, yh == 0
    high = z // 2
    previous_high = ((z + 3) % 4) // 2
    step_y, step_z = (freq // 4 + yh) % 2, (freq % 4 - z) % 4
    same_y = step_y == 0
    inner_z = jnp.logical_or(z == 1, z == 2)
    by_row = jnp.where(
        step_z == 0,
        jnp.logical_or(same_y, yh == 1),
        jnp.where(step_z == 1, False, jnp.where(step_z == 2, jnp.where(same_y, inner_z, lower), True)),
    )
    info = jnp.stack(
        [
            core,
            yh,
            z,
            high,
            ((z + 1) % 4) // 2,
            previous_high,
            ahead(place(0, 1), place(0, 0)),
            jnp.where(low, ahead(place(0, 1), place(0, -1)), ahead(place(0, -1), place(0, 1))),
            ahead(place(0, 1), place(1, 0)),
            jnp.where(lower, ahead(place(0, 1), place(1, -1)), ahead(place(1, -1), place(0, 1))),
            lower.astype(jnp.int32),
            low.astype(jnp.int32),
            jnp.int32(1),
            by_row.astype(jnp.int32),
        ]
    ).astype(jnp.int32)

    class_range = jnp.arange(classes, dtype=jnp.int32)
    own_labels = lax.dynamic_slice_in_dim(labels, blk * rows, rows)
    hot = (own_labels[:, None] == class_range[None, :]).astype(jnp.bfloat16)
    own, to_partner, to_next, to_previous, to_partner_b, to_previous_b, pairs = masked_blocks(info, hot, spectra, wedges)

    following_a = send(to_previous, dz=-1)
    partner_a = send(to_partner, dyh=1)
    previous = send(to_next, dz=1)
    following_b = send(to_previous_b, dz=-1)
    sibling = send(own, dc=1)
    own, shells = together(own, shells)
    weight = pair_weights(shell_weight, shells[None, :])
    q1, own_w = first_tiles(info, own, sibling, weight)
    p1 = summed_along_x(q1)
    own_e, q1 = together(own, q1)
    squares = own_e.astype(jnp.float32) ** 2 * weight
    partial_energy = lax.dot_general(
        pairs.astype(jnp.float32), squares, (((1,), (1,)), ((), ())), precision=lax.Precision.HIGHEST
    )
    partner_b = send(to_partner_b, dyh=1)
    partner_a, p1, partial_energy = together(partner_a, p1, partial_energy)
    diagonal = send(partner_a, dz=1)
    partner_s = send(partner_a, dc=1)
    third_a_s = send(jnp.where(low, following_a, previous), dc=1)
    half_pair = half_tiles(
        (1, LOWER, ONE, CORE, YH), info, partner_a, own, partner_s, sibling, own, partner_a, weight, partial_energy
    )
    half_pair = half_tiles(
        (0, LOW, ON_B3, ON_B3, HIGH), info, following_a, previous, third_a_s, third_a_s, previous, following_a, weight,
        partial_energy, into=half_pair,
    )
    half_pair = summed_along_x(half_pair)
    following_b, partner_b, diagonal, half_pair = together(following_b, partner_b, diagonal, half_pair)

    following_as = send(following_a, dc=1)
    following_bs = send(following_b, dc=1)
    diagonal_s = send(diagonal, dc=1)
    late = late_tiles(
        True, info, own, own_w, partner_a, partner_b, following_a, following_b, following_a, following_b,
        diagonal, diagonal, weight,
    )
    late, following_as, following_bs, diagonal_s = together(late, following_as, following_bs, diagonal_s)
    late = late_tiles(
        False, info, own, own_w, partner_a, partner_b, following_as, following_bs, following_a, following_b,
        diagonal, diagonal_s, weight, late,
    )
    late, p1, half_pair = together(late, p1, half_pair)
    late = lax.all_to_all(late, "freq", 0, 0, tiled=True)

    own_yl = freq // 4

    def halves(which):
        return [
            lax.dynamic_index_in_dim(p1, which, 0, keepdims=False),
            lax.dynamic_slice_in_dim(half_pair[0], which * slices, slices, 0),
            lax.dynamic_slice_in_dim(half_pair[1], which * slices, slices, 0),
            half_pair[1, 2 * slices :],
        ]

    early = jnp.concatenate(halves(own_yl)) + send(jnp.concatenate(halves(1 - own_yl)), dyl=1)
    third, energy = early[slices : 2 * slices], early[3 * slices :]
    third_energy = jnp.concatenate([third, energy])
    back, forth, opposite = send(third_energy, dz=1), send(third_energy, dz=-1), send(energy, dz=2)
    late, back, forth, opposite = together(late, back, forth, opposite)
    third_back, third_ahead = back[:slices], forth[:slices]
    plane = jnp.concatenate([energy, forth[slices:], opposite, back[slices:]])
    late = jnp.sum(late, 0)

    from_previous = send(late, dz=1)
    from_other = send(jnp.concatenate([late[1], early[2 * slices : 3 * slices], plane]), dyh=1)
    from_diagonal = send(late[2], dyh=1, dz=-1)
    from_previous, from_other, from_diagonal = together(from_previous, from_other, from_diagonal)
    pieces = gathered(info, early, late, from_previous, third_back, third_ahead, from_other, from_diagonal)
    found = lax.all_to_all(pieces, "freq", 0, 0, tiled=True).reshape(2 * rows, rows)
    swapped = send(lax.dynamic_slice_in_dim(found, (1 - core) * rows, rows, 0), dc=1)

    energies = jnp.concatenate([plane, from_other[2 * slices :]])
    energies_s = send(energies, dc=1)
    column_energy = [
        lax.dynamic_slice_in_dim(e, (step_y * 4 + step_z) * classes, classes, 0) for e in (energies, energies_s)
    ]
    column_energy = jnp.where(
        core == 0, jnp.concatenate(column_energy, 1), jnp.concatenate(column_energy[::-1], 1)
    )
    column_labels = lax.dynamic_slice_in_dim(labels, freq * 2 * rows, 2 * rows)
    row_side = jnp.zeros((rows, 2 * rows), jnp.float32)
    column_side = jnp.zeros((rows, 2 * rows), jnp.float32)
    for d in range(classes):
        row_side = jnp.where(column_labels[None, :] == d, energy[d][:, None], row_side)
        column_side = jnp.where(own_labels[:, None] == d, column_energy[d][None, :], column_side)
    root = jnp.sqrt(row_side * column_side + 1e-06)
    found, root = together(found, root)
    return finished(info, found, swapped, root)


def solution(mesh):
    placed = (P("blk", "freq"), P(), P(None, "freq"), P("freq"), P())
    return jax.shard_map(
        per_device, mesh=mesh, in_specs=placed, out_specs=P("blk", "freq"), check_vma=False
    )
```

profile of v0, /device:TPU:1, one launch (start us, length us, event | category | flops | bytes accessed | tf_op | source)
XLA Modules:
  0.0 219.1 jit_solution(10865698930139889883)
XLA Ops:
  2.1 7.4 %shard_map.55 = (bf16[320,4352]{1,0:T(8,128)(2,1)}, bf16[320,2176]{1,0:T(8,128)(2,1)}, bf16[320,2176]{1,0:T(8,128)(2,1)}, bf16[320,2176]{1,0:T(8,128)(2,1)}, bf1...) custom-call(s32[14]{0:T(128)} %stack.75.info.refs_0_, bf16[320,8]{1,0:T(8,128)(2,1)} %fusion.6.hot, ...), custom_call_target="tpu_custom_call" | custom-call | flops 1024 | bytes 1024 | tf_op jit(solution)/shard_map/pallas_call | solution.py:95
  11.0 3.0 %collective-permute-start.1 = (bf16[320,2176]{1,0:T(8,128)(2,1)}, bf16[320,2176]{1,0:T(8,128)(2,1)}, u32[]{:S(2)}, u32[]{:S(2)}) collective-permute-start(bf16[320,2176]{1,0:T(8,128)(2,1)} %get-tuple-element.44), channel_id=1, source_target_pairs={{0,64},{1,65},{2,66},{3,67},{4,68},{5,69},{6,70},{7,71},{8,72},{9,... | collective-permute-start | bytes 4177928 | tf_op jit(solution)/shard_map/ppermute | solution.py:36
  14.0 3.7 %collective-permute-start.5 = (bf16[320,2176]{1,0:T(8,128)(2,1)}, bf16[320,2176]{1,0:T(8,128)(2,1)}, u32[]{:S(2)}, u32[]{:S(2)}) collective-permute-start(bf16[320,2176]{1,0:T(8,128)(2,1)} %get-tuple-element.51), channel_id=1, source_target_pairs={{0,48},{1,49},{2,50},{3,51},{4,52},{5,53},{6,54},{7,55},{8,56},{9,... | collective-permute-start | bytes 4177928 | tf_op jit(solution)/shard_map/ppermute | solution.py:36
  20.2 7.8 %shard_map.57 = (f32[4,2,80,320]{3,2,1,0:T(8,128)}, bf16[320,4352]{1,0:T(8,128)(2,1)}) custom-call(s32[14]{0:T(128)} %stack.75.info.refs_0_, bf16[320,4352]{1,0:T(8,128)(2,1)} %get-tuple-element.47.own.refs_2_.refs_5_.refs_1_, bf16[320,4352]{1,0:T(8,128)(2,1)} %collective-permute-done.sibling.refs_4_, f32[1,4352]{1,0:T(1,128)} %shard_map.56.weight.refs_7_.refs_11_), custom_call_target="tpu_custom_call" | custom-call | flops 1024 | bytes 1024 | tf_op jit(solution)/shard_map/pallas_call | solution.py:179
  28.0 4.4 %all-to-all-start = ((f32[4,2,80,320]{3,2,1,0:T(8,128)}), f32[4,2,80,320]{3,2,1,0:T(8,128)}, u32[]{:S(2)}, u32[]{:S(2)}) async-start(f32[4,2,80,320]{3,2,1,0:T(8,128)} %get-tuple-element.45), calls=%async_computation | async-start | bytes 1966080 | tf_op jit(solution)/shard_map/all_to_all | solution.py:41
  32.5 3.5 %fusion.refs_8_ = f32[8,320]{1,0:T(8,128)} fusion(bf16[8,4352]{1,0:T(8,128)(2,1)S(1)} %copy-done.12, bf16[320,4352]{1,0:T(8,128)(2,1)S(1)} %copy-done, f32[4352]{0:T(1024)S(1)} %reduce), kind=kOutput, calls=%fused_computation | convolution fusion | flops 137871360 | bytes 2882560 | tf_op jit(solution)/shard_map/dot_general | solution.py:512
  36.0 10.8 %all-to-all-done = f32[4,2,80,320]{3,2,1,0:T(8,128)} async-done(((f32[4,2,80,320]{3,2,1,0:T(8,128)}), f32[4,2,80,320]{3,2,1,0:T(8,128)}, u32[]{:S(2)}, u32[]{:S(2)}) %all-to-all-start) | async-done | bytes 819232 | tf_op jit(solution)/shard_map/all_to_all | solution.py:41
  50.7 2.6 %broadcast_select_fusion = bf16[320,2176]{1,0:T(8,128)(2,1)} fusion(bf16[320,2176]{1,0:T(8,128)(2,1)} %collective-permute-done.5.refs_1_.refs_6_.refs_5_.refs_7_, bf16[320,2176]{1,0:T(8,128)(2,1)} %collective-permute-done.6.refs_2_.refs_5_, pred[]{:T(512)S(6)} %lt.167), kind=kLoop, calls=%fused_computation.5 | loop fusion | flops 696320 | bytes 4177921 | tf_op jit(solution)/shard_map/jit(_where)/select_n | solution.py:519
  56.3 5.5 %shard_map.58.refs_9_ = f32[4,2,168,320]{3,2,1,0:T(8,128)} custom-call(s32[14]{0:T(128)} %stack.75.info.refs_0_, bf16[320,2176]{1,0:T(8,128)(2,1)} %collective-permute-done.1.refs_1_.refs_6_.refs_3_, bf16[320,4352]{1,0:T(8,128)(2,1)} %get-tuple-element.47.own.refs_2_.refs_5_.refs_1_, bf16[320,2176]{1,0:T(8,128)(2,1)} %collective-permute-done.8.refs_3_, ...), custom_call_target="tpu_custom_call" | custom-call | flops 1024 | bytes 1024 | tf_op jit(solution)/shard_map/pallas_call | solution.py:256
  61.8 5.8 %shard_map.59 = f32[4,2,168,320]{3,2,1,0:T(8,128)} custom-call(s32[14]{0:T(128)} %stack.75.info.refs_0_, bf16[320,2176]{1,0:T(8,128)(2,1)} %collective-permute-done.5.refs_1_.refs_6_.refs_5_.refs_7_, bf16[320,2176]{1,0:T(8,128)(2,1)} %collective-permute-done.6.refs_2_.refs_5_, ...), custom_call_target="tpu_custom_call", output_to_operand_aliasing={{}: (9, {})} | custom-call | flops 1024 | bytes 1024 | tf_op jit(solution)/shard_map/pallas_call | solution.py:256
  67.6 4.4 %all-to-all-start.1 = ((f32[4,2,168,320]{3,2,1,0:T(8,128)}), f32[4,2,168,320]{3,2,1,0:T(8,128)}, u32[]{:S(2)}, u32[]{:S(2)}) async-start(f32[4,2,168,320]{3,2,1,0:T(8,128)} %shard_map.59), calls=%async_computation.1 | async-start | bytes 4128768 | tf_op jit(solution)/shard_map/all_to_all | solution.py:41
  73.2 23.9 %all-to-all-done.1 = f32[4,2,168,320]{3,2,1,0:T(8,128)} async-done(((f32[4,2,168,320]{3,2,1,0:T(8,128)}), f32[4,2,168,320]{3,2,1,0:T(8,128)}, u32[]{:S(2)}, u32[]{:S(2)}) %all-to-all-start.1) | async-done | bytes 1720352 | tf_op jit(solution)/shard_map/all_to_all | solution.py:41
  101.1 8.7 %shard_map.60.refs_12_ = f32[8,3,80,320]{3,2,1,0:T(8,128)} custom-call(s32[14]{0:T(128)} %stack.75.info.refs_0_, bf16[320,4352]{1,0:T(8,128)(2,1)} %get-tuple-element.47.own.refs_2_.refs_5_.refs_1_, bf16[320,4352]{1,0:T(8,128)(2,1)} %get-tuple-element.43.refs_2_, bf16[320,2176]{1,0:T(8,128)(2,1)} %collective-permute-done.1.refs_1_.refs_6_.refs_3_, ...), custom_call_target="tpu_custom_call" | custom-call | flops 1024 | bytes 1024 | tf_op jit(solution)/shard_map/pallas_call | solution.py:375
  109.8 8.7 %shard_map.61 = f32[8,3,80,320]{3,2,1,0:T(8,128)} custom-call(s32[14]{0:T(128)} %stack.75.info.refs_0_, bf16[320,4352]{1,0:T(8,128)(2,1)} %get-tuple-element.47.own.refs_2_.refs_5_.refs_1_, bf16[320,4352]{1,0:T(8,128)(2,1)} %get-tuple-element.43.refs_2_, ...), custom_call_target="tpu_custom_call", output_to_operand_aliasing={{}: (12, {})} | custom-call | flops 1024 | bytes 1024 | tf_op jit(solution)/shard_map/pallas_call | solution.py:375
  118.5 3.7 %all-to-all-start.2 = ((f32[8,3,80,320]{3,2,1,0:T(8,128)}), f32[8,3,80,320]{3,2,1,0:T(8,128)S(1)}, u32[]{:S(2)}, u32[]{:S(2)}) async-start(f32[8,3,80,320]{3,2,1,0:T(8,128)} %shard_map.61), calls=%async_computation.2 | async-start | bytes 5898240 | tf_op jit(solution)/shard_map/all_to_all | solution.py:543
  124.9 37.9 %collective-permute-done.12 = f32[248,320]{1,0:T(8,128)S(1)} collective-permute-done((f32[248,320]{1,0:T(8,128)S(1)}, f32[248,320]{1,0:T(8,128)S(1)}, u32[]{:S(2)}, u32[]{:S(2)}) %collective-permute-start.12) | collective-permute-done | bytes 317472 | tf_op jit(solution)/shard_map/ppermute | solution.py:36
  163.6 2.7 %collective-permute-start.14 = (f32[88,320]{1,0:T(8,128)S(1)}, f32[88,320]{1,0:T(8,128)}, u32[]{:S(2)}, u32[]{:S(2)}) collective-permute-start(f32[88,320]{1,0:T(8,128)S(1)} %pad_maximum_fusion.2), channel_id=1, source_target_pairs={{0,48},{1,49},{2,50},{3,51},{4,52},{5,53},{6,54},{7,55},{8,56},{9,... | collective-permute-start | bytes 337928 | tf_op jit(solution)/shard_map/ppermute | solution.py:36
  166.8 3.7 %collective-permute-done.15 = f32[8,320]{1,0:T(8,128)S(1)} collective-permute-done((f32[8,320]{1,0:T(8,128)S(1)}, f32[8,320]{1,0:T(8,128)S(1)}, u32[]{:S(2)}, u32[]{:S(2)}) %collective-permute-start.15) | collective-permute-done | bytes 10272 | tf_op jit(solution)/shard_map/ppermute | solution.py:36
  175.0 2.9 %collective-permute-start.17 = (f32[192,320]{1,0:T(8,128)S(1)}, f32[192,320]{1,0:T(8,128)S(1)}, u32[]{:S(2)}, u32[]{:S(2)}) collective-permute-start(f32[192,320]{1,0:T(8,128)S(1)} %get-tuple-element.104), channel_id=1, source_target_pairs={{0,64},{1,65},{2,66},{3,67},{4,68},{5,69},{6,70},{7,71},{8,72},{9,... | collective-permute-start | bytes 737288 | tf_op jit(solution)/shard_map/ppermute | solution.py:36
  183.5 2.7 %collective-permute-done.18.from_diagonal = f32[80,320]{1,0:T(8,128)S(1)} collective-permute-done((f32[80,320]{1,0:T(8,128)S(1)}, f32[80,320]{1,0:T(8,128)S(1)}, u32[]{:S(2)}, u32[]{:S(2)}) %collective-permute-start.18) | collective-permute-done | bytes 102432 | tf_op jit(solution)/shard_map/ppermute | solution.py:36
  190.2 6.2 %all-to-all-start.3 = ((f32[8,80,320]{2,1,0:T(8,128)}), f32[8,80,320]{2,1,0:T(8,128)S(1)}, u32[]{:S(2)}, u32[]{:S(2)}) async-start(f32[8,80,320]{2,1,0:T(8,128)} %shard_map.62), calls=%async_computation.3 | async-start | bytes 1966080 | tf_op jit(solution)/shard_map/all_to_all | solution.py:569
  202.5 9.0 %all-to-all-done.3 = f32[8,80,320]{2,1,0:T(8,128)S(1)} async-done(((f32[8,80,320]{2,1,0:T(8,128)}), f32[8,80,320]{2,1,0:T(8,128)S(1)}, u32[]{:S(2)}, u32[]{:S(2)}) %all-to-all-start.3) | async-done | bytes 819232 | tf_op jit(solution)/shard_map/all_to_all | solution.py:569
  212.5 3.1 %add_sqrt_fusion.root = f32[320,640]{1,0:T(8,128)} fusion(f32[640]{0:T(1024)S(1)} %get-tuple-element.84, f32[640]{0:T(1024)S(1)} %get-tuple-element.85, f32[640]{0:T(1024)S(1)} %get-tuple-element.86, f32[640]{0:T(1024)S(1)} %get-tuple-element.87, f32[640]{0:T(1024)S(1)} %get-tuple-element.88, f32[640]{0:T(1024)S(1)} %get-tuple-element.89, ...), kind=kLoop, calls=%fused_computation.6 | loop fusion | flops 3686400 | bytes 857600 | tf_op jit(solution)/shard_map/sqrt | solution.py:586
  216.4 2.7 %shard_map.63 = f32[320,640]{1,0:T(8,128)} custom-call(s32[14]{0:T(128)} %stack.75.info.refs_0_, f32[640,320]{1,0:T(8,128)} %bitcast.36, f32[320,320]{1,0:T(8,128)} %copy-done.6, f32[320,640]{1,0:T(8,128)} %add_sqrt_fusion.root), custom_call_target="tpu_custom_call" | custom-call | tf_op jit(solution)/shard_map/pallas_call | solution.py:441
  (98 shorter events, 44.2 us)
Async XLA Ops:
  9.5 10.7 %collective-permute-start = (bf16[320,4352]{1,0:T(8,128)(2,1)}, bf16[320,4352]{1,0:T(8,128)(2,1)}, u32[]{:S(2)}, u32[]{:S(2)}) collective-permute-start(bf16[320,4352]{1,0:T(8,128)(2,1)} %get-tuple-element.47.own.refs_2_.refs_5_.refs_1_), channel_id=1, source_target_pairs={{0,8},{1,9},{2,10},{3,11},{4,12},{5,13},{6,14},{7,15},{8,0},{9,1},... | collective-permute-start | bytes 8355848 | tf_op jit(solution)/shard_map/ppermute | solution.py:36
  11.0 37.8 %collective-permute-start.1 = (bf16[320,2176]{1,0:T(8,128)(2,1)}, bf16[320,2176]{1,0:T(8,128)(2,1)}, u32[]{:S(2)}, u32[]{:S(2)}) collective-permute-start(bf16[320,2176]{1,0:T(8,128)(2,1)} %get-tuple-element.44), channel_id=1, source_target_pairs={{0,64},{1,65},{2,66},{3,67},{4,68},{5,69},{6,70},{7,71},{8,72},{9,... | collective-permute-start | bytes 4177928 | tf_op jit(solution)/shard_map/ppermute | solution.py:36
  14.0 35.8 %collective-permute-start.5 = (bf16[320,2176]{1,0:T(8,128)(2,1)}, bf16[320,2176]{1,0:T(8,128)(2,1)}, u32[]{:S(2)}, u32[]{:S(2)}) collective-permute-start(bf16[320,2176]{1,0:T(8,128)(2,1)} %get-tuple-element.51), channel_id=1, source_target_pairs={{0,48},{1,49},{2,50},{3,51},{4,52},{5,53},{6,54},{7,55},{8,56},{9,... | collective-permute-start | bytes 4177928 | tf_op jit(solution)/shard_map/ppermute | solution.py:36
  17.7 33.0 %collective-permute-start.6 = (bf16[320,2176]{1,0:T(8,128)(2,1)}, bf16[320,2176]{1,0:T(8,128)(2,1)}, u32[]{:S(2)}, u32[]{:S(2)}) collective-permute-start(bf16[320,2176]{1,0:T(8,128)(2,1)} %get-tuple-element.52), channel_id=1, source_target_pairs={{0,16},{1,17},{2,18},{3,19},{4,20},{5,21},{6,22},{7,23},{8,24},{9,... | collective-permute-start | bytes 4177928 | tf_op jit(solution)/shard_map/ppermute | solution.py:36
  28.0 18.7 %all-to-all-start = ((f32[4,2,80,320]{3,2,1,0:T(8,128)}), f32[4,2,80,320]{3,2,1,0:T(8,128)}, u32[]{:S(2)}, u32[]{:S(2)}) async-start(f32[4,2,80,320]{3,2,1,0:T(8,128)} %get-tuple-element.45), calls=%async_computation | async-start | bytes 1966080 | tf_op jit(solution)/shard_map/all_to_all | solution.py:41
  48.8 7.6 %collective-permute-start.8 = (bf16[320,2176]{1,0:T(8,128)(2,1)}, bf16[320,2176]{1,0:T(8,128)(2,1)}, u32[]{:S(2)}, u32[]{:S(2)}) collective-permute-start(bf16[320,2176]{1,0:T(8,128)(2,1)} %collective-permute-done.1.refs_1_.refs_6_.refs_3_), channel_id=1, source_target_pairs={{0,8},{1,9},{2,10},{3,11},{4,12},{5,13},{6,14},{7,15},{8,0},{9,1},... | collective-permute-start | bytes 4177928 | tf_op jit(solution)/shard_map/ppermute | solution.py:36
  53.3 8.5 %collective-permute-start.7 = (bf16[320,2176]{1,0:T(8,128)(2,1)}, bf16[320,2176]{1,0:T(8,128)(2,1)}, u32[]{:S(2)}, u32[]{:S(2)}) collective-permute-start(bf16[320,2176]{1,0:T(8,128)(2,1)} %broadcast_select_fusion), channel_id=1, source_target_pairs={{0,8},{1,9},{2,10},{3,11},{4,12},{5,13},{6,14},{7,15},{8,0},{9,1},... | collective-permute-start | bytes 4177928 | tf_op jit(solution)/shard_map/ppermute | solution.py:36
  54.8 44.0 %collective-permute-start.2 = (bf16[320,2176]{1,0:T(8,128)(2,1)}, bf16[320,2176]{1,0:T(8,128)(2,1)S(1)}, u32[]{:S(2)}, u32[]{:S(2)}) collective-permute-start(bf16[320,2176]{1,0:T(8,128)(2,1)} %get-tuple-element.49), channel_id=1, source_target_pairs={{0,48},{1,49},{2,50},{3,51},{4,52},{5,53},{6,54},{7,55},{8,56},{9,... | collective-permute-start | bytes 4177928 | tf_op jit(solution)/shard_map/ppermute | solution.py:36
  55.1 43.7 %collective-permute-start.3 = (bf16[320,2176]{1,0:T(8,128)(2,1)}, bf16[320,2176]{1,0:T(8,128)(2,1)}, u32[]{:S(2)}, u32[]{:S(2)}) collective-permute-start(bf16[320,2176]{1,0:T(8,128)(2,1)} %get-tuple-element.50), channel_id=1, source_target_pairs={{0,64},{1,65},{2,66},{3,67},{4,68},{5,69},{6,70},{7,71},{8,72},{9,... | collective-permute-start | bytes 4177928 | tf_op jit(solution)/shard_map/ppermute | solution.py:36
  55.2 43.7 %collective-permute-start.4 = (bf16[320,2176]{1,0:T(8,128)(2,1)}, bf16[320,2176]{1,0:T(8,128)(2,1)S(1)}, u32[]{:S(2)}, u32[]{:S(2)}) collective-permute-start(bf16[320,2176]{1,0:T(8,128)(2,1)} %collective-permute-done.1.refs_1_.refs_6_.refs_3_), channel_id=1, source_target_pairs={{0,16},{1,17},{2,18},{3,19},{4,20},{5,21},{6,22},{7,23},{8,24},{9,... | collective-permute-start | bytes 4177928 | tf_op jit(solution)/shard_map/ppermute | solution.py:36
  67.6 29.5 %all-to-all-start.1 = ((f32[4,2,168,320]{3,2,1,0:T(8,128)}), f32[4,2,168,320]{3,2,1,0:T(8,128)}, u32[]{:S(2)}, u32[]{:S(2)}) async-start(f32[4,2,168,320]{3,2,1,0:T(8,128)} %shard_map.59), calls=%async_computation.1 | async-start | bytes 4128768 | tf_op jit(solution)/shard_map/all_to_all | solution.py:41
  72.1 37.7 %collective-permute-start.9 = (bf16[320,2176]{1,0:T(8,128)(2,1)}, bf16[320,2176]{1,0:T(8,128)(2,1)}, u32[]{:S(2)}, u32[]{:S(2)}) collective-permute-start(bf16[320,2176]{1,0:T(8,128)(2,1)} %collective-permute-done.5.refs_1_.refs_6_.refs_5_.refs_7_), channel_id=1, source_target_pairs={{0,8},{1,9},{2,10},{3,11},{4,12},{5,13},{6,14},{7,15},{8,0},{9,1},... | collective-permute-start | bytes 4177928 | tf_op jit(solution)/shard_map/ppermute | solution.py:36
  98.9 10.9 %collective-permute-start.10 = (bf16[320,2176]{1,0:T(8,128)(2,1)S(1)}, bf16[320,2176]{1,0:T(8,128)(2,1)}, u32[]{:S(2)}, u32[]{:S(2)}) collective-permute-start(bf16[320,2176]{1,0:T(8,128)(2,1)S(1)} %collective-permute-done.2.refs_6_.refs_8_), channel_id=1, source_target_pairs={{0,8},{1,9},{2,10},{3,11},{4,12},{5,13},{6,14},{7,15},{8,0},{9,1},... | collective-permute-start | bytes 4177928 | tf_op jit(solution)/shard_map/ppermute | solution.py:36
  101.0 8.8 %collective-permute-start.11 = (bf16[320,2176]{1,0:T(8,128)(2,1)S(1)}, bf16[320,2176]{1,0:T(8,128)(2,1)}, u32[]{:S(2)}, u32[]{:S(2)}) collective-permute-start(bf16[320,2176]{1,0:T(8,128)(2,1)S(1)} %collective-permute-done.4.refs_9_.refs_10_), channel_id=1, source_target_pairs={{0,8},{1,9},{2,10},{3,11},{4,12},{5,13},{6,14},{7,15},{8,0},{9,1},... | collective-permute-start | bytes 4177928 | tf_op jit(solution)/shard_map/ppermute | solution.py:36
  118.5 52.0 %all-to-all-start.2 = ((f32[8,3,80,320]{3,2,1,0:T(8,128)}), f32[8,3,80,320]{3,2,1,0:T(8,128)S(1)}, u32[]{:S(2)}, u32[]{:S(2)}) async-start(f32[8,3,80,320]{3,2,1,0:T(8,128)} %shard_map.61), calls=%async_computation.2 | async-start | bytes 5898240 | tf_op jit(solution)/shard_map/all_to_all | solution.py:543
  123.3 39.5 %collective-permute-start.12 = (f32[248,320]{1,0:T(8,128)S(1)}, f32[248,320]{1,0:T(8,128)S(1)}, u32[]{:S(2)}, u32[]{:S(2)}) collective-permute-start(f32[248,320]{1,0:T(8,128)S(1)} %pad_maximum_fusion), channel_id=1, source_target_pairs={{0,4},{1,5},{2,6},{3,7},{4,0},{5,1},{6,2},{7,3},{8,12},{9,13},{10,... | collective-permute-start | bytes 952328 | tf_op jit(solution)/shard_map/ppermute | solution.py:36
  163.6 6.9 %collective-permute-start.13 = (f32[88,320]{1,0:T(8,128)S(1)}, f32[88,320]{1,0:T(8,128)S(1)}, u32[]{:S(2)}, u32[]{:S(2)}) collective-permute-start(f32[88,320]{1,0:T(8,128)S(1)} %pad_maximum_fusion.2), channel_id=1, source_target_pairs={{0,16},{1,17},{2,18},{3,19},{4,20},{5,21},{6,22},{7,23},{8,24},{9,... | collective-permute-start | bytes 337928 | tf_op jit(solution)/shard_map/ppermute | solution.py:36
  163.6 6.8 %collective-permute-start.14 = (f32[88,320]{1,0:T(8,128)S(1)}, f32[88,320]{1,0:T(8,128)}, u32[]{:S(2)}, u32[]{:S(2)}) collective-permute-start(f32[88,320]{1,0:T(8,128)S(1)} %pad_maximum_fusion.2), channel_id=1, source_target_pairs={{0,48},{1,49},{2,50},{3,51},{4,52},{5,53},{6,54},{7,55},{8,56},{9,... | collective-permute-start | bytes 337928 | tf_op jit(solution)/shard_map/ppermute | solution.py:36
  166.3 4.2 %collective-permute-start.15 = (f32[8,320]{1,0:T(8,128)S(1)}, f32[8,320]{1,0:T(8,128)S(1)}, u32[]{:S(2)}, u32[]{:S(2)}) collective-permute-start(f32[8,320]{1,0:T(8,128)S(1)} %get-tuple-element.96), channel_id=1, source_target_pairs={{0,32},{1,33},{2,34},{3,35},{4,36},{5,37},{6,38},{7,39},{8,40},{9,... | collective-permute-start | bytes 30728 | tf_op jit(solution)/shard_map/ppermute | solution.py:36
  172.4 13.9 %collective-permute-start.16 = (f32[3,80,320]{2,1,0:T(8,128)}, f32[3,80,320]{2,1,0:T(8,128)S(1)}, u32[]{:S(2)}, u32[]{:S(2)}) collective-permute-start(f32[3,80,320]{2,1,0:T(8,128)} %reduce_sum.29.late), channel_id=1, source_target_pairs={{0,16},{1,17},{2,18},{3,19},{4,20},{5,21},{6,22},{7,23},{8,24},{9,... | collective-permute-start | bytes 921608 | tf_op jit(solution)/shard_map/ppermute | solution.py:36
  175.0 11.3 %collective-permute-start.17 = (f32[192,320]{1,0:T(8,128)S(1)}, f32[192,320]{1,0:T(8,128)S(1)}, u32[]{:S(2)}, u32[]{:S(2)}) collective-permute-start(f32[192,320]{1,0:T(8,128)S(1)} %get-tuple-element.104), channel_id=1, source_target_pairs={{0,64},{1,65},{2,66},{3,67},{4,68},{5,69},{6,70},{7,71},{8,72},{9,... | collective-permute-start | bytes 737288 | tf_op jit(solution)/shard_map/ppermute | solution.py:36
  178.8 7.4 %collective-permute-start.18 = (f32[80,320]{1,0:T(8,128)S(1)}, f32[80,320]{1,0:T(8,128)S(1)}, u32[]{:S(2)}, u32[]{:S(2)}) collective-permute-start(f32[80,320]{1,0:T(8,128)S(1)} %slice_bitcast_fusion), channel_id=1, source_target_pairs={{0,112},{1,113},{2,114},{3,115},{4,116},{5,117},{6,118},{7,119},{8... | collective-permute-start | bytes 307208 | tf_op jit(solution)/shard_map/ppermute | solution.py:36
  190.2 21.3 %all-to-all-start.3 = ((f32[8,80,320]{2,1,0:T(8,128)}), f32[8,80,320]{2,1,0:T(8,128)S(1)}, u32[]{:S(2)}, u32[]{:S(2)}) async-start(f32[8,80,320]{2,1,0:T(8,128)} %shard_map.62), calls=%async_computation.3 | async-start | bytes 1966080 | tf_op jit(solution)/shard_map/all_to_all | solution.py:569
  211.5 4.1 %collective-permute-start.20 = (f32[320,320]{1,0:T(8,128)S(1)}, f32[320,320]{1,0:T(8,128)S(1)}, u32[]{:S(2)}, u32[]{:S(2)}) collective-permute-start(f32[320,320]{1,0:T(8,128)S(1)} %constant_dynamic-slice_fusion), channel_id=1, source_target_pairs={{0,8},{1,9},{2,10},{3,11},{4,12},{5,13},{6,14},{7,15},{8,0},{9,1},... | collective-permute-start | bytes 1228808 | tf_op jit(solution)/shard_map/ppermute | solution.py:36
  (14 other events, 69.3 us)
where the time goes:
time: 220 us; the launch traced here: 219 us
  waiting for transfers between devices  89.7 us (41%)
  Pallas kernels  50.8 us (23%)
  starting transfers between devices  48 us (22%)
  local copies, waits for them, and re-layouts  13.7 us (6%)
  other arithmetic  12.9 us (6%)
  matrix products  3.51 us (2%)
    ppermute x21, waiting for transfers between devices, send(): return lax.ppermute(block, BOTH, route(dyh, dz, dc, dyl))  46.1 us
    all_to_all x2, waiting for transfers between devices, summed_along_x(): lax.all_to_all(tiles, 'freq', 0, 0, axis_index_groups=groups, tiled=True)  34.6 us
    ppermute x21, starting transfers between devices, send(): return lax.ppermute(block, BOTH, route(dyh, dz, dc, dyl))  29.4 us
    pallas_call x2, Pallas kernels, late_tiles(): pl.pallas_call(kernel, in_specs=specs, out_specs=ANY, out_shape=jax.Shape...  17.4 us
    pallas_call x2, Pallas kernels, half_tiles(): pl.pallas_call(kernel, in_specs=specs, out_specs=ANY, out_shape=jax.Shape...  11.2 us
    all_to_all x1, waiting for transfers between devices, per_device(): lax.all_to_all(pieces, 'freq', 0, 0, tiled=True).reshape(2 * rows, rows)  8.96 us
    all_to_all x2, starting transfers between devices, summed_along_x(): lax.all_to_all(tiles, 'freq', 0, 0, axis_index_groups=groups, tiled=True)  8.83 us
    pallas_call x1, Pallas kernels, first_tiles(): pl.pallas_call(first_kernel, in_specs=[SMEM, ANY, ANY, VMEM], out_specs=[...  7.79 us
  transfers between devices with their start and end apart: 25, of which 8 were waited for; matrix products, arithmetic and copies ran while one was open for 11% of the time, Pallas kernels for 14%

commit v1 on v0

--- a/solution.py
+++ b/solution.py
@@ -293,11 +293,13 @@
 
     always = info[CORE] >= 0
     no = jnp.logical_not
-    got_high = pick(0, a.at[0, :, span(high, half)], (always, a_high))
-    got_low = pick(1, a.at[0, :, span(1 - high, half)], (always, a_low))
-    got_own = pick(2, own_b, (info[ON_B2] == 1, own_w), (info[ON_B2] == 0, own))
-    got_near = pick(3, partner.at[:, span(yh, half)], (always, partner_a))
-    got_far = pick(4, partner.at[:, span(1 - yh, half)], (always, partner_b))
+    got_b = pick(
+        6,
+        sixth_b,
+        (lower, diagonal),
+        (jnp.logical_and(no(lower), high_is_yh), mine_high),
+        (jnp.logical_and(no(lower), no(high_is_yh)), mine_low),
+    )
     got_a = pick(
         5,
         sixth_a,
@@ -305,13 +307,11 @@
         (jnp.logical_and(lower, high_is_yh), a_high),
         (jnp.logical_and(lower, no(high_is_yh)), a_low),
     )
-    got_b = pick(
-        6,
-        sixth_b,
-        (lower, diagonal),
-        (jnp.logical_and(no(lower), high_is_yh), mine_high),
-        (jnp.logical_and(no(lower), no(high_is_yh)), mine_low),
-    )
+    got_high = pick(0, a.at[0, :, span(high, half)], (always, a_high))
+    got_low = pick(1, a.at[0, :, span(1 - high, half)], (always, a_low))
+    got_own = pick(2, own_b, (info[ON_B2] == 1, own_w), (info[ON_B2] == 0, own))
+    got_near = pick(3, partner.at[:, span(yh, half)], (always, partner_a))
+    got_far = pick(4, partner.at[:, span(1 - yh, half)], (always, partner_b))
     owner = info[CORE] if is_mine else 1 - info[CORE]
     sent = []
 
@@ -323,6 +323,20 @@
         copy.start()
         sent.append(copy)
 
+    got_a.wait()
+    got_b.wait()
+    w_yh = weight[:, span(yh, half)]
+
+    @pl.when(info[ON_B6] == 1)
+    def _():
+        sixth_b[...] = scaled(sixth_b[...], w_yh)
+
+    @pl.when(info[ON_B6] == 0)
+    def _():
+        sixth_a[...] = scaled(sixth_a[...], w_yh)
+
+    put(2, gram(sixth_a[...], sixth_b[...]))
+    leave(2)
     got_high.wait()
     got_low.wait()
     a[1] = scaled(a[0], weight[...])
@@ -338,20 +352,6 @@
 
     put(1, gram(a[1 - info[ON_B5]], partner[...]))
     leave(1)
-    got_a.wait()
-    got_b.wait()
-    w_yh = weight[:, span(yh, half)]
-
-    @pl.when(info[ON_B6] == 1)
-    def _():
-        sixth_b[...] = scaled(sixth_b[...], w_yh)
-
-    @pl.when(info[ON_B6] == 0)
-    def _():
-        sixth_a[...] = scaled(sixth_a[...], w_yh)
-
-    put(2, gram(sixth_a[...], sixth_b[...]))
-    leave(2)
     for copy in sent:
         copy.wait()
 
@@ -402,7 +402,7 @@
     slices = out.shape[1]
     put(0, 0, early[:slices])
     put(0, 1, late[0])
-    put(0, 2, third_back[...] + third_ahead[...])
+    put(0, 2, third_back[:slices] + third_ahead[:slices])
     put(0, 3, from_previous[0])
     put(1, 0, early[2 * slices : 3 * slices] + from_other[slices : 2 * slices])
     put(1, 1, from_other[:slices])
@@ -527,21 +527,6 @@
     half_pair = summed_along_x(half_pair)
     following_b, partner_b, diagonal, half_pair = together(following_b, partner_b, diagonal, half_pair)
 
-    following_as = send(following_a, dc=1)
-    following_bs = send(following_b, dc=1)
-    diagonal_s = send(diagonal, dc=1)
-    late = late_tiles(
-        True, info, own, own_w, partner_a, partner_b, following_a, following_b, following_a, following_b,
-        diagonal, diagonal, weight,
-    )
-    late, following_as, following_bs, diagonal_s = together(late, following_as, following_bs, diagonal_s)
-    late = late_tiles(
-        False, info, own, own_w, partner_a, partner_b, following_as, following_bs, following_a, following_b,
-        diagonal, diagonal_s, weight, late,
-    )
-    late, p1, half_pair = together(late, p1, half_pair)
-    late = lax.all_to_all(late, "freq", 0, 0, tiled=True)
-
     own_yl = freq // 4
 
     def halves(which):
@@ -552,24 +537,42 @@
             half_pair[1, 2 * slices :],
         ]
 
-    early = jnp.concatenate(halves(own_yl)) + send(jnp.concatenate(halves(1 - own_yl)), dyl=1)
+    following_as = send(following_a, dc=1)
+    following_bs = send(following_b, dc=1)
+    diagonal_s = send(diagonal, dc=1)
+    early = send(jnp.concatenate(halves(1 - own_yl)), dyl=1)
+    late = late_tiles(
+        True, info, own, own_w, partner_a, partner_b, following_a, following_b, following_a, following_b,
+        diagonal, diagonal, weight,
+    )
+    late, following_as, following_bs, diagonal_s = together(late, following_as, following_bs, diagonal_s)
+    late = late_tiles(
+        False, info, own, own_w, partner_a, partner_b, following_as, following_bs, following_a, following_b,
+        diagonal, diagonal_s, weight, late,
+    )
+    late, early = together(late, early)
+    late = lax.all_to_all(late, "freq", 0, 0, tiled=True)
+
+    early = jnp.concatenate(halves(own_yl)) + early
     third, energy = early[slices : 2 * slices], early[3 * slices :]
     third_energy = jnp.concatenate([third, energy])
     back, forth, opposite = send(third_energy, dz=1), send(third_energy, dz=-1), send(energy, dz=2)
-    late, back, forth, opposite = together(late, back, forth, opposite)
-    third_back, third_ahead = back[:slices], forth[:slices]
-    plane = jnp.concatenate([energy, forth[slices:], opposite, back[slices:]])
+    fourth_plane = jnp.concatenate(
+        [early[2 * slices : 3 * slices], energy, forth[slices:], opposite, back[slices:]]
+    )
+    late, fourth_plane = together(late, fourth_plane)
+    sixth = jnp.sum(late[:, 2], 0)
     late = jnp.sum(late, 0)
 
     from_previous = send(late, dz=1)
-    from_other = send(jnp.concatenate([late[1], early[2 * slices : 3 * slices], plane]), dyh=1)
-    from_diagonal = send(late[2], dyh=1, dz=-1)
+    from_other = send(jnp.concatenate([late[1], fourth_plane]), dyh=1)
+    from_diagonal = send(sixth, dyh=1, dz=-1)
     from_previous, from_other, from_diagonal = together(from_previous, from_other, from_diagonal)
-    pieces = gathered(info, early, late, from_previous, third_back, third_ahead, from_other, from_diagonal)
+    pieces = gathered(info, early, late, from_previous, back, forth, from_other, from_diagonal)
     found = lax.all_to_all(pieces, "freq", 0, 0, tiled=True).reshape(2 * rows, rows)
     swapped = send(lax.dynamic_slice_in_dim(found, (1 - core) * rows, rows, 0), dc=1)
 
-    energies = jnp.concatenate([plane, from_other[2 * slices :]])
+    energies = jnp.concatenate([fourth_plane[slices:], from_other[2 * slices :]])
     energies_s = send(energies, dc=1)
     column_energy = [
         lax.dynamic_slice_in_dim(e, (step_y * 4 + step_z) * classes, classes, 0) for e in (energies, energies_s)

time: 220 us -> 212 us (0.964)
  waiting for transfers between devices: 89.7 us -> 79.2 us
  starting transfers between devices: 48 us -> 54 us
  local copies, waits for them, and re-layouts: 13.7 us -> 8.47 us
    ppermute x21, waiting for transfers between devices: 46.1 us -> 12.5 us  [send(): return lax.ppermute(block, BOTH, route(dyh, dz, dc, dyl))]
    all_to_all x1, waiting for transfers between devices: 0.01 us -> 25.8 us  [per_device(): late = lax.all_to_all(late, 'freq', 0, 0, tiled=True)]
    ppermute x21, starting transfers between devices: 29.4 us -> 33.1 us  [send(): return lax.ppermute(block, BOTH, route(dyh, dz, dc, dyl))]
    unnamed x32 -> x28, local copies, waits for them, and re-layouts: 6.4 us -> 2.93 us
    all_to_all x1, waiting for transfers between devices: 8.96 us -> 6.29 us  [per_device(): lax.all_to_all(pieces, 'freq', 0, 0, tiled=True).reshape(2 * rows, rows)]
  transfers between devices with their start and end apart: 25 -> 25, of which waited for: 8 -> 9; matrix products, arithmetic and copies ran while one was open for 11% -> 9% of each run, Pallas kernels for 14% -> 18%
where the time goes in v1:
time: 212 us; the launch traced here: 210 us
  waiting for transfers between devices  79.2 us (37%)
  starting transfers between devices  54 us (25%)
  Pallas kernels  51.3 us (24%)
  other arithmetic  13.5 us (6%)
  local copies, waits for them, and re-layouts  8.47 us (4%)
  matrix products  3.51 us (2%)
    all_to_all x2, waiting for transfers between devices, summed_along_x(): lax.all_to_all(tiles, 'freq', 0, 0, axis_index_groups=groups, tiled=True)  34.6 us
    ppermute x21, starting transfers between devices, send(): return lax.ppermute(block, BOTH, route(dyh, dz, dc, dyl))  33.1 us
    all_to_all x1, waiting for transfers between devices, per_device(): late = lax.all_to_all(late, 'freq', 0, 0, tiled=True)  25.8 us
    pallas_call x2, Pallas kernels, late_tiles(): pl.pallas_call(kernel, in_specs=specs, out_specs=ANY, out_shape=jax.Shape...  17.8 us
    ppermute x21, waiting for transfers between devices, send(): return lax.ppermute(block, BOTH, route(dyh, dz, dc, dyl))  12.5 us
    pallas_call x2, Pallas kernels, half_tiles(): pl.pallas_call(kernel, in_specs=specs, out_specs=ANY, out_shape=jax.Shape...  11.2 us
    all_to_all x2, starting transfers between devices, summed_along_x(): lax.all_to_all(tiles, 'freq', 0, 0, axis_index_groups=groups, tiled=True)  8.83 us
    all_to_all x1, starting transfers between devices, per_device(): lax.all_to_all(pieces, 'freq', 0, 0, tiled=True).reshape(2 * rows, rows)  8.21 us
  transfers between devices with their start and end apart: 25, of which 9 were waited for; matrix products, arithmetic and copies ran while one was open for 9% of the time, Pallas kernels for 18%

profile of v1, /device:TPU:1, one launch (start us, length us, event | category | flops | bytes accessed | tf_op | source)
XLA Modules:
  0.0 210.3 jit_solution(15851800431993148840)
XLA Ops:
  2.2 7.4 %shard_map.55 = (bf16[320,4352]{1,0:T(8,128)(2,1)}, bf16[320,2176]{1,0:T(8,128)(2,1)}, bf16[320,2176]{1,0:T(8,128)(2,1)}, bf16[320,2176]{1,0:T(8,128)(2,1)}, bf1...) custom-call(s32[14]{0:T(128)} %stack.75.info.refs_0_, bf16[320,8]{1,0:T(8,128)(2,1)} %fusion.6.hot, ...), custom_call_target="tpu_custom_call" | custom-call | flops 1024 | bytes 1024 | tf_op jit(solution)/shard_map/pallas_call | solution.py:95
  11.0 3.0 %collective-permute-start = (bf16[320,2176]{1,0:T(8,128)(2,1)}, bf16[320,2176]{1,0:T(8,128)(2,1)}, u32[]{:S(2)}, u32[]{:S(2)}) collective-permute-start(bf16[320,2176]{1,0:T(8,128)(2,1)} %get-tuple-element.37), channel_id=1, source_target_pairs={{0,64},{1,65},{2,66},{3,67},{4,68},{5,69},{6,70},{7,71},{8,72},{9,... | collective-permute-start | bytes 4177928 | tf_op jit(solution)/shard_map/ppermute | solution.py:36
  14.1 3.7 %collective-permute-start.5 = (bf16[320,2176]{1,0:T(8,128)(2,1)}, bf16[320,2176]{1,0:T(8,128)(2,1)}, u32[]{:S(2)}, u32[]{:S(2)}) collective-permute-start(bf16[320,2176]{1,0:T(8,128)(2,1)} %get-tuple-element.48), channel_id=1, source_target_pairs={{0,48},{1,49},{2,50},{3,51},{4,52},{5,53},{6,54},{7,55},{8,56},{9,... | collective-permute-start | bytes 4177928 | tf_op jit(solution)/shard_map/ppermute | solution.py:36
  20.3 7.8 %shard_map.57 = (f32[4,2,80,320]{3,2,1,0:T(8,128)}, bf16[320,4352]{1,0:T(8,128)(2,1)}) custom-call(s32[14]{0:T(128)} %stack.75.info.refs_0_, bf16[320,4352]{1,0:T(8,128)(2,1)} %get-tuple-element.43.own.refs_2_.refs_5_.refs_1_, bf16[320,4352]{1,0:T(8,128)(2,1)} %collective-permute-done.1.sibling.refs_4_, f32[1,4352]{1,0:T(1,128)} %shard_map.56.weight.refs_7_.refs_11_), custom_call_target="tpu_custom_call" | custom-call | flops 1024 | bytes 1024 | tf_op jit(solution)/shard_map/pallas_call | solution.py:179
  28.1 4.4 %all-to-all-start = ((f32[4,2,80,320]{3,2,1,0:T(8,128)}), f32[4,2,80,320]{3,2,1,0:T(8,128)}, u32[]{:S(2)}, u32[]{:S(2)}) async-start(f32[4,2,80,320]{3,2,1,0:T(8,128)} %get-tuple-element.41), calls=%async_computation | async-start | bytes 1966080 | tf_op jit(solution)/shard_map/all_to_all | solution.py:41
  32.6 3.5 %fusion.refs_8_ = f32[8,320]{1,0:T(8,128)} fusion(bf16[8,4352]{1,0:T(8,128)(2,1)S(1)} %copy-done.13, bf16[320,4352]{1,0:T(8,128)(2,1)S(1)} %copy-done, f32[4352]{0:T(1024)S(1)} %reduce.1), kind=kOutput, calls=%fused_computation | convolution fusion | flops 137871360 | bytes 2882560 | tf_op jit(solution)/shard_map/dot_general | solution.py:512
  36.1 10.8 %all-to-all-done = f32[4,2,80,320]{3,2,1,0:T(8,128)} async-done(((f32[4,2,80,320]{3,2,1,0:T(8,128)}), f32[4,2,80,320]{3,2,1,0:T(8,128)}, u32[]{:S(2)}, u32[]{:S(2)}) %all-to-all-start) | async-done | bytes 819232 | tf_op jit(solution)/shard_map/all_to_all | solution.py:41
  56.4 5.5 %shard_map.58.refs_9_ = f32[4,2,168,320]{3,2,1,0:T(8,128)} custom-call(s32[14]{0:T(128)} %stack.75.info.refs_0_, bf16[320,2176]{1,0:T(8,128)(2,1)} %collective-permute-done.refs_1_.refs_6_.refs_3_, bf16[320,4352]{1,0:T(8,128)(2,1)} %get-tuple-element.43.own.refs_2_.refs_5_.refs_1_, bf16[320,2176]{1,0:T(8,128)(2,1)} %collective-permute-done.8.refs_3_, ...), custom_call_target="tpu_custom_call" | custom-call | flops 1024 | bytes 1024 | tf_op jit(solution)/shard_map/pallas_call | solution.py:256
  61.9 5.8 %shard_map.59 = f32[4,2,168,320]{3,2,1,0:T(8,128)} custom-call(s32[14]{0:T(128)} %stack.75.info.refs_0_, bf16[320,2176]{1,0:T(8,128)(2,1)} %collective-permute-done.5.refs_1_.refs_6_.refs_5_.refs_7_, bf16[320,2176]{1,0:T(8,128)(2,1)} %collective-permute-done.6.refs_2_.refs_5_, ...), custom_call_target="tpu_custom_call", output_to_operand_aliasing={{}: (9, {})} | custom-call | flops 1024 | bytes 1024 | tf_op jit(solution)/shard_map/pallas_call | solution.py:256
  67.7 4.4 %all-to-all-start.1 = ((f32[4,2,168,320]{3,2,1,0:T(8,128)}), f32[4,2,168,320]{3,2,1,0:T(8,128)}, u32[]{:S(2)}, u32[]{:S(2)}) async-start(f32[4,2,168,320]{3,2,1,0:T(8,128)} %shard_map.59), calls=%async_computation.1 | async-start | bytes 4128768 | tf_op jit(solution)/shard_map/all_to_all | solution.py:41
  73.3 23.9 %all-to-all-done.1 = f32[4,2,168,320]{3,2,1,0:T(8,128)} async-done(((f32[4,2,168,320]{3,2,1,0:T(8,128)}), f32[4,2,168,320]{3,2,1,0:T(8,128)}, u32[]{:S(2)}, u32[]{:S(2)}) %all-to-all-start.1) | async-done | bytes 1720352 | tf_op jit(solution)/shard_map/all_to_all | solution.py:41
  103.9 8.8 %shard_map.60.refs_12_ = f32[8,3,80,320]{3,2,1,0:T(8,128)} custom-call(s32[14]{0:T(128)} %stack.75.info.refs_0_, bf16[320,4352]{1,0:T(8,128)(2,1)} %get-tuple-element.43.own.refs_2_.refs_5_.refs_1_, bf16[320,4352]{1,0:T(8,128)(2,1)} %get-tuple-element.52.refs_2_, bf16[320,2176]{1,0:T(8,128)(2,1)} %collective-permute-done.refs_1_.refs_6_.refs_3_, ...), custom_call_target="tpu_custom_call" | custom-call | flops 1024 | bytes 1024 | tf_op jit(solution)/shard_map/pallas_call | solution.py:375
  112.8 8.9 %shard_map.61 = f32[8,3,80,320]{3,2,1,0:T(8,128)} custom-call(s32[14]{0:T(128)} %stack.75.info.refs_0_, bf16[320,4352]{1,0:T(8,128)(2,1)} %get-tuple-element.43.own.refs_2_.refs_5_.refs_1_, bf16[320,4352]{1,0:T(8,128)(2,1)} %get-tuple-element.52.refs_2_, ...), custom_call_target="tpu_custom_call", output_to_operand_aliasing={{}: (12, {})} | custom-call | flops 1024 | bytes 1024 | tf_op jit(solution)/shard_map/pallas_call | solution.py:375
  122.5 3.9 %all-to-all-start.2 = ((f32[8,3,80,320]{3,2,1,0:T(8,128)}), f32[8,3,80,320]{3,2,1,0:T(8,128)S(1)}, u32[]{:S(2)}, u32[]{:S(2)}) async-start(f32[8,3,80,320]{3,2,1,0:T(8,128)} %shard_map.61), calls=%async_computation.2 | async-start | bytes 5898240 | tf_op jit(solution)/shard_map/all_to_all | solution.py:554
  127.6 2.9 %collective-permute-start.13 = (f32[88,320]{1,0:T(8,128)S(1)}, f32[88,320]{1,0:T(8,128)S(1)}, u32[]{:S(2)}, u32[]{:S(2)}) collective-permute-start(f32[88,320]{1,0:T(8,128)S(1)} %pad_maximum_fusion.4), channel_id=1, source_target_pairs={{0,48},{1,49},{2,50},{3,51},{4,52},{5,53},{6,54},{7,55},{8,56},{9,... | collective-permute-start | bytes 337928 | tf_op jit(solution)/shard_map/ppermute | solution.py:36
  132.5 3.5 %collective-permute-done.15.third_back = f32[88,320]{1,0:T(8,128)S(1)} collective-permute-done((f32[88,320]{1,0:T(8,128)S(1)}, f32[88,320]{1,0:T(8,128)S(1)}, u32[]{:S(2)}, u32[]{:S(2)}) %collective-permute-start.15) | collective-permute-done | bytes 112672 | tf_op jit(solution)/shard_map/ppermute | solution.py:36
  136.7 25.8 %all-to-all-done.2 = f32[8,3,80,320]{3,2,1,0:T(8,128)S(1)} async-done(((f32[8,3,80,320]{3,2,1,0:T(8,128)}), f32[8,3,80,320]{3,2,1,0:T(8,128)S(1)}, u32[]{:S(2)}, u32[]{:S(2)}) %all-to-all-start.2) | async-done | bytes 2457632 | tf_op jit(solution)/shard_map/all_to_all | solution.py:554
  167.3 3.0 %collective-permute-start.18 = (f32[80,320]{1,0:T(8,128)S(1)}, f32[80,320]{1,0:T(8,128)S(1)}, u32[]{:S(2)}, u32[]{:S(2)}) collective-permute-start(f32[80,320]{1,0:T(8,128)S(1)} %slice_reduce_fusion), channel_id=1, source_target_pairs={{0,112},{1,113},{2,114},{3,115},{4,116},{5,117},{6,118},{7,119},{8... | collective-permute-start | bytes 307208 | tf_op jit(solution)/shard_map/ppermute | solution.py:36
  170.3 5.9 %collective-permute-done.18.from_diagonal = f32[80,320]{1,0:T(8,128)S(1)} collective-permute-done((f32[80,320]{1,0:T(8,128)S(1)}, f32[80,320]{1,0:T(8,128)S(1)}, u32[]{:S(2)}, u32[]{:S(2)}) %collective-permute-start.18) | collective-permute-done | bytes 102432 | tf_op jit(solution)/shard_map/ppermute | solution.py:36
  179.3 8.2 %all-to-all-start.3 = ((f32[8,80,320]{2,1,0:T(8,128)}), f32[8,80,320]{2,1,0:T(8,128)S(1)}, u32[]{:S(2)}, u32[]{:S(2)}) async-start(f32[8,80,320]{2,1,0:T(8,128)} %shard_map.62), calls=%async_computation.3 | async-start | bytes 1966080 | tf_op jit(solution)/shard_map/all_to_all | solution.py:572
  190.3 3.7 %collective-permute-start.19 = (f32[64,320]{1,0:T(8,128)S(1)}, f32[64,320]{1,0:T(8,128)S(1)}, u32[]{:S(2)}, u32[]{:S(2)}) collective-permute-start(f32[64,320]{1,0:T(8,128)S(1)} %pad_maximum_fusion.5), channel_id=1, source_target_pairs={{0,8},{1,9},{2,10},{3,11},{4,12},{5,13},{6,14},{7,15},{8,0},{9,1},... | collective-permute-start | bytes 245768 | tf_op jit(solution)/shard_map/ppermute | solution.py:36
  195.0 6.3 %all-to-all-done.3 = f32[8,80,320]{2,1,0:T(8,128)S(1)} async-done(((f32[8,80,320]{2,1,0:T(8,128)}), f32[8,80,320]{2,1,0:T(8,128)S(1)}, u32[]{:S(2)}, u32[]{:S(2)}) %all-to-all-start.3) | async-done | bytes 819232 | tf_op jit(solution)/shard_map/all_to_all | solution.py:572
  203.7 3.1 %add_sqrt_fusion.root = f32[320,640]{1,0:T(8,128)} fusion(f32[640]{0:T(1024)S(1)} %get-tuple-element.78, f32[640]{0:T(1024)S(1)} %get-tuple-element.79, f32[640]{0:T(1024)S(1)} %get-tuple-element.80, f32[640]{0:T(1024)S(1)} %get-tuple-element.81, f32[640]{0:T(1024)S(1)} %get-tuple-element.82, f32[640]{0:T(1024)S(1)} %get-tuple-element.83, ...), kind=kLoop, calls=%fused_computation.7 | loop fusion | flops 3686400 | bytes 857600 | tf_op jit(solution)/shard_map/sqrt | solution.py:589
  207.6 2.7 %shard_map.63 = f32[320,640]{1,0:T(8,128)} custom-call(s32[14]{0:T(128)} %stack.75.info.refs_0_, f32[640,320]{1,0:T(8,128)} %bitcast.32, f32[320,320]{1,0:T(8,128)} %copy-done.6, f32[320,640]{1,0:T(8,128)} %add_sqrt_fusion.root), custom_call_target="tpu_custom_call" | custom-call | tf_op jit(solution)/shard_map/pallas_call | solution.py:441
  (101 shorter events, 43.0 us)
Async XLA Ops:
  9.6 10.7 %collective-permute-start.1 = (bf16[320,4352]{1,0:T(8,128)(2,1)}, bf16[320,4352]{1,0:T(8,128)(2,1)}, u32[]{:S(2)}, u32[]{:S(2)}) collective-permute-start(bf16[320,4352]{1,0:T(8,128)(2,1)} %get-tuple-element.43.own.refs_2_.refs_5_.refs_1_), channel_id=1, source_target_pairs={{0,8},{1,9},{2,10},{3,11},{4,12},{5,13},{6,14},{7,15},{8,0},{9,1},... | collective-permute-start | bytes 8355848 | tf_op jit(solution)/shard_map/ppermute | solution.py:36
  11.0 37.1 %collective-permute-start = (bf16[320,2176]{1,0:T(8,128)(2,1)}, bf16[320,2176]{1,0:T(8,128)(2,1)}, u32[]{:S(2)}, u32[]{:S(2)}) collective-permute-start(bf16[320,2176]{1,0:T(8,128)(2,1)} %get-tuple-element.37), channel_id=1, source_target_pairs={{0,64},{1,65},{2,66},{3,67},{4,68},{5,69},{6,70},{7,71},{8,72},{9,... | collective-permute-start | bytes 4177928 | tf_op jit(solution)/shard_map/ppermute | solution.py:36
  14.1 35.2 %collective-permute-start.5 = (bf16[320,2176]{1,0:T(8,128)(2,1)}, bf16[320,2176]{1,0:T(8,128)(2,1)}, u32[]{:S(2)}, u32[]{:S(2)}) collective-permute-start(bf16[320,2176]{1,0:T(8,128)(2,1)} %get-tuple-element.48), channel_id=1, source_target_pairs={{0,48},{1,49},{2,50},{3,51},{4,52},{5,53},{6,54},{7,55},{8,56},{9,... | collective-permute-start | bytes 4177928 | tf_op jit(solution)/shard_map/ppermute | solution.py:36
  17.8 33.0 %collective-permute-start.6 = (bf16[320,2176]{1,0:T(8,128)(2,1)}, bf16[320,2176]{1,0:T(8,128)(2,1)}, u32[]{:S(2)}, u32[]{:S(2)}) collective-permute-start(bf16[320,2176]{1,0:T(8,128)(2,1)} %get-tuple-element.49), channel_id=1, source_target_pairs={{0,16},{1,17},{2,18},{3,19},{4,20},{5,21},{6,22},{7,23},{8,24},{9,... | collective-permute-start | bytes 4177928 | tf_op jit(solution)/shard_map/ppermute | solution.py:36
  28.1 18.7 %all-to-all-start = ((f32[4,2,80,320]{3,2,1,0:T(8,128)}), f32[4,2,80,320]{3,2,1,0:T(8,128)}, u32[]{:S(2)}, u32[]{:S(2)}) async-start(f32[4,2,80,320]{3,2,1,0:T(8,128)} %get-tuple-element.41), calls=%async_computation | async-start | bytes 1966080 | tf_op jit(solution)/shard_map/all_to_all | solution.py:41
  48.2 8.3 %collective-permute-start.8 = (bf16[320,2176]{1,0:T(8,128)(2,1)}, bf16[320,2176]{1,0:T(8,128)(2,1)}, u32[]{:S(2)}, u32[]{:S(2)}) collective-permute-start(bf16[320,2176]{1,0:T(8,128)(2,1)} %collective-permute-done.refs_1_.refs_6_.refs_3_), channel_id=1, source_target_pairs={{0,8},{1,9},{2,10},{3,11},{4,12},{5,13},{6,14},{7,15},{8,0},{9,1},... | collective-permute-start | bytes 4177928 | tf_op jit(solution)/shard_map/ppermute | solution.py:36
  53.4 8.5 %collective-permute-start.7 = (bf16[320,2176]{1,0:T(8,128)(2,1)}, bf16[320,2176]{1,0:T(8,128)(2,1)}, u32[]{:S(2)}, u32[]{:S(2)}) collective-permute-start(bf16[320,2176]{1,0:T(8,128)(2,1)} %broadcast_select_fusion), channel_id=1, source_target_pairs={{0,8},{1,9},{2,10},{3,11},{4,12},{5,13},{6,14},{7,15},{8,0},{9,1},... | collective-permute-start | bytes 4177928 | tf_op jit(solution)/shard_map/ppermute | solution.py:36
  54.9 44.0 %collective-permute-start.2 = (bf16[320,2176]{1,0:T(8,128)(2,1)}, bf16[320,2176]{1,0:T(8,128)(2,1)S(1)}, u32[]{:S(2)}, u32[]{:S(2)}) collective-permute-start(bf16[320,2176]{1,0:T(8,128)(2,1)} %get-tuple-element.45), channel_id=1, source_target_pairs={{0,48},{1,49},{2,50},{3,51},{4,52},{5,53},{6,54},{7,55},{8,56},{9,... | collective-permute-start | bytes 4177928 | tf_op jit(solution)/shard_map/ppermute | solution.py:36
  54.9 44.0 %collective-permute-start.3 = (bf16[320,2176]{1,0:T(8,128)(2,1)}, bf16[320,2176]{1,0:T(8,128)(2,1)}, u32[]{:S(2)}, u32[]{:S(2)}) collective-permute-start(bf16[320,2176]{1,0:T(8,128)(2,1)} %get-tuple-element.46), channel_id=1, source_target_pairs={{0,64},{1,65},{2,66},{3,67},{4,68},{5,69},{6,70},{7,71},{8,72},{9,... | collective-permute-start | bytes 4177928 | tf_op jit(solution)/shard_map/ppermute | solution.py:36
  55.2 43.7 %collective-permute-start.4 = (bf16[320,2176]{1,0:T(8,128)(2,1)}, bf16[320,2176]{1,0:T(8,128)(2,1)S(1)}, u32[]{:S(2)}, u32[]{:S(2)}) collective-permute-start(bf16[320,2176]{1,0:T(8,128)(2,1)} %collective-permute-done.refs_1_.refs_6_.refs_3_), channel_id=1, source_target_pairs={{0,16},{1,17},{2,18},{3,19},{4,20},{5,21},{6,22},{7,23},{8,24},{9,... | collective-permute-start | bytes 4177928 | tf_op jit(solution)/shard_map/ppermute | solution.py:36
  67.7 29.5 %all-to-all-start.1 = ((f32[4,2,168,320]{3,2,1,0:T(8,128)}), f32[4,2,168,320]{3,2,1,0:T(8,128)}, u32[]{:S(2)}, u32[]{:S(2)}) async-start(f32[4,2,168,320]{3,2,1,0:T(8,128)} %shard_map.59), calls=%async_computation.1 | async-start | bytes 4128768 | tf_op jit(solution)/shard_map/all_to_all | solution.py:41
  72.1 40.7 %collective-permute-start.9 = (bf16[320,2176]{1,0:T(8,128)(2,1)}, bf16[320,2176]{1,0:T(8,128)(2,1)}, u32[]{:S(2)}, u32[]{:S(2)}) collective-permute-start(bf16[320,2176]{1,0:T(8,128)(2,1)} %collective-permute-done.5.refs_1_.refs_6_.refs_5_.refs_7_), channel_id=1, source_target_pairs={{0,8},{1,9},{2,10},{3,11},{4,12},{5,13},{6,14},{7,15},{8,0},{9,1},... | collective-permute-start | bytes 4177928 | tf_op jit(solution)/shard_map/ppermute | solution.py:36
  99.0 13.9 %collective-permute-start.10 = (bf16[320,2176]{1,0:T(8,128)(2,1)S(1)}, bf16[320,2176]{1,0:T(8,128)(2,1)}, u32[]{:S(2)}, u32[]{:S(2)}) collective-permute-start(bf16[320,2176]{1,0:T(8,128)(2,1)S(1)} %collective-permute-done.2.refs_6_.refs_8_), channel_id=1, source_target_pairs={{0,8},{1,9},{2,10},{3,11},{4,12},{5,13},{6,14},{7,15},{8,0},{9,1},... | collective-permute-start | bytes 4177928 | tf_op jit(solution)/shard_map/ppermute | solution.py:36
  101.0 11.8 %collective-permute-start.11 = (bf16[320,2176]{1,0:T(8,128)(2,1)S(1)}, bf16[320,2176]{1,0:T(8,128)(2,1)}, u32[]{:S(2)}, u32[]{:S(2)}) collective-permute-start(bf16[320,2176]{1,0:T(8,128)(2,1)S(1)} %collective-permute-done.4.refs_9_.refs_10_), channel_id=1, source_target_pairs={{0,8},{1,9},{2,10},{3,11},{4,12},{5,13},{6,14},{7,15},{8,0},{9,1},... | collective-permute-start | bytes 4177928 | tf_op jit(solution)/shard_map/ppermute | solution.py:36
  102.6 19.2 %collective-permute-start.12 = (f32[248,320]{1,0:T(8,128)S(1)}, f32[248,320]{1,0:T(8,128)S(1)}, u32[]{:S(2)}, u32[]{:S(2)}) collective-permute-start(f32[248,320]{1,0:T(8,128)S(1)} %pad_maximum_fusion), channel_id=1, source_target_pairs={{0,4},{1,5},{2,6},{3,7},{4,0},{5,1},{6,2},{7,3},{8,12},{9,13},{10,... | collective-permute-start | bytes 952328 | tf_op jit(solution)/shard_map/ppermute | solution.py:36
  122.5 40.0 %all-to-all-start.2 = ((f32[8,3,80,320]{3,2,1,0:T(8,128)}), f32[8,3,80,320]{3,2,1,0:T(8,128)S(1)}, u32[]{:S(2)}, u32[]{:S(2)}) async-start(f32[8,3,80,320]{3,2,1,0:T(8,128)} %shard_map.61), calls=%async_computation.2 | async-start | bytes 5898240 | tf_op jit(solution)/shard_map/all_to_all | solution.py:554
  127.6 4.9 %collective-permute-start.13 = (f32[88,320]{1,0:T(8,128)S(1)}, f32[88,320]{1,0:T(8,128)S(1)}, u32[]{:S(2)}, u32[]{:S(2)}) collective-permute-start(f32[88,320]{1,0:T(8,128)S(1)} %pad_maximum_fusion.4), channel_id=1, source_target_pairs={{0,48},{1,49},{2,50},{3,51},{4,52},{5,53},{6,54},{7,55},{8,56},{9,... | collective-permute-start | bytes 337928 | tf_op jit(solution)/shard_map/ppermute | solution.py:36
  130.5 5.5 %collective-permute-start.15 = (f32[88,320]{1,0:T(8,128)S(1)}, f32[88,320]{1,0:T(8,128)S(1)}, u32[]{:S(2)}, u32[]{:S(2)}) collective-permute-start(f32[88,320]{1,0:T(8,128)S(1)} %pad_maximum_fusion.4), channel_id=1, source_target_pairs={{0,16},{1,17},{2,18},{3,19},{4,20},{5,21},{6,22},{7,23},{8,24},{9,... | collective-permute-start | bytes 337928 | tf_op jit(solution)/shard_map/ppermute | solution.py:36
  130.5 5.5 %collective-permute-start.14 = (f32[8,320]{1,0:T(8,128)S(1)}, f32[8,320]{1,0:T(8,128)S(1)}, u32[]{:S(2)}, u32[]{:S(2)}) collective-permute-start(f32[8,320]{1,0:T(8,128)S(1)} %slice.126), channel_id=1, source_target_pairs={{0,32},{1,33},{2,34},{3,35},{4,36},{5,37},{6,38},{7,39},{8,40},{9,... | collective-permute-start | bytes 30728 | tf_op jit(solution)/shard_map/ppermute | solution.py:36
  164.4 11.7 %collective-permute-start.16 = (f32[3,80,320]{2,1,0:T(8,128)}, f32[3,80,320]{2,1,0:T(8,128)}, u32[]{:S(2)}, u32[]{:S(2)}) collective-permute-start(f32[3,80,320]{2,1,0:T(8,128)} %reduce_sum.38.late), channel_id=1, source_target_pairs={{0,16},{1,17},{2,18},{3,19},{4,20},{5,21},{6,22},{7,23},{8,24},{9,... | collective-permute-start | bytes 921608 | tf_op jit(solution)/shard_map/ppermute | solution.py:36
  164.5 11.6 %collective-permute-start.17 = (f32[192,320]{1,0:T(8,128)S(1)}, f32[192,320]{1,0:T(8,128)S(1)}, u32[]{:S(2)}, u32[]{:S(2)}) collective-permute-start(f32[192,320]{1,0:T(8,128)S(1)} %pad_maximum_fusion.2), channel_id=1, source_target_pairs={{0,64},{1,65},{2,66},{3,67},{4,68},{5,69},{6,70},{7,71},{8,72},{9,... | collective-permute-start | bytes 737288 | tf_op jit(solution)/shard_map/ppermute | solution.py:36
  167.3 8.9 %collective-permute-start.18 = (f32[80,320]{1,0:T(8,128)S(1)}, f32[80,320]{1,0:T(8,128)S(1)}, u32[]{:S(2)}, u32[]{:S(2)}) collective-permute-start(f32[80,320]{1,0:T(8,128)S(1)} %slice_reduce_fusion), channel_id=1, source_target_pairs={{0,112},{1,113},{2,114},{3,115},{4,116},{5,117},{6,118},{7,119},{8... | collective-permute-start | bytes 307208 | tf_op jit(solution)/shard_map/ppermute | solution.py:36
  179.3 21.9 %all-to-all-start.3 = ((f32[8,80,320]{2,1,0:T(8,128)}), f32[8,80,320]{2,1,0:T(8,128)S(1)}, u32[]{:S(2)}, u32[]{:S(2)}) async-start(f32[8,80,320]{2,1,0:T(8,128)} %shard_map.62), calls=%async_computation.3 | async-start | bytes 1966080 | tf_op jit(solution)/shard_map/all_to_all | solution.py:572
  201.3 5.5 %collective-permute-start.20 = (f32[320,320]{1,0:T(8,128)S(1)}, f32[320,320]{1,0:T(8,128)S(1)}, u32[]{:S(2)}, u32[]{:S(2)}) collective-permute-start(f32[320,320]{1,0:T(8,128)S(1)} %constant_dynamic-slice_fusion), channel_id=1, source_target_pairs={{0,8},{1,9},{2,10},{3,11},{4,12},{5,13},{6,14},{7,15},{8,0},{9,1},... | collective-permute-start | bytes 1228808 | tf_op jit(solution)/shard_map/ppermute | solution.py:36
  (15 other events, 97.3 us)

commit v2 on v1

--- a/solution.py
+++ b/solution.py
@@ -65,7 +65,7 @@
     return (lax.broadcasted_iota(jnp.int32, (LANES, 2 * LANES), 1) // 2 == place).astype(jnp.bfloat16)
 
 
-def mask_kernel(info, hot, spectra, wedges, own, to_partner, to_next, to_previous, to_partner_b, to_previous_b, pairs):
+def mask_kernel(info, hots, spectra, sibling, wedges, own, own_sibling, to_partner_b, to_previous_b, pairs):
     half = spectra.shape[1] // 2
 
     @pl.when(pl.program_id(0) == 0)
@@ -76,38 +76,84 @@
             wide = jnp.dot(some, spread, preferred_element_type=jnp.float32)
             pairs[:, pl.ds(j * 2 * LANES, 2 * LANES)] = wide.astype(jnp.bfloat16)
 
-    keep = jnp.dot(hot[...], pairs[...], preferred_element_type=jnp.float32).astype(jnp.bfloat16)
-    own[...] = spectra[...] * keep
-    to_partner[...] = own[:, span(1 - info[YH], half)]
-    to_next[...] = own[:, span(info[NEXT_HIGH], half)]
-    to_previous[...] = own[:, span(info[PREV_HIGH], half)]
+    for k, (block, out) in enumerate(((spectra, own), (sibling, own_sibling))):
+        keep = jnp.dot(hots[k], pairs[...], preferred_element_type=jnp.float32).astype(jnp.bfloat16)
+        out[...] = block[...] * keep
     to_partner_b[...] = own[:, span(info[YH], half)]
     to_previous_b[...] = own[:, span(1 - info[PREV_HIGH], half)]
 
 
-def masked_blocks(info, hot, spectra, wedges):
+def masked_blocks(info, hots, spectra, sibling, wedges):
     rows, width = spectra.shape
     classes = wedges.shape[0]
     part = rows // 4
     whole = lambda *shape: pl.BlockSpec(shape, lambda i, info: (0, 0))
     slab = lambda n: pl.BlockSpec((part, n), lambda i, info: (i, 0))
+    block = jax.ShapeDtypeStruct((rows, width), jnp.bfloat16)
     half_block = jax.ShapeDtypeStruct((rows, width // 2), jnp.bfloat16)
     return pl.pallas_call(
         mask_kernel,
         grid_spec=pltpu.PrefetchScalarGridSpec(
             num_scalar_prefetch=1,
             grid=(4,),
-            in_specs=[slab(classes), slab(width), whole(classes, width // 2)],
-            out_specs=[slab(width)] + [slab(width // 2)] * 5 + [whole(classes, width)],
+            in_specs=[
+                pl.BlockSpec((2, part, classes), lambda i, info: (0, i, 0)),
+                slab(width),
+                slab(width),
+                whole(classes, width // 2),
+            ],
+            out_specs=[slab(width)] * 2 + [slab(width // 2)] * 2 + [whole(classes, width)],
         ),
-        out_shape=[
-            jax.ShapeDtypeStruct((rows, width), jnp.bfloat16),
-            *[half_block] * 5,
-            jax.ShapeDtypeStruct((classes, width), jnp.bfloat16),
-        ],
+        out_shape=[block, block, half_block, half_block, jax.ShapeDtypeStruct((classes, width), jnp.bfloat16)],
         compiler_params=PARAMS,
         cost_estimate=COST,
-    )(info, hot, spectra, wedges)
+    )(info, hots, spectra, sibling, wedges)
+
+
+def received_kernel(info, hots, pairs, following, partner, previous, out_following, out_partner, out_previous, third):
+    half = following.shape[1]
+
+    def masked(k, block, at):
+        keep = jnp.dot(hots[k], pairs[:, at], preferred_element_type=jnp.float32).astype(jnp.bfloat16)
+        return block[...] * keep
+
+    at_high = span(info[HIGH], half)
+    out_following[...] = masked(0, following, at_high)
+    out_partner[...] = masked(1, partner, span(info[YH], half))
+    out_previous[...] = masked(2, previous, at_high)
+
+    @pl.when(info[LOW] == 1)
+    def _():
+        third[...] = out_following[...]
+
+    @pl.when(info[LOW] == 0)
+    def _():
+        third[...] = out_previous[...]
+
+
+def masked_received(info, hots, pairs, *blocks):
+    rows, half = blocks[0].shape
+    classes, width = pairs.shape
+    part = rows // 4
+    slab = pl.BlockSpec((part, half), lambda i, info: (i, 0))
+    return pl.pallas_call(
+        received_kernel,
+        grid_spec=pltpu.PrefetchScalarGridSpec(
+            num_scalar_prefetch=1,
+            grid=(4,),
+            in_specs=[
+                pl.BlockSpec((3, part, classes), lambda i, info: (0, i, 0)),
+                pl.BlockSpec((classes, width), lambda i, info: (0, 0)),
+                slab,
+                slab,
+                slab,
+            ],
+            out_specs=[slab] * 4,
+        ),
+        out_shape=[jax.ShapeDtypeStruct((rows, half), jnp.bfloat16)] * 4,
+        compiler_params=PARAMS,
+        cost_estimate=COST,
+    )(info, hots, pairs, *blocks)
 
 
 def weight_kernel(shell_weight, shells, weight):
@@ -494,15 +540,23 @@
     ).astype(jnp.int32)
 
     class_range = jnp.arange(classes, dtype=jnp.int32)
-    own_labels = lax.dynamic_slice_in_dim(labels, blk * rows, rows)
-    hot = (own_labels[:, None] == class_range[None, :]).astype(jnp.bfloat16)
-    own, to_partner, to_next, to_previous, to_partner_b, to_previous_b, pairs = masked_blocks(info, hot, spectra, wedges)
-
-    following_a = send(to_previous, dz=-1)
-    partner_a = send(to_partner, dyh=1)
-    previous = send(to_next, dz=1)
+    following_a = send(columns(spectra, previous_high), dz=-1)
+    partner_a = send(columns(spectra, 1 - yh), dyh=1)
+    previous = send(columns(spectra, (z + 1) % 4 // 2), dz=1)
+
+    sibling = send(spectra, dc=1)
+
+    def labels_of(block):
+        return lax.dynamic_slice_in_dim(labels, block * rows, rows)
+
+    own_labels = labels_of(blk)
+    hots = jnp.stack(
+        [own_labels, labels_of(blk + 1 - 2 * core)]
+        + [labels_of(place(dyh, dz) * 2 + core) for dyh, dz in ((0, 1), (1, 0), (0, -1))]
+    )
+    hots = (hots[:, :, None] == class_range[None, None, :]).astype(jnp.bfloat16)
+    own, sibling, to_partner_b, to_previous_b, pairs = masked_blocks(info, hots[:2], spectra, sibling, wedges)
     following_b = send(to_previous_b, dz=-1)
-    sibling = send(own, dc=1)
     own, shells = together(own, shells)
     weight = pair_weights(shell_weight, shells[None, :])
     q1, own_w = first_tiles(info, own, sibling, weight)
@@ -514,9 +568,10 @@
     )
     partner_b = send(to_partner_b, dyh=1)
     partner_a, p1, partial_energy = together(partner_a, p1, partial_energy)
+    following_a, partner_a, previous, third_a = masked_received(info, hots[2:], pairs, following_a, partner_a, previous)
     diagonal = send(partner_a, dz=1)
     partner_s = send(partner_a, dc=1)
-    third_a_s = send(jnp.where(low, following_a, previous), dc=1)
+    third_a_s = send(third_a, dc=1)
     half_pair = half_tiles(
         (1, LOWER, ONE, CORE, YH), info, partner_a, own, partner_s, sibling, own, partner_a, weight, partial_energy
     )

time: 212 us -> 225 us (1.061)
  local copies, waits for them, and re-layouts: 8.47 us -> 16.9 us
  Pallas kernels: 51.3 us -> 58.3 us
  other arithmetic: 13.5 us -> 9.7 us
    pallas_call x0 -> x1, Pallas kernels: none -> 6.54 us  [masked_received(): pl.pallas_call(received_kernel, grid_spec=pltpu.PrefetchScalarGridSpec(nu...]
    dynamic_slice x0 -> x2, local copies, waits for them, and re-layouts: none -> 4.33 us  [the longest x1 4.24 us: columns(): return lax.dynamic_slice_in_dim(block, which * half, half, 1)]
    unnamed x28 -> x34, local copies, waits for them, and re-layouts: 2.93 us -> 5.59 us
    select_n x1 -> x0, other arithmetic: 2.6 us -> none  [per_device(): third_a_s = send(jnp.where(low, following_a, previous), dc=1)]
  transfers between devices with their start and end apart: 25 -> 25, of which waited for: 9 -> 9; matrix products, arithmetic and copies ran while one was open for 9% -> 10% of each run, Pallas kernels for 18% -> 21%
where the time goes in v2:
time: 225 us; the launch traced here: 223 us
  waiting for transfers between devices  79.2 us (35%)
  Pallas kernels  58.3 us (26%)
  starting transfers between devices  55.3 us (25%)
  local copies, waits for them, and re-layouts  16.9 us (8%)
  other arithmetic  9.7 us (4%)
  matrix products  3.51 us (2%)
    all_to_all x2, waiting for transfers between devices, summed_along_x(): lax.all_to_all(tiles, 'freq', 0, 0, axis_index_groups=groups, tiled=True)  34.9 us
    ppermute x21, starting transfers between devices, send(): return lax.ppermute(block, BOTH, route(dyh, dz, dc, dyl))  32.6 us
    all_to_all x1, waiting for transfers between devices, per_device(): late = lax.all_to_all(late, 'freq', 0, 0, tiled=True)  24.4 us
    pallas_call x2, Pallas kernels, late_tiles(): pl.pallas_call(kernel, in_specs=specs, out_specs=ANY, out_shape=jax.Shape...  18.1 us
    ppermute x21, waiting for transfers between devices, send(): return lax.ppermute(block, BOTH, route(dyh, dz, dc, dyl))  12.7 us
    pallas_call x2, Pallas kernels, half_tiles(): pl.pallas_call(kernel, in_specs=specs, out_specs=ANY, out_shape=jax.Shape...  11.1 us
    all_to_all x1, starting transfers between devices, per_device(): lax.all_to_all(pieces, 'freq', 0, 0, tiled=True).reshape(2 * rows, rows)  10.1 us
    all_to_all x2, starting transfers between devices, summed_along_x(): lax.all_to_all(tiles, 'freq', 0, 0, axis_index_groups=groups, tiled=True)  8.97 us
  transfers between devices with their start and end apart: 25, of which 9 were waited for; matrix products, arithmetic and copies ran while one was open for 10% of the time, Pallas kernels for 21%

profile of v2, /device:TPU:1, one launch (start us, length us, event | category | flops | bytes accessed | tf_op | source)
XLA Modules:
  0.0 223.4 jit_solution(13403241178465123476)
XLA Ops:
  1.4 4.2 %constant_dynamic-slice_fusion.2 = (bf16[320,2176]{1,0:T(8,128)(2,1)}, bf16[320,2176]{1,0:T(8,128)(2,1)}, bf16[320,2176]{1,0:T(8,128)(2,1)}) fusion(bf16[320,4352]{1,0:T(8,128)(2,1)} %spectra.1, s32[]{:T(128)S(6)} %select_n.311, s32[]{:T(128)S(6)} %select_n.303, s32[]{:T(128)S(6)} %select_n.310), kind=kLoop, calls=%fused_computation.30 | loop fusion | bytes 8355852 | tf_op jit(solution)/shard_map/dynamic_slice | solution.py:510
  8.7 3.8 %collective-permute-start.4 = (bf16[320,2176]{1,0:T(8,128)(2,1)}, bf16[320,2176]{1,0:T(8,128)(2,1)}, u32[]{:S(2)}, u32[]{:S(2)}) collective-permute-start(bf16[320,2176]{1,0:T(8,128)(2,1)} %get-tuple-element.93), channel_id=1, source_target_pairs={{0,48},{1,49},{2,50},{3,51},{4,52},{5,53},{6,54},{7,55},{8,56},{9,... | collective-permute-start | bytes 4177928 | tf_op jit(solution)/shard_map/ppermute | solution.py:36
  15.9 7.9 %shard_map.55 = (bf16[320,4352]{1,0:T(8,128)(2,1)}, bf16[320,4352]{1,0:T(8,128)(2,1)}, bf16[320,2176]{1,0:T(8,128)(2,1)}, bf16[320,2176]{1,0:T(8,128)(2,1)}, bf16[8,4352]{1,0:T(8,128)(2,1)}) custom-call(s32[14]{0:T(128)} %stack.93.info.refs_0_, bf16[2,320,8]{2,1,0:T(8,128)(2,1)} %slice.132.hots, bf16[320,4352]{1,0:T(8,128)(2,1)} %spectra.1, ...), custom_call_target="tpu_custom_call" | custom-call | flops 1024 | bytes 1024 | tf_op jit(solution)/shard_map/pallas_call | solution.py:94
  26.2 7.8 %shard_map.57 = (f32[4,2,80,320]{3,2,1,0:T(8,128)}, bf16[320,4352]{1,0:T(8,128)(2,1)}) custom-call(s32[14]{0:T(128)} %stack.93.info.refs_0_, bf16[320,4352]{1,0:T(8,128)(2,1)} %get-tuple-element.45.own.refs_2_.refs_5_.refs_1_, bf16[320,4352]{1,0:T(8,128)(2,1)} %get-tuple-element.41.sibling.refs_4_, f32[1,4352]{1,0:T(1,128)} %shard_map.56.weight.refs_7_.refs_11_), custom_call_target="tpu_custom_call" | custom-call | flops 1024 | bytes 1024 | tf_op jit(solution)/shard_map/pallas_call | solution.py:225
  34.0 4.4 %all-to-all-start = ((f32[4,2,80,320]{3,2,1,0:T(8,128)}), f32[4,2,80,320]{3,2,1,0:T(8,128)}, u32[]{:S(2)}, u32[]{:S(2)}) async-start(f32[4,2,80,320]{3,2,1,0:T(8,128)} %get-tuple-element.43), calls=%async_computation | async-start | bytes 1966080 | tf_op jit(solution)/shard_map/all_to_all | solution.py:41
  39.2 3.5 %fusion.refs_8_ = f32[8,320]{1,0:T(8,128)} fusion(bf16[8,4352]{1,0:T(8,128)(2,1)S(1)} %copy-done.14, bf16[320,4352]{1,0:T(8,128)(2,1)S(1)} %copy-done, f32[4352]{0:T(1024)S(1)} %reduce.1), kind=kOutput, calls=%fused_computation | convolution fusion | flops 137871360 | bytes 2882560 | tf_op jit(solution)/shard_map/dot_general | solution.py:566
  42.7 10.1 %all-to-all-done = f32[4,2,80,320]{3,2,1,0:T(8,128)} async-done(((f32[4,2,80,320]{3,2,1,0:T(8,128)}), f32[4,2,80,320]{3,2,1,0:T(8,128)}, u32[]{:S(2)}, u32[]{:S(2)}) %all-to-all-start) | async-done | bytes 819232 | tf_op jit(solution)/shard_map/all_to_all | solution.py:41
  54.1 6.5 %shard_map.58 = (bf16[320,2176]{1,0:T(8,128)(2,1)}, bf16[320,2176]{1,0:T(8,128)(2,1)}, bf16[320,2176]{1,0:T(8,128)(2,1)}, bf16[320,2176]{1,0:T(8,128)(2,1)}) custom-call(s32[14]{0:T(128)} %stack.93.info.refs_0_, bf16[3,320,8]{2,1,0:T(8,128)(2,1)} %slice.133.hots, bf16[8,4352]{1,0:T(8,128)(2,1)} %get-tuple-element.44.pairs, ...), custom_call_target="tpu_custom_call" | custom-call | flops 1024 | bytes 1024 | tf_op jit(solution)/shard_map/pallas_call | solution.py:139
  65.9 5.3 %shard_map.59.refs_9_ = f32[4,2,168,320]{3,2,1,0:T(8,128)} custom-call(s32[14]{0:T(128)} %stack.93.info.refs_0_, bf16[320,2176]{1,0:T(8,128)(2,1)} %get-tuple-element.50.refs_1_.refs_6_.refs_3_, bf16[320,4352]{1,0:T(8,128)(2,1)} %get-tuple-element.45.own.refs_2_.refs_5_.refs_1_, bf16[320,2176]{1,0:T(8,128)(2,1)} %collective-permute-done.8.refs_3_, ...), custom_call_target="tpu_custom_call" | custom-call | flops 1024 | bytes 1024 | tf_op jit(solution)/shard_map/pallas_call | solution.py:302
  72.3 5.8 %shard_map.60 = f32[4,2,168,320]{3,2,1,0:T(8,128)} custom-call(s32[14]{0:T(128)} %stack.93.info.refs_0_, bf16[320,2176]{1,0:T(8,128)(2,1)} %get-tuple-element.51.refs_1_.refs_6_.refs_5_.refs_7_, bf16[320,2176]{1,0:T(8,128)(2,1)} %get-tuple-element.52.refs_2_.refs_5_, bf16[320,2176]{1,0:T(8,128)(2,1)} %copy-done.4, ...), custom_call_target="tpu_custom_call", output_to_operand_aliasing={{}: (9, {})} | custom-call | flops 1024 | bytes 1024 | tf_op jit(solution)/shard_map/pallas_call | solution.py:302
  78.1 4.6 %all-to-all-start.1 = ((f32[4,2,168,320]{3,2,1,0:T(8,128)}), f32[4,2,168,320]{3,2,1,0:T(8,128)}, u32[]{:S(2)}, u32[]{:S(2)}) async-start(f32[4,2,168,320]{3,2,1,0:T(8,128)} %shard_map.60), calls=%async_computation.1 | async-start | bytes 4128768 | tf_op jit(solution)/shard_map/all_to_all | solution.py:41
  83.4 24.8 %all-to-all-done.1 = f32[4,2,168,320]{3,2,1,0:T(8,128)} async-done(((f32[4,2,168,320]{3,2,1,0:T(8,128)}), f32[4,2,168,320]{3,2,1,0:T(8,128)}, u32[]{:S(2)}, u32[]{:S(2)}) %all-to-all-start.1) | async-done | bytes 1720352 | tf_op jit(solution)/shard_map/all_to_all | solution.py:41
  113.6 9.1 %shard_map.61.refs_12_ = f32[8,3,80,320]{3,2,1,0:T(8,128)} custom-call(s32[14]{0:T(128)} %stack.93.info.refs_0_, bf16[320,4352]{1,0:T(8,128)(2,1)} %get-tuple-element.45.own.refs_2_.refs_5_.refs_1_, bf16[320,4352]{1,0:T(8,128)(2,1)} %get-tuple-element.56.refs_2_, bf16[320,2176]{1,0:T(8,128)(2,1)} %get-tuple-element.50.refs_1_.refs_6_.refs_3_, ...), custom_call_target="tpu_custom_call" | custom-call | flops 1024 | bytes 1024 | tf_op jit(solution)/shard_map/pallas_call | solution.py:421
  122.7 9.0 %shard_map.62 = f32[8,3,80,320]{3,2,1,0:T(8,128)} custom-call(s32[14]{0:T(128)} %stack.93.info.refs_0_, bf16[320,4352]{1,0:T(8,128)(2,1)} %get-tuple-element.45.own.refs_2_.refs_5_.refs_1_, bf16[320,4352]{1,0:T(8,128)(2,1)} %get-tuple-element.56.refs_2_, ...), custom_call_target="tpu_custom_call", output_to_operand_aliasing={{}: (12, {})} | custom-call | flops 1024 | bytes 1024 | tf_op jit(solution)/shard_map/pallas_call | solution.py:421
  132.4 3.6 %all-to-all-start.2 = ((f32[8,3,80,320]{3,2,1,0:T(8,128)}), f32[8,3,80,320]{3,2,1,0:T(8,128)S(1)}, u32[]{:S(2)}, u32[]{:S(2)}) async-start(f32[8,3,80,320]{3,2,1,0:T(8,128)} %shard_map.62), calls=%async_computation.2 | async-start | bytes 5898240 | tf_op jit(solution)/shard_map/all_to_all | solution.py:609
  137.3 4.3 %collective-permute-start.13 = (f32[88,320]{1,0:T(8,128)S(1)}, f32[88,320]{1,0:T(8,128)S(1)}, u32[]{:S(2)}, u32[]{:S(2)}) collective-permute-start(f32[88,320]{1,0:T(8,128)S(1)} %pad_maximum_fusion.4), channel_id=1, source_target_pairs={{0,48},{1,49},{2,50},{3,51},{4,52},{5,53},{6,54},{7,55},{8,56},{9,... | collective-permute-start | bytes 337928 | tf_op jit(solution)/shard_map/ppermute | solution.py:36
  143.8 3.4 %collective-permute-done.15.third_back = f32[88,320]{1,0:T(8,128)S(1)} collective-permute-done((f32[88,320]{1,0:T(8,128)S(1)}, f32[88,320]{1,0:T(8,128)S(1)}, u32[]{:S(2)}, u32[]{:S(2)}) %collective-permute-start.15) | collective-permute-done | bytes 112672 | tf_op jit(solution)/shard_map/ppermute | solution.py:36
  147.8 24.4 %all-to-all-done.2 = f32[8,3,80,320]{3,2,1,0:T(8,128)S(1)} async-done(((f32[8,3,80,320]{3,2,1,0:T(8,128)}), f32[8,3,80,320]{3,2,1,0:T(8,128)S(1)}, u32[]{:S(2)}, u32[]{:S(2)}) %all-to-all-start.2) | async-done | bytes 2457632 | tf_op jit(solution)/shard_map/all_to_all | solution.py:609
  176.5 4.9 %collective-permute-start.18 = (f32[80,320]{1,0:T(8,128)S(1)}, f32[80,320]{1,0:T(8,128)S(1)}, u32[]{:S(2)}, u32[]{:S(2)}) collective-permute-start(f32[80,320]{1,0:T(8,128)S(1)} %slice_reduce_fusion), channel_id=1, source_target_pairs={{0,112},{1,113},{2,114},{3,115},{4,116},{5,117},{6,118},{7,119},{8... | collective-permute-start | bytes 307208 | tf_op jit(solution)/shard_map/ppermute | solution.py:36
  181.3 6.0 %collective-permute-done.18.from_diagonal = f32[80,320]{1,0:T(8,128)S(1)} collective-permute-done((f32[80,320]{1,0:T(8,128)S(1)}, f32[80,320]{1,0:T(8,128)S(1)}, u32[]{:S(2)}, u32[]{:S(2)}) %collective-permute-start.18) | collective-permute-done | bytes 102432 | tf_op jit(solution)/shard_map/ppermute | solution.py:36
  190.6 10.1 %all-to-all-start.3 = ((f32[8,80,320]{2,1,0:T(8,128)}), f32[8,80,320]{2,1,0:T(8,128)S(1)}, u32[]{:S(2)}, u32[]{:S(2)}) async-start(f32[8,80,320]{2,1,0:T(8,128)} %shard_map.63), calls=%async_computation.3 | async-start | bytes 1966080 | tf_op jit(solution)/shard_map/all_to_all | solution.py:627
  203.4 3.4 %collective-permute-start.19 = (f32[64,320]{1,0:T(8,128)S(1)}, f32[64,320]{1,0:T(8,128)S(1)}, u32[]{:S(2)}, u32[]{:S(2)}) collective-permute-start(f32[64,320]{1,0:T(8,128)S(1)} %pad_maximum_fusion.5), channel_id=1, source_target_pairs={{0,8},{1,9},{2,10},{3,11},{4,12},{5,13},{6,14},{7,15},{8,0},{9,1},... | collective-permute-start | bytes 245768 | tf_op jit(solution)/shard_map/ppermute | solution.py:36
  207.8 7.3 %all-to-all-done.3 = f32[8,80,320]{2,1,0:T(8,128)S(1)} async-done(((f32[8,80,320]{2,1,0:T(8,128)}), f32[8,80,320]{2,1,0:T(8,128)S(1)}, u32[]{:S(2)}, u32[]{:S(2)}) %all-to-all-start.3) | async-done | bytes 819232 | tf_op jit(solution)/shard_map/all_to_all | solution.py:627
  216.8 3.1 %add_sqrt_fusion.root = f32[320,640]{1,0:T(8,128)} fusion(f32[640]{0:T(1024)S(1)} %get-tuple-element.82, f32[640]{0:T(1024)S(1)} %get-tuple-element.83, f32[640]{0:T(1024)S(1)} %get-tuple-element.84, f32[640]{0:T(1024)S(1)} %get-tuple-element.85, f32[640]{0:T(1024)S(1)} %get-tuple-element.86, f32[640]{0:T(1024)S(1)} %get-tuple-element.87, ...), kind=kLoop, calls=%fused_computation.6 | loop fusion | flops 3686400 | bytes 857600 | tf_op jit(solution)/shard_map/sqrt | solution.py:644
  (117 shorter events, 45.9 us)
Async XLA Ops:
  0.0 14.3 %collective-permute-start.1 = (bf16[320,4352]{1,0:T(8,128)(2,1)}, bf16[320,4352]{1,0:T(8,128)(2,1)S(1)}, u32[]{:S(2)}, u32[]{:S(2)}) collective-permute-start(bf16[320,4352]{1,0:T(8,128)(2,1)} %spectra.1), channel_id=1, source_target_pairs={{0,8},{1,9},{2,10},{3,11},{4,12},{5,13},{6,14},{7,15},{8,0},{9,1},... | collective-permute-start | bytes 8355848 | tf_op jit(solution)/shard_map/ppermute | solution.py:36
  5.7 48.4 %collective-permute-start = (bf16[320,2176]{1,0:T(8,128)(2,1)}, bf16[320,2176]{1,0:T(8,128)(2,1)}, u32[]{:S(2)}, u32[]{:S(2)}) collective-permute-start(bf16[320,2176]{1,0:T(8,128)(2,1)} %get-tuple-element.92), channel_id=1, source_target_pairs={{0,64},{1,65},{2,66},{3,67},{4,68},{5,69},{6,70},{7,71},{8,72},{9,... | collective-permute-start | bytes 4177928 | tf_op jit(solution)/shard_map/ppermute | solution.py:36
  8.7 45.4 %collective-permute-start.4 = (bf16[320,2176]{1,0:T(8,128)(2,1)}, bf16[320,2176]{1,0:T(8,128)(2,1)}, u32[]{:S(2)}, u32[]{:S(2)}) collective-permute-start(bf16[320,2176]{1,0:T(8,128)(2,1)} %get-tuple-element.93), channel_id=1, source_target_pairs={{0,48},{1,49},{2,50},{3,51},{4,52},{5,53},{6,54},{7,55},{8,56},{9,... | collective-permute-start | bytes 4177928 | tf_op jit(solution)/shard_map/ppermute | solution.py:36
  12.4 41.7 %collective-permute-start.5 = (bf16[320,2176]{1,0:T(8,128)(2,1)}, bf16[320,2176]{1,0:T(8,128)(2,1)}, u32[]{:S(2)}, u32[]{:S(2)}) collective-permute-start(bf16[320,2176]{1,0:T(8,128)(2,1)} %get-tuple-element.91), channel_id=1, source_target_pairs={{0,16},{1,17},{2,18},{3,19},{4,20},{5,21},{6,22},{7,23},{8,24},{9,... | collective-permute-start | bytes 4177928 | tf_op jit(solution)/shard_map/ppermute | solution.py:36
  34.0 18.8 %all-to-all-start = ((f32[4,2,80,320]{3,2,1,0:T(8,128)}), f32[4,2,80,320]{3,2,1,0:T(8,128)}, u32[]{:S(2)}, u32[]{:S(2)}) async-start(f32[4,2,80,320]{3,2,1,0:T(8,128)} %get-tuple-element.43), calls=%async_computation | async-start | bytes 1966080 | tf_op jit(solution)/shard_map/all_to_all | solution.py:41
  60.6 5.3 %collective-permute-start.8 = (bf16[320,2176]{1,0:T(8,128)(2,1)}, bf16[320,2176]{1,0:T(8,128)(2,1)}, u32[]{:S(2)}, u32[]{:S(2)}) collective-permute-start(bf16[320,2176]{1,0:T(8,128)(2,1)} %get-tuple-element.50.refs_1_.refs_6_.refs_3_), channel_id=1, source_target_pairs={{0,8},{1,9},{2,10},{3,11},{4,12},{5,13},{6,14},{7,15},{8,0},{9,1},... | collective-permute-start | bytes 4177928 | tf_op jit(solution)/shard_map/ppermute | solution.py:36
  61.7 9.5 %collective-permute-start.7 = (bf16[320,2176]{1,0:T(8,128)(2,1)}, bf16[320,2176]{1,0:T(8,128)(2,1)S(1)}, u32[]{:S(2)}, u32[]{:S(2)}) collective-permute-start(bf16[320,2176]{1,0:T(8,128)(2,1)} %get-tuple-element.53), channel_id=1, source_target_pairs={{0,8},{1,9},{2,10},{3,11},{4,12},{5,13},{6,14},{7,15},{8,0},{9,1},... | collective-permute-start | bytes 4177928 | tf_op jit(solution)/shard_map/ppermute | solution.py:36
  61.8 48.2 %collective-permute-start.2 = (bf16[320,2176]{1,0:T(8,128)(2,1)}, bf16[320,2176]{1,0:T(8,128)(2,1)S(1)}, u32[]{:S(2)}, u32[]{:S(2)}) collective-permute-start(bf16[320,2176]{1,0:T(8,128)(2,1)} %get-tuple-element.47), channel_id=1, source_target_pairs={{0,48},{1,49},{2,50},{3,51},{4,52},{5,53},{6,54},{7,55},{8,56},{9,... | collective-permute-start | bytes 4177928 | tf_op jit(solution)/shard_map/ppermute | solution.py:36
  64.4 45.5 %collective-permute-start.3 = (bf16[320,2176]{1,0:T(8,128)(2,1)}, bf16[320,2176]{1,0:T(8,128)(2,1)}, u32[]{:S(2)}, u32[]{:S(2)}) collective-permute-start(bf16[320,2176]{1,0:T(8,128)(2,1)} %get-tuple-element.48), channel_id=1, source_target_pairs={{0,64},{1,65},{2,66},{3,67},{4,68},{5,69},{6,70},{7,71},{8,72},{9,... | collective-permute-start | bytes 4177928 | tf_op jit(solution)/shard_map/ppermute | solution.py:36
  64.5 45.5 %collective-permute-start.6 = (bf16[320,2176]{1,0:T(8,128)(2,1)}, bf16[320,2176]{1,0:T(8,128)(2,1)}, u32[]{:S(2)}, u32[]{:S(2)}) collective-permute-start(bf16[320,2176]{1,0:T(8,128)(2,1)} %get-tuple-element.50.refs_1_.refs_6_.refs_3_), channel_id=1, source_target_pairs={{0,16},{1,17},{2,18},{3,19},{4,20},{5,21},{6,22},{7,23},{8,24},{9,... | collective-permute-start | bytes 4177928 | tf_op jit(solution)/shard_map/ppermute | solution.py:36
  78.1 30.1 %all-to-all-start.1 = ((f32[4,2,168,320]{3,2,1,0:T(8,128)}), f32[4,2,168,320]{3,2,1,0:T(8,128)}, u32[]{:S(2)}, u32[]{:S(2)}) async-start(f32[4,2,168,320]{3,2,1,0:T(8,128)} %shard_map.60), calls=%async_computation.1 | async-start | bytes 4128768 | tf_op jit(solution)/shard_map/all_to_all | solution.py:41
  82.7 40.0 %collective-permute-start.9 = (bf16[320,2176]{1,0:T(8,128)(2,1)S(1)}, bf16[320,2176]{1,0:T(8,128)(2,1)}, u32[]{:S(2)}, u32[]{:S(2)}) collective-permute-start(bf16[320,2176]{1,0:T(8,128)(2,1)S(1)} %copy-done.1), channel_id=1, source_target_pairs={{0,8},{1,9},{2,10},{3,11},{4,12},{5,13},{6,14},{7,15},{8,0},{9,1},... | collective-permute-start | bytes 4177928 | tf_op jit(solution)/shard_map/ppermute | solution.py:36
  110.0 12.7 %collective-permute-start.10 = (bf16[320,2176]{1,0:T(8,128)(2,1)S(1)}, bf16[320,2176]{1,0:T(8,128)(2,1)}, u32[]{:S(2)}, u32[]{:S(2)}) collective-permute-start(bf16[320,2176]{1,0:T(8,128)(2,1)S(1)} %collective-permute-done.2.refs_6_.refs_8_), channel_id=1, source_target_pairs={{0,8},{1,9},{2,10},{3,11},{4,12},{5,13},{6,14},{7,15},{8,0},{9,1},... | collective-permute-start | bytes 4177928 | tf_op jit(solution)/shard_map/ppermute | solution.py:36
  111.6 11.2 %collective-permute-start.11 = (bf16[320,2176]{1,0:T(8,128)(2,1)}, bf16[320,2176]{1,0:T(8,128)(2,1)}, u32[]{:S(2)}, u32[]{:S(2)}) collective-permute-start(bf16[320,2176]{1,0:T(8,128)(2,1)} %collective-permute-done.6.refs_9_.refs_10_), channel_id=1, source_target_pairs={{0,8},{1,9},{2,10},{3,11},{4,12},{5,13},{6,14},{7,15},{8,0},{9,1},... | collective-permute-start | bytes 4177928 | tf_op jit(solution)/shard_map/ppermute | solution.py:36
  113.1 18.6 %collective-permute-start.12 = (f32[248,320]{1,0:T(8,128)S(1)}, f32[248,320]{1,0:T(8,128)S(1)}, u32[]{:S(2)}, u32[]{:S(2)}) collective-permute-start(f32[248,320]{1,0:T(8,128)S(1)} %pad_maximum_fusion), channel_id=1, source_target_pairs={{0,4},{1,5},{2,6},{3,7},{4,0},{5,1},{6,2},{7,3},{8,12},{9,13},{10,... | collective-permute-start | bytes 952328 | tf_op jit(solution)/shard_map/ppermute | solution.py:36
  132.4 39.8 %all-to-all-start.2 = ((f32[8,3,80,320]{3,2,1,0:T(8,128)}), f32[8,3,80,320]{3,2,1,0:T(8,128)S(1)}, u32[]{:S(2)}, u32[]{:S(2)}) async-start(f32[8,3,80,320]{3,2,1,0:T(8,128)} %shard_map.62), calls=%async_computation.2 | async-start | bytes 5898240 | tf_op jit(solution)/shard_map/all_to_all | solution.py:609
  137.3 6.5 %collective-permute-start.13 = (f32[88,320]{1,0:T(8,128)S(1)}, f32[88,320]{1,0:T(8,128)S(1)}, u32[]{:S(2)}, u32[]{:S(2)}) collective-permute-start(f32[88,320]{1,0:T(8,128)S(1)} %pad_maximum_fusion.4), channel_id=1, source_target_pairs={{0,48},{1,49},{2,50},{3,51},{4,52},{5,53},{6,54},{7,55},{8,56},{9,... | collective-permute-start | bytes 337928 | tf_op jit(solution)/shard_map/ppermute | solution.py:36
  141.6 5.6 %collective-permute-start.15 = (f32[88,320]{1,0:T(8,128)S(1)}, f32[88,320]{1,0:T(8,128)S(1)}, u32[]{:S(2)}, u32[]{:S(2)}) collective-permute-start(f32[88,320]{1,0:T(8,128)S(1)} %pad_maximum_fusion.4), channel_id=1, source_target_pairs={{0,16},{1,17},{2,18},{3,19},{4,20},{5,21},{6,22},{7,23},{8,24},{9,... | collective-permute-start | bytes 337928 | tf_op jit(solution)/shard_map/ppermute | solution.py:36
  141.6 5.6 %collective-permute-start.14 = (f32[8,320]{1,0:T(8,128)S(1)}, f32[8,320]{1,0:T(8,128)S(1)}, u32[]{:S(2)}, u32[]{:S(2)}) collective-permute-start(f32[8,320]{1,0:T(8,128)S(1)} %slice.136), channel_id=1, source_target_pairs={{0,32},{1,33},{2,34},{3,35},{4,36},{5,37},{6,38},{7,39},{8,40},{9,... | collective-permute-start | bytes 30728 | tf_op jit(solution)/shard_map/ppermute | solution.py:36
  174.1 13.3 %collective-permute-start.16 = (f32[3,80,320]{2,1,0:T(8,128)}, f32[3,80,320]{2,1,0:T(8,128)}, u32[]{:S(2)}, u32[]{:S(2)}) collective-permute-start(f32[3,80,320]{2,1,0:T(8,128)} %reduce_sum.38.late), channel_id=1, source_target_pairs={{0,16},{1,17},{2,18},{3,19},{4,20},{5,21},{6,22},{7,23},{8,24},{9,... | collective-permute-start | bytes 921608 | tf_op jit(solution)/shard_map/ppermute | solution.py:36
  174.2 13.1 %collective-permute-start.17 = (f32[192,320]{1,0:T(8,128)S(1)}, f32[192,320]{1,0:T(8,128)S(1)}, u32[]{:S(2)}, u32[]{:S(2)}) collective-permute-start(f32[192,320]{1,0:T(8,128)S(1)} %pad_maximum_fusion.2), channel_id=1, source_target_pairs={{0,64},{1,65},{2,66},{3,67},{4,68},{5,69},{6,70},{7,71},{8,72},{9,... | collective-permute-start | bytes 737288 | tf_op jit(solution)/shard_map/ppermute | solution.py:36
  176.5 10.9 %collective-permute-start.18 = (f32[80,320]{1,0:T(8,128)S(1)}, f32[80,320]{1,0:T(8,128)S(1)}, u32[]{:S(2)}, u32[]{:S(2)}) collective-permute-start(f32[80,320]{1,0:T(8,128)S(1)} %slice_reduce_fusion), channel_id=1, source_target_pairs={{0,112},{1,113},{2,114},{3,115},{4,116},{5,117},{6,118},{7,119},{8... | collective-permute-start | bytes 307208 | tf_op jit(solution)/shard_map/ppermute | solution.py:36
  190.6 24.4 %all-to-all-start.3 = ((f32[8,80,320]{2,1,0:T(8,128)}), f32[8,80,320]{2,1,0:T(8,128)S(1)}, u32[]{:S(2)}, u32[]{:S(2)}) async-start(f32[8,80,320]{2,1,0:T(8,128)} %shard_map.63), calls=%async_computation.3 | async-start | bytes 1966080 | tf_op jit(solution)/shard_map/all_to_all | solution.py:627
  215.1 4.9 %collective-permute-start.20 = (f32[320,320]{1,0:T(8,128)S(1)}, f32[320,320]{1,0:T(8,128)S(1)}, u32[]{:S(2)}, u32[]{:S(2)}) collective-permute-start(f32[320,320]{1,0:T(8,128)S(1)} %constant_dynamic-slice_fusion), channel_id=1, source_target_pairs={{0,8},{1,9},{2,10},{3,11},{4,12},{5,13},{6,14},{7,15},{8,0},{9,1},... | collective-permute-start | bytes 1228808 | tf_op jit(solution)/shard_map/ppermute | solution.py:36
  (18 other events, 106.2 us)

commit v3 on v1

--- a/solution.py
+++ b/solution.py
@@ -65,7 +65,7 @@
     return (lax.broadcasted_iota(jnp.int32, (LANES, 2 * LANES), 1) // 2 == place).astype(jnp.bfloat16)
 
 
-def mask_kernel(info, hot, spectra, wedges, own, to_partner, to_next, to_previous, to_partner_b, to_previous_b, pairs):
+def mask_kernel(info, hot, spectra, wedges, own, to_partner, to_next, to_previous, pairs):
     half = spectra.shape[1] // 2
 
     @pl.when(pl.program_id(0) == 0)
@@ -81,8 +81,6 @@
     to_partner[...] = own[:, span(1 - info[YH], half)]
     to_next[...] = own[:, span(info[NEXT_HIGH], half)]
     to_previous[...] = own[:, span(info[PREV_HIGH], half)]
-    to_partner_b[...] = own[:, span(info[YH], half)]
-    to_previous_b[...] = own[:, span(1 - info[PREV_HIGH], half)]
 
 
 def masked_blocks(info, hot, spectra, wedges):
@@ -98,11 +96,11 @@
             num_scalar_prefetch=1,
             grid=(4,),
             in_specs=[slab(classes), slab(width), whole(classes, width // 2)],
-            out_specs=[slab(width)] + [slab(width // 2)] * 5 + [whole(classes, width)],
+            out_specs=[slab(width)] + [slab(width // 2)] * 3 + [whole(classes, width)],
         ),
         out_shape=[
             jax.ShapeDtypeStruct((rows, width), jnp.bfloat16),
-            *[half_block] * 5,
+            *[half_block] * 3,
             jax.ShapeDtypeStruct((classes, width), jnp.bfloat16),
         ],
         compiler_params=PARAMS,
@@ -196,28 +194,11 @@
     )(info, own, sibling, weight)
 
 
-def half_kernel(
-    k_tile, first_at, on_b_at, on_b_other_at, half_at, info, a_yes, a_no, other_yes, other_no, b_yes, b_no,
-    weight, energy, *rest,
-):
-    out, a, b, tiles, sems, out_sems = rest[-6:]
-    rows, half = b.shape[1:]
-    slices = tiles.shape[2]
-    core, first, at = info[CORE], info[first_at] == 1, span(info[half_at], half)
-    w = weight[:, at]
-
-    def pick(n, dst, yes, no):
-        for chosen, src in ((first, yes), (jnp.logical_not(first), no)):
-            src = src if src.shape[1] == half else src.at[:, at]
-
-            @pl.when(chosen)
-            def _(src=src):
-                pltpu.make_async_copy(src, dst, sems.at[n]).start()
-
-        return pltpu.make_async_copy(src, dst, sems.at[n])
-
-    got_b = pick(0, b.at[0], b_yes, b_no)
-    got_a = [pick(1, a.at[0], a_yes, a_no), pick(2, a.at[2], other_yes, other_no)]
+def half_kernel(jobs, info, *refs):
+    operands, (weight, energy, out, a, b, tiles, sems, out_sems) = refs[:-8], refs[-8:]
+    rows, half = b.shape[2:]
+    slices = tiles.shape[3]
+    core = info[CORE]
     sent = []
 
     def go(src, dst, n):
@@ -225,47 +206,64 @@
         copy.start()
         sent.append(copy)
 
-    for x in range(4):
-        go(energy, out.at[x, k_tile, pl.ds(2 * slices, energy.shape[0])], 2 + x)
-    got_b.wait()
-    b[1] = scaled(b[0], w)
-    for k, (on_b, owner) in enumerate(((info[on_b_at], core), (info[on_b_other_at], 1 - core))):
-        got_a[k].wait()
-
-        @pl.when(on_b == 0)
-        def _(k=k):
-            a[2 * k + 1] = scaled(a[2 * k], w)
-
-        tiles[k] = gram(a[2 * k + 1 - on_b], b[on_b]).reshape(tiles.shape[1:])
-        go(tiles.at[k], out.at[:, k_tile, pl.ds(pl.multiple_of(owner * slices, 8), slices)], k)
+    def fetch(k, first_at, half_at):
+        first, at = info[first_at] == 1, span(info[half_at], half)
+
+        def pick(n, dst, yes, no):
+            for chosen, src in ((first, yes), (jnp.logical_not(first), no)):
+                src = src if src.shape[1] == half else src.at[:, at]
+
+                @pl.when(chosen)
+                def _(src=src):
+                    pltpu.make_async_copy(src, dst, sems.at[k, n]).start()
+
+            return pltpu.make_async_copy(src, dst, sems.at[k, n])
+
+        a_yes, a_no, other_yes, other_no, b_yes, b_no = operands[6 * k : 6 * k + 6]
+        got_b = pick(0, b.at[k, 0], b_yes, b_no)
+        return got_b, [pick(1, a.at[k, 0], a_yes, a_no), pick(2, a.at[k, 2], other_yes, other_no)]
+
+    got = [fetch(k, job[0], job[3]) for k, job in enumerate(jobs)]
+    for k in range(len(jobs)):
+        for x in range(4):
+            go(energy, out.at[x, k, pl.ds(2 * slices, energy.shape[0])], 6 * k + 2 + x)
+    for k, (_, on_b_at, on_b_other_at, half_at) in enumerate(jobs):
+        got_b, got_a = got[k]
+        w = weight[:, span(info[half_at], half)]
+        got_b.wait()
+        b[k, 1] = scaled(b[k, 0], w)
+        for n, (on_b, owner) in enumerate(((info[on_b_at], core), (info[on_b_other_at], 1 - core))):
+            got_a[n].wait()
+
+            @pl.when(on_b == 0)
+            def _(n=n, k=k, w=w):
+                a[k, 2 * n + 1] = scaled(a[k, 2 * n], w)
+
+            tiles[k, n] = gram(a[k, 2 * n + 1 - on_b], b[k, on_b]).reshape(tiles.shape[2:])
+            go(tiles.at[k, n], out.at[:, k, pl.ds(pl.multiple_of(owner * slices, 8), slices)], 6 * k + n)
     for copy in sent:
         copy.wait()
 
 
-def half_tiles(places_of, info, *operands, into=None):
+def half_tiles(jobs, info, *operands):
     rows, classes = operands[0].shape[0], operands[-1].shape[0]
     half = operands[-2].shape[1] // 2
-    specs, aliases = [SMEM] + [ANY] * 6 + [VMEM] * 2, {}
-    if into is not None:
-        aliases = {len(specs): 0}
-        specs, operands = specs + [ANY], operands + (into,)
 
     def kernel(*refs):
-        half_kernel(*places_of, *refs)
+        half_kernel(jobs, *refs)
 
     return pl.pallas_call(
         kernel,
-        in_specs=specs,
+        in_specs=[SMEM] + [ANY] * (len(operands) - 2) + [VMEM] * 2,
         out_specs=ANY,
         out_shape=jax.ShapeDtypeStruct((4, 2, rows // 2 + classes, rows), jnp.float32),
         scratch_shapes=[
-            pltpu.VMEM((4, rows, half), jnp.bfloat16),
-            pltpu.VMEM((2, rows, half), jnp.bfloat16),
-            pltpu.VMEM((2, 4, rows // 4, rows), jnp.float32),
-            pltpu.SemaphoreType.DMA((3,)),
-            pltpu.SemaphoreType.DMA((6,)),
+            pltpu.VMEM((2, 4, rows, half), jnp.bfloat16),
+            pltpu.VMEM((2, 2, rows, half), jnp.bfloat16),
+            pltpu.VMEM((2, 2, 4, rows // 4, rows), jnp.float32),
+            pltpu.SemaphoreType.DMA((2, 3)),
+            pltpu.SemaphoreType.DMA((12,)),
         ],
-        input_output_aliases=aliases,
         compiler_params=PARAMS,
         cost_estimate=COST,
     )(info, *operands)
@@ -496,12 +494,11 @@
     class_range = jnp.arange(classes, dtype=jnp.int32)
     own_labels = lax.dynamic_slice_in_dim(labels, blk * rows, rows)
     hot = (own_labels[:, None] == class_range[None, :]).astype(jnp.bfloat16)
-    own, to_partner, to_next, to_previous, to_partner_b, to_previous_b, pairs = masked_blocks(info, hot, spectra, wedges)
+    own, to_partner, to_next, to_previous, pairs = masked_blocks(info, hot, spectra, wedges)
 
     following_a = send(to_previous, dz=-1)
     partner_a = send(to_partner, dyh=1)
     previous = send(to_next, dz=1)
-    following_b = send(to_previous_b, dz=-1)
     sibling = send(own, dc=1)
     own, shells = together(own, shells)
     weight = pair_weights(shell_weight, shells[None, :])
@@ -512,17 +509,18 @@
     partial_energy = lax.dot_general(
         pairs.astype(jnp.float32), squares, (((1,), (1,)), ((), ())), precision=lax.Precision.HIGHEST
     )
+    to_previous_b, to_partner_b = columns(own_e, 1 - previous_high), columns(own_e, yh)
+    following_a, partner_a, previous, p1, partial_energy, to_previous_b, to_partner_b = together(
+        following_a, partner_a, previous, p1, partial_energy, to_previous_b, to_partner_b
+    )
+    following_b = send(to_previous_b, dz=-1)
     partner_b = send(to_partner_b, dyh=1)
-    partner_a, p1, partial_energy = together(partner_a, p1, partial_energy)
     diagonal = send(partner_a, dz=1)
     partner_s = send(partner_a, dc=1)
     third_a_s = send(jnp.where(low, following_a, previous), dc=1)
     half_pair = half_tiles(
-        (1, LOWER, ONE, CORE, YH), info, partner_a, own, partner_s, sibling, own, partner_a, weight, partial_energy
-    )
-    half_pair = half_tiles(
-        (0, LOW, ON_B3, ON_B3, HIGH), info, following_a, previous, third_a_s, third_a_s, previous, following_a, weight,
-        partial_energy, into=half_pair,
+        ((LOWER, ONE, CORE, YH), (LOW, ON_B3, ON_B3, HIGH)), info, partner_a, own, partner_s, sibling, own, partner_a,
+        following_a, previous, third_a_s, third_a_s, previous, following_a, weight, partial_energy,
     )
     half_pair = summed_along_x(half_pair)
     following_b, partner_b, diagonal, half_pair = together(following_b, partner_b, diagonal, half_pair)
@@ -532,9 +530,9 @@
     def halves(which):
         return [
             lax.dynamic_index_in_dim(p1, which, 0, keepdims=False),
+            lax.dynamic_slice_in_dim(half_pair[1], which * slices, slices, 0),
             lax.dynamic_slice_in_dim(half_pair[0], which * slices, slices, 0),
-            lax.dynamic_slice_in_dim(half_pair[1], which * slices, slices, 0),
-            half_pair[1, 2 * slices :],
+            half_pair[0, 2 * slices :],
         ]
 
     following_as = send(following_a, dc=1)

time: 212 us -> 209 us (0.986)
  starting transfers between devices: 54 us -> 49.9 us
  Pallas kernels: 51.3 us -> 47.8 us
  waiting for transfers between devices: 79.2 us -> 82.5 us
    ppermute x21, starting transfers between devices: 33.1 us -> 29.2 us  [send(): return lax.ppermute(block, BOTH, route(dyh, dz, dc, dyl))]
    pallas_call x2 -> x1, Pallas kernels: 11.2 us -> 7.98 us  [half_tiles(): pl.pallas_call(kernel, in_specs=[SMEM] + [ANY] * (len(operands) - 2) + [V...]
    ppermute x21, waiting for transfers between devices: 12.5 us -> 15.5 us  [send(): return lax.ppermute(block, BOTH, route(dyh, dz, dc, dyl))]
  transfers between devices with their start and end apart: 25 -> 25, of which waited for: 9 -> 11; matrix products, arithmetic and copies ran while one was open for 9% -> 9% of each run, Pallas kernels for 18% -> 17%
where the time goes in v3:
time: 209 us; the launch traced here: 207 us
  waiting for transfers between devices  82.5 us (39%)
  starting transfers between devices  49.9 us (24%)
  Pallas kernels  47.8 us (23%)
  other arithmetic  13.1 us (6%)
  local copies, waits for them, and re-layouts  10.1 us (5%)
  matrix products  3.51 us (2%)
    all_to_all x2, waiting for transfers between devices, summed_along_x(): lax.all_to_all(tiles, 'freq', 0, 0, axis_index_groups=groups, tiled=True)  33.9 us
    ppermute x21, starting transfers between devices, send(): return lax.ppermute(block, BOTH, route(dyh, dz, dc, dyl))  29.2 us
    all_to_all x1, waiting for transfers between devices, per_device(): late = lax.all_to_all(late, 'freq', 0, 0, tiled=True)  26.8 us
    pallas_call x2, Pallas kernels, late_tiles(): pl.pallas_call(kernel, in_specs=specs, out_specs=ANY, out_shape=jax.Shape...  18.3 us
    ppermute x21, waiting for transfers between devices, send(): return lax.ppermute(block, BOTH, route(dyh, dz, dc, dyl))  15.5 us
    all_to_all x2, starting transfers between devices, summed_along_x(): lax.all_to_all(tiles, 'freq', 0, 0, axis_index_groups=groups, tiled=True)  8.83 us
    all_to_all x1, starting transfers between devices, per_device(): lax.all_to_all(pieces, 'freq', 0, 0, tiled=True).reshape(2 * rows, rows)  8.27 us
    pallas_call x1, Pallas kernels, half_tiles(): pl.pallas_call(kernel, in_specs=[SMEM] + [ANY] * (len(operands) - 2) + [V...  7.98 us
  transfers between devices with their start and end apart: 25, of which 11 were waited for; matrix products, arithmetic and copies ran while one was open for 9% of the time, Pallas kernels for 17%

profile of v3, /device:TPU:1, one launch (start us, length us, event | category | flops | bytes accessed | tf_op | source)
XLA Modules:
  0.0 207.3 jit_solution(5194736120387543178)
XLA Ops:
  2.1 6.7 %shard_map.55 = (bf16[320,4352]{1,0:T(8,128)(2,1)}, bf16[320,2176]{1,0:T(8,128)(2,1)}, bf16[320,2176]{1,0:T(8,128)(2,1)}, bf16[320,2176]{1,0:T(8,128)(2,1)}, bf16[8,4352]{1,0:T(8,128)(2,1)}) custom-call(s32[14]{0:T(128)} %stack.75.info.refs_0_, bf16[320,8]{1,0:T(8,128)(2,1)} %fusion.6.hot, bf16[320,4352]{1,0:T(8,128)(2,1)} %spectra.1, s32[8,2176]{1,0:T(8,128)} %wedges.1), custom_call_target="tpu_custom_call" | custom-call | flops 1024 | bytes 1024 | tf_op jit(solution)/shard_map/pallas_call | solution.py:93
  10.2 3.8 %collective-permute-start = (bf16[320,2176]{1,0:T(8,128)(2,1)}, bf16[320,2176]{1,0:T(8,128)(2,1)}, u32[]{:S(2)}, u32[]{:S(2)}) collective-permute-start(bf16[320,2176]{1,0:T(8,128)(2,1)} %get-tuple-element.39), channel_id=1, source_target_pairs={{0,48},{1,49},{2,50},{3,51},{4,52},{5,53},{6,54},{7,55},{8,56},{9,... | collective-permute-start | bytes 4177928 | tf_op jit(solution)/shard_map/ppermute | solution.py:36
  14.1 2.9 %collective-permute-start.1 = (bf16[320,2176]{1,0:T(8,128)(2,1)}, bf16[320,2176]{1,0:T(8,128)(2,1)}, u32[]{:S(2)}, u32[]{:S(2)}) collective-permute-start(bf16[320,2176]{1,0:T(8,128)(2,1)} %get-tuple-element.40), channel_id=1, source_target_pairs={{0,64},{1,65},{2,66},{3,67},{4,68},{5,69},{6,70},{7,71},{8,72},{9,... | collective-permute-start | bytes 4177928 | tf_op jit(solution)/shard_map/ppermute | solution.py:36
  20.2 7.8 %shard_map.57 = (f32[4,2,80,320]{3,2,1,0:T(8,128)}, bf16[320,4352]{1,0:T(8,128)(2,1)}) custom-call(s32[14]{0:T(128)} %stack.75.info.refs_0_, bf16[320,4352]{1,0:T(8,128)(2,1)} %get-tuple-element.47.own.refs_2_.refs_5_.refs_1_, bf16[320,4352]{1,0:T(8,128)(2,1)} %collective-permute-done.3.sibling.refs_4_, f32[1,4352]{1,0:T(1,128)} %shard_map.56.weight.refs_13_.refs_11_), custom_call_target="tpu_custom_call" | custom-call | flops 1024 | bytes 1024 | tf_op jit(solution)/shard_map/pallas_call | solution.py:177
  28.0 4.4 %all-to-all-start = ((f32[4,2,80,320]{3,2,1,0:T(8,128)}), f32[4,2,80,320]{3,2,1,0:T(8,128)}, u32[]{:S(2)}, u32[]{:S(2)}) async-start(f32[4,2,80,320]{3,2,1,0:T(8,128)} %get-tuple-element.45), calls=%async_computation | async-start | bytes 1966080 | tf_op jit(solution)/shard_map/all_to_all | solution.py:41
  32.5 3.5 %fusion.refs_14_ = f32[8,320]{1,0:T(8,128)} fusion(bf16[8,4352]{1,0:T(8,128)(2,1)S(1)} %copy-done.12, bf16[320,4352]{1,0:T(8,128)(2,1)S(1)} %copy-done, f32[4352]{0:T(1024)S(1)} %reduce.1), kind=kOutput, calls=%fused_computation | convolution fusion | flops 137871360 | bytes 2882560 | tf_op jit(solution)/shard_map/dot_general | solution.py:509
  37.7 9.1 %all-to-all-done = f32[4,2,80,320]{3,2,1,0:T(8,128)} async-done(((f32[4,2,80,320]{3,2,1,0:T(8,128)}), f32[4,2,80,320]{3,2,1,0:T(8,128)}, u32[]{:S(2)}, u32[]{:S(2)}) %all-to-all-start) | async-done | bytes 819232 | tf_op jit(solution)/shard_map/all_to_all | solution.py:41
  58.1 8.0 %shard_map.58 = f32[4,2,168,320]{3,2,1,0:T(8,128)} custom-call(s32[14]{0:T(128)} %stack.75.info.refs_0_, bf16[320,2176]{1,0:T(8,128)(2,1)} %collective-permute-done.1.refs_1_.refs_6_.refs_3_, bf16[320,4352]{1,0:T(8,128)(2,1)} %get-tuple-element.47.own.refs_2_.refs_5_.refs_1_, bf16[320,2176]{1,0:T(8,128)(2,1)} %collective-permute-done.7.refs_3_, ...), custom_call_target="tpu_custom_call" | custom-call | flops 1024 | bytes 1024 | tf_op jit(solution)/shard_map/pallas_call | solution.py:255
  66.1 4.4 %all-to-all-start.1 = ((f32[4,2,168,320]{3,2,1,0:T(8,128)}), f32[4,2,168,320]{3,2,1,0:T(8,128)}, u32[]{:S(2)}, u32[]{:S(2)}) async-start(f32[4,2,168,320]{3,2,1,0:T(8,128)} %shard_map.58), calls=%async_computation.1 | async-start | bytes 4128768 | tf_op jit(solution)/shard_map/all_to_all | solution.py:41
  71.3 24.8 %all-to-all-done.1 = f32[4,2,168,320]{3,2,1,0:T(8,128)} async-done(((f32[4,2,168,320]{3,2,1,0:T(8,128)}), f32[4,2,168,320]{3,2,1,0:T(8,128)}, u32[]{:S(2)}, u32[]{:S(2)}) %all-to-all-start.1) | async-done | bytes 1720352 | tf_op jit(solution)/shard_map/all_to_all | solution.py:41
  101.5 9.3 %shard_map.59.refs_12_ = f32[8,3,80,320]{3,2,1,0:T(8,128)} custom-call(s32[14]{0:T(128)} %stack.75.info.refs_0_, bf16[320,4352]{1,0:T(8,128)(2,1)} %get-tuple-element.47.own.refs_2_.refs_5_.refs_1_, bf16[320,4352]{1,0:T(8,128)(2,1)} %get-tuple-element.56.refs_2_, bf16[320,2176]{1,0:T(8,128)(2,1)} %collective-permute-done.1.refs_1_.refs_6_.refs_3_, ...), custom_call_target="tpu_custom_call" | custom-call | flops 1024 | bytes 1024 | tf_op jit(solution)/shard_map/pallas_call | solution.py:373
  110.9 9.0 %shard_map.60 = f32[8,3,80,320]{3,2,1,0:T(8,128)} custom-call(s32[14]{0:T(128)} %stack.75.info.refs_0_, bf16[320,4352]{1,0:T(8,128)(2,1)} %get-tuple-element.47.own.refs_2_.refs_5_.refs_1_, bf16[320,4352]{1,0:T(8,128)(2,1)} %get-tuple-element.56.refs_2_, ...), custom_call_target="tpu_custom_call", output_to_operand_aliasing={{}: (12, {})} | custom-call | flops 1024 | bytes 1024 | tf_op jit(solution)/shard_map/pallas_call | solution.py:373
  120.6 3.6 %all-to-all-start.2 = ((f32[8,3,80,320]{3,2,1,0:T(8,128)}), f32[8,3,80,320]{3,2,1,0:T(8,128)S(1)}, u32[]{:S(2)}, u32[]{:S(2)}) async-start(f32[8,3,80,320]{3,2,1,0:T(8,128)} %shard_map.60), calls=%async_computation.2 | async-start | bytes 5898240 | tf_op jit(solution)/shard_map/all_to_all | solution.py:552
  129.6 3.2 %collective-permute-done.15.third_back = f32[88,320]{1,0:T(8,128)S(1)} collective-permute-done((f32[88,320]{1,0:T(8,128)S(1)}, f32[88,320]{1,0:T(8,128)S(1)}, u32[]{:S(2)}, u32[]{:S(2)}) %collective-permute-start.15) | collective-permute-done | bytes 112672 | tf_op jit(solution)/shard_map/ppermute | solution.py:36
  133.5 26.8 %all-to-all-done.2 = f32[8,3,80,320]{3,2,1,0:T(8,128)S(1)} async-done(((f32[8,3,80,320]{3,2,1,0:T(8,128)}), f32[8,3,80,320]{3,2,1,0:T(8,128)S(1)}, u32[]{:S(2)}, u32[]{:S(2)}) %all-to-all-start.2) | async-done | bytes 2457632 | tf_op jit(solution)/shard_map/all_to_all | solution.py:552
  163.8 4.0 %collective-permute-start.18 = (f32[80,320]{1,0:T(8,128)S(1)}, f32[80,320]{1,0:T(8,128)S(1)}, u32[]{:S(2)}, u32[]{:S(2)}) collective-permute-start(f32[80,320]{1,0:T(8,128)S(1)} %slice_reduce_fusion), channel_id=1, source_target_pairs={{0,112},{1,113},{2,114},{3,115},{4,116},{5,117},{6,118},{7,119},{8... | collective-permute-start | bytes 307208 | tf_op jit(solution)/shard_map/ppermute | solution.py:36
  167.9 5.2 %collective-permute-done.18.from_diagonal = f32[80,320]{1,0:T(8,128)S(1)} collective-permute-done((f32[80,320]{1,0:T(8,128)S(1)}, f32[80,320]{1,0:T(8,128)S(1)}, u32[]{:S(2)}, u32[]{:S(2)}) %collective-permute-start.18) | collective-permute-done | bytes 102432 | tf_op jit(solution)/shard_map/ppermute | solution.py:36
  173.8 2.5 %shard_map.61 = f32[8,80,320]{2,1,0:T(8,128)} custom-call(s32[14]{0:T(128)} %stack.75.info.refs_0_, f32[248,320]{1,0:T(8,128)} %copy-done.4, f32[3,80,320]{2,1,0:T(8,128)} %reduce_sum.38.late, f32[3,80,320]{2,1,0:T(8,128)} %collective-permute-done.16.from_previous, f32[88,320]{1,0:T(8,128)} %copy-done.9, f32[88,320]{1,0:T(8,128)} %copy-done.8, ...), custom_call_target="tpu_custom_call" | custom-call | tf_op jit(solution)/shard_map/pallas_call | solution.py:413
  176.3 8.3 %all-to-all-start.3 = ((f32[8,80,320]{2,1,0:T(8,128)}), f32[8,80,320]{2,1,0:T(8,128)S(1)}, u32[]{:S(2)}, u32[]{:S(2)}) async-start(f32[8,80,320]{2,1,0:T(8,128)} %shard_map.61), calls=%async_computation.3 | async-start | bytes 1966080 | tf_op jit(solution)/shard_map/all_to_all | solution.py:570
  187.2 3.7 %collective-permute-start.19 = (f32[64,320]{1,0:T(8,128)S(1)}, f32[64,320]{1,0:T(8,128)S(1)}, u32[]{:S(2)}, u32[]{:S(2)}) collective-permute-start(f32[64,320]{1,0:T(8,128)S(1)} %pad_maximum_fusion.5), channel_id=1, source_target_pairs={{0,8},{1,9},{2,10},{3,11},{4,12},{5,13},{6,14},{7,15},{8,0},{9,1},... | collective-permute-start | bytes 245768 | tf_op jit(solution)/shard_map/ppermute | solution.py:36
  192.0 6.3 %all-to-all-done.3 = f32[8,80,320]{2,1,0:T(8,128)S(1)} async-done(((f32[8,80,320]{2,1,0:T(8,128)}), f32[8,80,320]{2,1,0:T(8,128)S(1)}, u32[]{:S(2)}, u32[]{:S(2)}) %all-to-all-start.3) | async-done | bytes 819232 | tf_op jit(solution)/shard_map/all_to_all | solution.py:570
  198.3 2.3 %collective-permute-start.20 = (f32[320,320]{1,0:T(8,128)S(1)}, f32[320,320]{1,0:T(8,128)S(1)}, u32[]{:S(2)}, u32[]{:S(2)}) collective-permute-start(f32[320,320]{1,0:T(8,128)S(1)} %constant_dynamic-slice_fusion), channel_id=1, source_target_pairs={{0,8},{1,9},{2,10},{3,11},{4,12},{5,13},{6,14},{7,15},{8,0},{9,1},... | collective-permute-start | bytes 1228808 | tf_op jit(solution)/shard_map/ppermute | solution.py:36
  200.7 3.1 %add_sqrt_fusion.root = f32[320,640]{1,0:T(8,128)} fusion(f32[640]{0:T(1024)S(1)} %get-tuple-element.82, f32[640]{0:T(1024)S(1)} %get-tuple-element.83, f32[640]{0:T(1024)S(1)} %get-tuple-element.84, f32[640]{0:T(1024)S(1)} %get-tuple-element.85, f32[640]{0:T(1024)S(1)} %get-tuple-element.86, f32[640]{0:T(1024)S(1)} %get-tuple-element.87, ...), kind=kLoop, calls=%fused_computation.7 | loop fusion | flops 3686400 | bytes 857600 | tf_op jit(solution)/shard_map/sqrt | solution.py:587
  204.6 2.7 %shard_map.62 = f32[320,640]{1,0:T(8,128)} custom-call(s32[14]{0:T(128)} %stack.75.info.refs_0_, f32[640,320]{1,0:T(8,128)} %bitcast.32, f32[320,320]{1,0:T(8,128)} %copy-done.5, f32[320,640]{1,0:T(8,128)} %add_sqrt_fusion.root), custom_call_target="tpu_custom_call" | custom-call | tf_op jit(solution)/shard_map/pallas_call | solution.py:439
  (99 shorter events, 41.4 us)
Async XLA Ops:
  8.8 11.4 %collective-permute-start.3 = (bf16[320,4352]{1,0:T(8,128)(2,1)}, bf16[320,4352]{1,0:T(8,128)(2,1)}, u32[]{:S(2)}, u32[]{:S(2)}) collective-permute-start(bf16[320,4352]{1,0:T(8,128)(2,1)} %get-tuple-element.47.own.refs_2_.refs_5_.refs_1_), channel_id=1, source_target_pairs={{0,8},{1,9},{2,10},{3,11},{4,12},{5,13},{6,14},{7,15},{8,0},{9,1},... | collective-permute-start | bytes 8355848 | tf_op jit(solution)/shard_map/ppermute | solution.py:36
  10.2 37.8 %collective-permute-start = (bf16[320,2176]{1,0:T(8,128)(2,1)}, bf16[320,2176]{1,0:T(8,128)(2,1)}, u32[]{:S(2)}, u32[]{:S(2)}) collective-permute-start(bf16[320,2176]{1,0:T(8,128)(2,1)} %get-tuple-element.39), channel_id=1, source_target_pairs={{0,48},{1,49},{2,50},{3,51},{4,52},{5,53},{6,54},{7,55},{8,56},{9,... | collective-permute-start | bytes 4177928 | tf_op jit(solution)/shard_map/ppermute | solution.py:36
  14.1 34.0 %collective-permute-start.1 = (bf16[320,2176]{1,0:T(8,128)(2,1)}, bf16[320,2176]{1,0:T(8,128)(2,1)}, u32[]{:S(2)}, u32[]{:S(2)}) collective-permute-start(bf16[320,2176]{1,0:T(8,128)(2,1)} %get-tuple-element.40), channel_id=1, source_target_pairs={{0,64},{1,65},{2,66},{3,67},{4,68},{5,69},{6,70},{7,71},{8,72},{9,... | collective-permute-start | bytes 4177928 | tf_op jit(solution)/shard_map/ppermute | solution.py:36
  17.0 33.0 %collective-permute-start.2 = (bf16[320,2176]{1,0:T(8,128)(2,1)}, bf16[320,2176]{1,0:T(8,128)(2,1)}, u32[]{:S(2)}, u32[]{:S(2)}) collective-permute-start(bf16[320,2176]{1,0:T(8,128)(2,1)} %get-tuple-element.41), channel_id=1, source_target_pairs={{0,16},{1,17},{2,18},{3,19},{4,20},{5,21},{6,22},{7,23},{8,24},{9,... | collective-permute-start | bytes 4177928 | tf_op jit(solution)/shard_map/ppermute | solution.py:36
  28.0 18.7 %all-to-all-start = ((f32[4,2,80,320]{3,2,1,0:T(8,128)}), f32[4,2,80,320]{3,2,1,0:T(8,128)}, u32[]{:S(2)}, u32[]{:S(2)}) async-start(f32[4,2,80,320]{3,2,1,0:T(8,128)} %get-tuple-element.45), calls=%async_computation | async-start | bytes 1966080 | tf_op jit(solution)/shard_map/all_to_all | solution.py:41
  51.4 5.5 %collective-permute-start.8 = (bf16[320,2176]{1,0:T(8,128)(2,1)S(1)}, bf16[320,2176]{1,0:T(8,128)(2,1)}, u32[]{:S(2)}, u32[]{:S(2)}) collective-permute-start(bf16[320,2176]{1,0:T(8,128)(2,1)S(1)} %broadcast_select_fusion), channel_id=1, source_target_pairs={{0,8},{1,9},{2,10},{3,11},{4,12},{5,13},{6,14},{7,15},{8,0},{9,1},... | collective-permute-start | bytes 4177928 | tf_op jit(solution)/shard_map/ppermute | solution.py:36
  53.0 5.1 %collective-permute-start.7 = (bf16[320,2176]{1,0:T(8,128)(2,1)}, bf16[320,2176]{1,0:T(8,128)(2,1)}, u32[]{:S(2)}, u32[]{:S(2)}) collective-permute-start(bf16[320,2176]{1,0:T(8,128)(2,1)} %collective-permute-done.1.refs_1_.refs_6_.refs_3_), channel_id=1, source_target_pairs={{0,8},{1,9},{2,10},{3,11},{4,12},{5,13},{6,14},{7,15},{8,0},{9,1},... | collective-permute-start | bytes 4177928 | tf_op jit(solution)/shard_map/ppermute | solution.py:36
  53.1 44.8 %collective-permute-start.4 = (bf16[320,2176]{1,0:T(8,128)(2,1)}, bf16[320,2176]{1,0:T(8,128)(2,1)S(1)}, u32[]{:S(2)}, u32[]{:S(2)}) collective-permute-start(bf16[320,2176]{1,0:T(8,128)(2,1)} %get-tuple-element.49), channel_id=1, source_target_pairs={{0,48},{1,49},{2,50},{3,51},{4,52},{5,53},{6,54},{7,55},{8,56},{9,... | collective-permute-start | bytes 4177928 | tf_op jit(solution)/shard_map/ppermute | solution.py:36
  53.5 44.4 %collective-permute-start.5 = (bf16[320,2176]{1,0:T(8,128)(2,1)}, bf16[320,2176]{1,0:T(8,128)(2,1)}, u32[]{:S(2)}, u32[]{:S(2)}) collective-permute-start(bf16[320,2176]{1,0:T(8,128)(2,1)} %get-tuple-element.50), channel_id=1, source_target_pairs={{0,64},{1,65},{2,66},{3,67},{4,68},{5,69},{6,70},{7,71},{8,72},{9,... | collective-permute-start | bytes 4177928 | tf_op jit(solution)/shard_map/ppermute | solution.py:36
  53.6 44.3 %collective-permute-start.6 = (bf16[320,2176]{1,0:T(8,128)(2,1)}, bf16[320,2176]{1,0:T(8,128)(2,1)S(1)}, u32[]{:S(2)}, u32[]{:S(2)}) collective-permute-start(bf16[320,2176]{1,0:T(8,128)(2,1)} %collective-permute-done.1.refs_1_.refs_6_.refs_3_), channel_id=1, source_target_pairs={{0,16},{1,17},{2,18},{3,19},{4,20},{5,21},{6,22},{7,23},{8,24},{9,... | collective-permute-start | bytes 4177928 | tf_op jit(solution)/shard_map/ppermute | solution.py:36
  66.1 30.0 %all-to-all-start.1 = ((f32[4,2,168,320]{3,2,1,0:T(8,128)}), f32[4,2,168,320]{3,2,1,0:T(8,128)}, u32[]{:S(2)}, u32[]{:S(2)}) async-start(f32[4,2,168,320]{3,2,1,0:T(8,128)} %shard_map.58), calls=%async_computation.1 | async-start | bytes 4128768 | tf_op jit(solution)/shard_map/all_to_all | solution.py:41
  70.6 40.3 %collective-permute-start.9 = (bf16[320,2176]{1,0:T(8,128)(2,1)}, bf16[320,2176]{1,0:T(8,128)(2,1)}, u32[]{:S(2)}, u32[]{:S(2)}) collective-permute-start(bf16[320,2176]{1,0:T(8,128)(2,1)} %collective-permute-done.refs_7_.refs_12_.refs_5_), channel_id=1, source_target_pairs={{0,8},{1,9},{2,10},{3,11},{4,12},{5,13},{6,14},{7,15},{8,0},{9,1},... | collective-permute-start | bytes 4177928 | tf_op jit(solution)/shard_map/ppermute | solution.py:36
  97.9 12.9 %collective-permute-start.10 = (bf16[320,2176]{1,0:T(8,128)(2,1)S(1)}, bf16[320,2176]{1,0:T(8,128)(2,1)}, u32[]{:S(2)}, u32[]{:S(2)}) collective-permute-start(bf16[320,2176]{1,0:T(8,128)(2,1)S(1)} %collective-permute-done.4.refs_6_.refs_8_), channel_id=1, source_target_pairs={{0,8},{1,9},{2,10},{3,11},{4,12},{5,13},{6,14},{7,15},{8,0},{9,1},... | collective-permute-start | bytes 4177928 | tf_op jit(solution)/shard_map/ppermute | solution.py:36
  99.5 11.4 %collective-permute-start.11 = (bf16[320,2176]{1,0:T(8,128)(2,1)S(1)}, bf16[320,2176]{1,0:T(8,128)(2,1)}, u32[]{:S(2)}, u32[]{:S(2)}) collective-permute-start(bf16[320,2176]{1,0:T(8,128)(2,1)S(1)} %collective-permute-done.6.refs_9_.refs_10_), channel_id=1, source_target_pairs={{0,8},{1,9},{2,10},{3,11},{4,12},{5,13},{6,14},{7,15},{8,0},{9,1},... | collective-permute-start | bytes 4177928 | tf_op jit(solution)/shard_map/ppermute | solution.py:36
  101.0 18.8 %collective-permute-start.12 = (f32[248,320]{1,0:T(8,128)S(1)}, f32[248,320]{1,0:T(8,128)S(1)}, u32[]{:S(2)}, u32[]{:S(2)}) collective-permute-start(f32[248,320]{1,0:T(8,128)S(1)} %pad_maximum_fusion), channel_id=1, source_target_pairs={{0,4},{1,5},{2,6},{3,7},{4,0},{5,1},{6,2},{7,3},{8,12},{9,13},{10,... | collective-permute-start | bytes 952328 | tf_op jit(solution)/shard_map/ppermute | solution.py:36
  120.6 39.8 %all-to-all-start.2 = ((f32[8,3,80,320]{3,2,1,0:T(8,128)}), f32[8,3,80,320]{3,2,1,0:T(8,128)S(1)}, u32[]{:S(2)}, u32[]{:S(2)}) async-start(f32[8,3,80,320]{3,2,1,0:T(8,128)} %shard_map.60), calls=%async_computation.2 | async-start | bytes 5898240 | tf_op jit(solution)/shard_map/all_to_all | solution.py:552
  127.3 5.5 %collective-permute-start.15 = (f32[88,320]{1,0:T(8,128)S(1)}, f32[88,320]{1,0:T(8,128)S(1)}, u32[]{:S(2)}, u32[]{:S(2)}) collective-permute-start(f32[88,320]{1,0:T(8,128)S(1)} %pad_maximum_fusion.4), channel_id=1, source_target_pairs={{0,16},{1,17},{2,18},{3,19},{4,20},{5,21},{6,22},{7,23},{8,24},{9,... | collective-permute-start | bytes 337928 | tf_op jit(solution)/shard_map/ppermute | solution.py:36
  127.3 5.5 %collective-permute-start.14 = (f32[8,320]{1,0:T(8,128)S(1)}, f32[8,320]{1,0:T(8,128)S(1)}, u32[]{:S(2)}, u32[]{:S(2)}) collective-permute-start(f32[8,320]{1,0:T(8,128)S(1)} %slice.126), channel_id=1, source_target_pairs={{0,32},{1,33},{2,34},{3,35},{4,36},{5,37},{6,38},{7,39},{8,40},{9,... | collective-permute-start | bytes 30728 | tf_op jit(solution)/shard_map/ppermute | solution.py:36
  162.2 10.9 %collective-permute-start.16 = (f32[3,80,320]{2,1,0:T(8,128)}, f32[3,80,320]{2,1,0:T(8,128)}, u32[]{:S(2)}, u32[]{:S(2)}) collective-permute-start(f32[3,80,320]{2,1,0:T(8,128)} %reduce_sum.38.late), channel_id=1, source_target_pairs={{0,16},{1,17},{2,18},{3,19},{4,20},{5,21},{6,22},{7,23},{8,24},{9,... | collective-permute-start | bytes 921608 | tf_op jit(solution)/shard_map/ppermute | solution.py:36
  162.3 10.7 %collective-permute-start.17 = (f32[192,320]{1,0:T(8,128)S(1)}, f32[192,320]{1,0:T(8,128)S(1)}, u32[]{:S(2)}, u32[]{:S(2)}) collective-permute-start(f32[192,320]{1,0:T(8,128)S(1)} %pad_maximum_fusion.2), channel_id=1, source_target_pairs={{0,64},{1,65},{2,66},{3,67},{4,68},{5,69},{6,70},{7,71},{8,72},{9,... | collective-permute-start | bytes 737288 | tf_op jit(solution)/shard_map/ppermute | solution.py:36
  163.8 9.2 %collective-permute-start.18 = (f32[80,320]{1,0:T(8,128)S(1)}, f32[80,320]{1,0:T(8,128)S(1)}, u32[]{:S(2)}, u32[]{:S(2)}) collective-permute-start(f32[80,320]{1,0:T(8,128)S(1)} %slice_reduce_fusion), channel_id=1, source_target_pairs={{0,112},{1,113},{2,114},{3,115},{4,116},{5,117},{6,118},{7,119},{8... | collective-permute-start | bytes 307208 | tf_op jit(solution)/shard_map/ppermute | solution.py:36
  176.3 22.0 %all-to-all-start.3 = ((f32[8,80,320]{2,1,0:T(8,128)}), f32[8,80,320]{2,1,0:T(8,128)S(1)}, u32[]{:S(2)}, u32[]{:S(2)}) async-start(f32[8,80,320]{2,1,0:T(8,128)} %shard_map.61), calls=%async_computation.3 | async-start | bytes 1966080 | tf_op jit(solution)/shard_map/all_to_all | solution.py:570
  187.2 4.7 %collective-permute-start.19 = (f32[64,320]{1,0:T(8,128)S(1)}, f32[64,320]{1,0:T(8,128)S(1)}, u32[]{:S(2)}, u32[]{:S(2)}) collective-permute-start(f32[64,320]{1,0:T(8,128)S(1)} %pad_maximum_fusion.5), channel_id=1, source_target_pairs={{0,8},{1,9},{2,10},{3,11},{4,12},{5,13},{6,14},{7,15},{8,0},{9,1},... | collective-permute-start | bytes 245768 | tf_op jit(solution)/shard_map/ppermute | solution.py:36
  198.3 5.5 %collective-permute-start.20 = (f32[320,320]{1,0:T(8,128)S(1)}, f32[320,320]{1,0:T(8,128)S(1)}, u32[]{:S(2)}, u32[]{:S(2)}) collective-permute-start(f32[320,320]{1,0:T(8,128)S(1)} %constant_dynamic-slice_fusion), channel_id=1, source_target_pairs={{0,8},{1,9},{2,10},{3,11},{4,12},{5,13},{6,14},{7,15},{8,0},{9,1},... | collective-permute-start | bytes 1228808 | tf_op jit(solution)/shard_map/ppermute | solution.py:36
  (14 other events, 90.2 us)

commit v4 on v3

--- a/solution.py
+++ b/solution.py
@@ -25,15 +25,15 @@
     return (((yh % 2) * 4 + z % 4) * 2 + c % 2) * 8 + f % 8
 
 
-def route(dyh, dz, dc, dyl):
+def route(dyh, dz, dc, dyl, dx):
     return [
-        (place_index(yh, z, c, f), place_index(yh + dyh, z + dz, c + dc, f + 4 * dyl))
+        (place_index(yh, z, c, f), place_index(yh + dyh, z + dz, c + dc, (f // 4 + dyl) * 4 + (f + dx) % 4))
         for yh, z, c, f in places()
     ]
 
 
-def send(block, dyh=0, dz=0, dc=0, dyl=0):
-    return lax.ppermute(block, BOTH, route(dyh, dz, dc, dyl))
+def send(block, dyh=0, dz=0, dc=0, dyl=0, dx=0):
+    return lax.ppermute(block, BOTH, route(dyh, dz, dc, dyl, dx))
 
 
 def summed_along_x(tiles):
@@ -53,7 +53,7 @@
     return lax.dot_general(a, b, (((1,), (1,)), ((), ())), preferred_element_type=jnp.float32)
 
 
-CORE, YH, Z, HIGH, NEXT_HIGH, PREV_HIGH, ON_B2, ON_B3, ON_B5, ON_B6, LOWER, LOW, ONE, BY_ROW = range(14)
+CORE, YH, Z, HIGH, NEXT_HIGH, PREV_HIGH, ON_B2, ON_B3, ON_B5, ON_B6, LOWER, LOW, ONE, BY_ROW, X = range(15)
 
 
 def span(which, half):
@@ -195,7 +195,7 @@
 
 
 def half_kernel(jobs, info, *refs):
-    operands, (weight, energy, out, a, b, tiles, sems, out_sems) = refs[:-8], refs[-8:]
+    operands, (weight, energy), outs, (a, b, tiles, sems, out_sems) = refs[:-11], refs[-11:-9], refs[-9:-5], refs[-5:]
     rows, half = b.shape[2:]
     slices = tiles.shape[3]
     core = info[CORE]
@@ -226,7 +226,7 @@
     got = [fetch(k, job[0], job[3]) for k, job in enumerate(jobs)]
     for k in range(len(jobs)):
         for x in range(4):
-            go(energy, out.at[x, k, pl.ds(2 * slices, energy.shape[0])], 6 * k + 2 + x)
+            go(energy, outs[x].at[k, pl.ds(2 * slices, energy.shape[0])], 12 * k + 8 + x)
     for k, (_, on_b_at, on_b_other_at, half_at) in enumerate(jobs):
         got_b, got_a = got[k]
         w = weight[:, span(info[half_at], half)]
@@ -240,7 +240,9 @@
                 a[k, 2 * n + 1] = scaled(a[k, 2 * n], w)
 
             tiles[k, n] = gram(a[k, 2 * n + 1 - on_b], b[k, on_b]).reshape(tiles.shape[2:])
-            go(tiles.at[k, n], out.at[:, k, pl.ds(pl.multiple_of(owner * slices, 8), slices)], 6 * k + n)
+            at = pl.ds(pl.multiple_of(owner * slices, 8), slices)
+            for x in range(4):
+                go(tiles.at[k, n, (info[X] + x) % 4], outs[x].at[k, at], 12 * k + 4 * n + x)
     for copy in sent:
         copy.wait()
 
@@ -255,14 +257,14 @@
     return pl.pallas_call(
         kernel,
         in_specs=[SMEM] + [ANY] * (len(operands) - 2) + [VMEM] * 2,
-        out_specs=ANY,
-        out_shape=jax.ShapeDtypeStruct((4, 2, rows // 2 + classes, rows), jnp.float32),
+        out_specs=[ANY] * 4,
+        out_shape=[jax.ShapeDtypeStruct((2, rows // 2 + classes, rows), jnp.float32)] * 4,
         scratch_shapes=[
             pltpu.VMEM((2, 4, rows, half), jnp.bfloat16),
             pltpu.VMEM((2, 2, rows, half), jnp.bfloat16),
             pltpu.VMEM((2, 2, 4, rows // 4, rows), jnp.float32),
             pltpu.SemaphoreType.DMA((2, 3)),
-            pltpu.SemaphoreType.DMA((12,)),
+            pltpu.SemaphoreType.DMA((24,)),
         ],
         compiler_params=PARAMS,
         cost_estimate=COST,
@@ -488,6 +490,7 @@
             low.astype(jnp.int32),
             jnp.int32(1),
             by_row.astype(jnp.int32),
+            freq % 4,
         ]
     ).astype(jnp.int32)
 
@@ -522,7 +525,7 @@
         ((LOWER, ONE, CORE, YH), (LOW, ON_B3, ON_B3, HIGH)), info, partner_a, own, partner_s, sibling, own, partner_a,
         following_a, previous, third_a_s, third_a_s, previous, following_a, weight, partial_energy,
     )
-    half_pair = summed_along_x(half_pair)
+    half_pair = half_pair[0] + send(half_pair[1], dx=1) + send(half_pair[2], dx=2) + send(half_pair[3], dx=-1)
     following_b, partner_b, diagonal, half_pair = together(following_b, partner_b, diagonal, half_pair)
 
     own_yl = freq // 4
@@ -578,6 +581,8 @@
     column_energy = jnp.where(
         core == 0, jnp.concatenate(column_energy, 1), jnp.concatenate(column_energy[::-1], 1)
     )
+    labels, pieces = together(labels, pieces)
+    own_labels = lax.dynamic_slice_in_dim(labels, blk * rows, rows)
     column_labels = lax.dynamic_slice_in_dim(labels, freq * 2 * rows, 2 * rows)
     row_side = jnp.zeros((rows, 2 * rows), jnp.float32)
     column_side = jnp.zeros((rows, 2 * rows), jnp.float32)

time: 209 us -> 206 us (0.986)
  waiting for transfers between devices: 82.5 us -> 78.5 us
    all_to_all x2 -> x1, waiting for transfers between devices: 33.9 us -> 9.07 us  [summed_along_x(): lax.all_to_all(tiles, 'freq', 0, 0, axis_index_groups=groups, tiled=True)]
    ppermute x21 -> x24, waiting for transfers between devices: 15.5 us -> 35.7 us  [send(): return lax.ppermute(block, BOTH, route(dyh, dz, dc, dyl, dx))]
    ppermute x21 -> x24, starting transfers between devices: 29.2 us -> 34.4 us  [send(): return lax.ppermute(block, BOTH, route(dyh, dz, dc, dyl, dx))]
    all_to_all x2 -> x1, starting transfers between devices: 8.83 us -> 4.36 us  [summed_along_x(): lax.all_to_all(tiles, 'freq', 0, 0, axis_index_groups=groups, tiled=True)]
  transfers between devices with their start and end apart: 25 -> 27, of which waited for: 11 -> 11; matrix products, arithmetic and copies ran while one was open for 9% -> 10% of each run, Pallas kernels for 17% -> 17%
where the time goes in v4:
time: 206 us; the launch traced here: 204 us
  waiting for transfers between devices  78.5 us (38%)
  starting transfers between devices  50.1 us (24%)
  Pallas kernels  47.6 us (23%)
  other arithmetic  13.9 us (7%)
  local copies, waits for them, and re-layouts  10.4 us (5%)
  matrix products  3.51 us (2%)
    ppermute x24, waiting for transfers between devices, send(): return lax.ppermute(block, BOTH, route(dyh, dz, dc, dyl, dx))  35.7 us
    ppermute x24, starting transfers between devices, send(): return lax.ppermute(block, BOTH, route(dyh, dz, dc, dyl, dx))  34.4 us
    all_to_all x1, waiting for transfers between devices, per_device(): late = lax.all_to_all(late, 'freq', 0, 0, tiled=True)  27.9 us
    pallas_call x2, Pallas kernels, late_tiles(): pl.pallas_call(kernel, in_specs=specs, out_specs=ANY, out_shape=jax.Shape...  18 us
    all_to_all x1, waiting for transfers between devices, summed_along_x(): lax.all_to_all(tiles, 'freq', 0, 0, axis_index_groups=groups, tiled=True)  9.07 us
    pallas_call x1, Pallas kernels, half_tiles(): pl.pallas_call(kernel, in_specs=[SMEM] + [ANY] * (len(operands) - 2) + [V...  8.15 us
    pallas_call x1, Pallas kernels, first_tiles(): pl.pallas_call(first_kernel, in_specs=[SMEM, ANY, ANY, VMEM], out_specs=[...  7.67 us
    all_to_all x1, starting transfers between devices, per_device(): lax.all_to_all(pieces, 'freq', 0, 0, tiled=True).reshape(2 * rows, rows)  6.73 us
  transfers between devices with their start and end apart: 27, of which 11 were waited for; matrix products, arithmetic and copies ran while one was open for 10% of the time, Pallas kernels for 17%

profile of v4, /device:TPU:1, one launch (start us, length us, event | category | flops | bytes accessed | tf_op | source)
XLA Modules:
  0.0 204.4 jit_solution(8700887735752595732)
XLA Ops:
  2.2 6.7 %shard_map.55 = (bf16[320,4352]{1,0:T(8,128)(2,1)}, bf16[320,2176]{1,0:T(8,128)(2,1)}, bf16[320,2176]{1,0:T(8,128)(2,1)}, bf16[320,2176]{1,0:T(8,128)(2,1)}, bf16[8,4352]{1,0:T(8,128)(2,1)}) custom-call(s32[15]{0:T(128)} %stack.79.info.refs_0_, bf16[320,8]{1,0:T(8,128)(2,1)} %fusion.6.hot, bf16[320,4352]{1,0:T(8,128)(2,1)} %spectra.1, s32[8,2176]{1,0:T(8,128)} %wedges.1), custom_call_target="tpu_custom_call" | custom-call | flops 1024 | bytes 1024 | tf_op jit(solution)/shard_map/pallas_call | solution.py:93
  10.3 3.8 %collective-permute-start = (bf16[320,2176]{1,0:T(8,128)(2,1)}, bf16[320,2176]{1,0:T(8,128)(2,1)}, u32[]{:S(2)}, u32[]{:S(2)}) collective-permute-start(bf16[320,2176]{1,0:T(8,128)(2,1)} %get-tuple-element.44), channel_id=1, source_target_pairs={{0,48},{1,49},{2,50},{3,51},{4,52},{5,53},{6,54},{7,55},{8,56},{9,... | collective-permute-start | bytes 4177928 | tf_op jit(solution)/shard_map/ppermute | solution.py:36
  14.2 2.9 %collective-permute-start.1 = (bf16[320,2176]{1,0:T(8,128)(2,1)}, bf16[320,2176]{1,0:T(8,128)(2,1)}, u32[]{:S(2)}, u32[]{:S(2)}) collective-permute-start(bf16[320,2176]{1,0:T(8,128)(2,1)} %get-tuple-element.45), channel_id=1, source_target_pairs={{0,64},{1,65},{2,66},{3,67},{4,68},{5,69},{6,70},{7,71},{8,72},{9,... | collective-permute-start | bytes 4177928 | tf_op jit(solution)/shard_map/ppermute | solution.py:36
  20.4 7.7 %shard_map.57 = (f32[4,2,80,320]{3,2,1,0:T(8,128)}, bf16[320,4352]{1,0:T(8,128)(2,1)}) custom-call(s32[15]{0:T(128)} %stack.79.info.refs_0_, bf16[320,4352]{1,0:T(8,128)(2,1)} %get-tuple-element.52.own.refs_2_.refs_5_.refs_1_, bf16[320,4352]{1,0:T(8,128)(2,1)} %collective-permute-done.3.sibling.refs_4_, f32[1,4352]{1,0:T(1,128)} %shard_map.56.weight.refs_13_.refs_11_), custom_call_target="tpu_custom_call" | custom-call | flops 1024 | bytes 1024 | tf_op jit(solution)/shard_map/pallas_call | solution.py:177
  28.1 4.4 %all-to-all-start = ((f32[4,2,80,320]{3,2,1,0:T(8,128)}), f32[4,2,80,320]{3,2,1,0:T(8,128)}, u32[]{:S(2)}, u32[]{:S(2)}) async-start(f32[4,2,80,320]{3,2,1,0:T(8,128)} %get-tuple-element.50), calls=%async_computation | async-start | bytes 1966080 | tf_op jit(solution)/shard_map/all_to_all | solution.py:41
  32.4 3.5 %fusion.refs_14_ = f32[8,320]{1,0:T(8,128)} fusion(bf16[8,4352]{1,0:T(8,128)(2,1)S(1)} %copy-done.12, bf16[320,4352]{1,0:T(8,128)(2,1)S(1)} %copy-done, f32[4352]{0:T(1024)S(1)} %reduce.1), kind=kOutput, calls=%fused_computation | convolution fusion | flops 137871360 | bytes 2882560 | tf_op jit(solution)/shard_map/dot_general | solution.py:512
  37.7 9.1 %all-to-all-done = f32[4,2,80,320]{3,2,1,0:T(8,128)} async-done(((f32[4,2,80,320]{3,2,1,0:T(8,128)}), f32[4,2,80,320]{3,2,1,0:T(8,128)}, u32[]{:S(2)}, u32[]{:S(2)}) %all-to-all-start) | async-done | bytes 819232 | tf_op jit(solution)/shard_map/all_to_all | solution.py:41
  58.3 8.2 %shard_map.58 = (f32[2,168,320]{2,1,0:T(8,128)}, f32[2,168,320]{2,1,0:T(8,128)}, f32[2,168,320]{2,1,0:T(8,128)}, f32[2,168,320]{2,1,0:T(8,128)}) custom-call(s32[15]{0:T(128)} %stack.79.info.refs_0_, bf16[320,2176]{1,0:T(8,128)(2,1)} %collective-permute-done.1.refs_1_.refs_6_.refs_3_, bf16[320,4352]{1,0:T(8,128)(2,1)} %get-tuple-element.52.own.refs_2_.refs_5_.refs_1_, ...), custom_call_target="tpu_custom_call" | custom-call | flops 1024 | bytes 1024 | tf_op jit(solution)/shard_map/pallas_call | solution.py:257
  70.1 10.6 %collective-permute-done.9 = f32[2,168,320]{2,1,0:T(8,128)S(1)} collective-permute-done((f32[2,168,320]{2,1,0:T(8,128)}, f32[2,168,320]{2,1,0:T(8,128)S(1)}, u32[]{:S(2)}, u32[]{:S(2)}) %collective-permute-start.9) | collective-permute-done | bytes 430112 | tf_op jit(solution)/shard_map/ppermute | solution.py:36
  82.0 10.7 %collective-permute-done.10 = f32[2,168,320]{2,1,0:T(8,128)S(1)} collective-permute-done((f32[2,168,320]{2,1,0:T(8,128)}, f32[2,168,320]{2,1,0:T(8,128)S(1)}, u32[]{:S(2)}, u32[]{:S(2)}) %collective-permute-start.10) | collective-permute-done | bytes 430112 | tf_op jit(solution)/shard_map/ppermute | solution.py:36
  98.3 8.8 %shard_map.59.refs_12_ = f32[8,3,80,320]{3,2,1,0:T(8,128)} custom-call(s32[15]{0:T(128)} %stack.79.info.refs_0_, bf16[320,4352]{1,0:T(8,128)(2,1)} %get-tuple-element.52.own.refs_2_.refs_5_.refs_1_, bf16[320,4352]{1,0:T(8,128)(2,1)} %get-tuple-element.65.refs_2_, bf16[320,2176]{1,0:T(8,128)(2,1)} %collective-permute-done.1.refs_1_.refs_6_.refs_3_, ...), custom_call_target="tpu_custom_call" | custom-call | flops 1024 | bytes 1024 | tf_op jit(solution)/shard_map/pallas_call | solution.py:375
  107.1 9.2 %shard_map.60 = f32[8,3,80,320]{3,2,1,0:T(8,128)} custom-call(s32[15]{0:T(128)} %stack.79.info.refs_0_, bf16[320,4352]{1,0:T(8,128)(2,1)} %get-tuple-element.52.own.refs_2_.refs_5_.refs_1_, bf16[320,4352]{1,0:T(8,128)(2,1)} %get-tuple-element.65.refs_2_, ...), custom_call_target="tpu_custom_call", output_to_operand_aliasing={{}: (12, {})} | custom-call | flops 1024 | bytes 1024 | tf_op jit(solution)/shard_map/pallas_call | solution.py:375
  117.1 4.6 %all-to-all-start.1 = ((f32[8,3,80,320]{3,2,1,0:T(8,128)}), f32[8,3,80,320]{3,2,1,0:T(8,128)S(1)}, u32[]{:S(2)}, u32[]{:S(2)}) async-start(f32[8,3,80,320]{3,2,1,0:T(8,128)} %shard_map.60), calls=%async_computation.1 | async-start | bytes 5898240 | tf_op jit(solution)/shard_map/all_to_all | solution.py:555
  123.0 2.7 %collective-permute-start.16 = (f32[88,320]{1,0:T(8,128)S(1)}, f32[88,320]{1,0:T(8,128)S(1)}, u32[]{:S(2)}, u32[]{:S(2)}) collective-permute-start(f32[88,320]{1,0:T(8,128)S(1)} %pad_maximum_fusion.4), channel_id=1, source_target_pairs={{0,48},{1,49},{2,50},{3,51},{4,52},{5,53},{6,54},{7,55},{8,56},{9,... | collective-permute-start | bytes 337928 | tf_op jit(solution)/shard_map/ppermute | solution.py:36
  125.7 2.7 %collective-permute-done.18.third_back = f32[88,320]{1,0:T(8,128)S(1)} collective-permute-done((f32[88,320]{1,0:T(8,128)S(1)}, f32[88,320]{1,0:T(8,128)S(1)}, u32[]{:S(2)}, u32[]{:S(2)}) %collective-permute-start.18) | collective-permute-done | bytes 112672 | tf_op jit(solution)/shard_map/ppermute | solution.py:36
  130.0 27.9 %all-to-all-done.1 = f32[8,3,80,320]{3,2,1,0:T(8,128)S(1)} async-done(((f32[8,3,80,320]{3,2,1,0:T(8,128)}), f32[8,3,80,320]{3,2,1,0:T(8,128)S(1)}, u32[]{:S(2)}, u32[]{:S(2)}) %all-to-all-start.1) | async-done | bytes 2457632 | tf_op jit(solution)/shard_map/all_to_all | solution.py:555
  162.3 4.3 %collective-permute-start.21 = (f32[80,320]{1,0:T(8,128)}, f32[80,320]{1,0:T(8,128)S(1)}, u32[]{:S(2)}, u32[]{:S(2)}) collective-permute-start(f32[80,320]{1,0:T(8,128)} %slice_reduce_fusion), channel_id=1, source_target_pairs={{0,112},{1,113},{2,114},{3,115},{4,116},{5,117},{6,118},{7,119},{8... | collective-permute-start | bytes 307208 | tf_op jit(solution)/shard_map/ppermute | solution.py:36
  166.7 4.9 %collective-permute-done.21.from_diagonal = f32[80,320]{1,0:T(8,128)S(1)} collective-permute-done((f32[80,320]{1,0:T(8,128)}, f32[80,320]{1,0:T(8,128)S(1)}, u32[]{:S(2)}, u32[]{:S(2)}) %collective-permute-start.21) | collective-permute-done | bytes 102432 | tf_op jit(solution)/shard_map/ppermute | solution.py:36
  174.8 6.7 %all-to-all-start.2 = ((f32[8,80,320]{2,1,0:T(8,128)}), f32[8,80,320]{2,1,0:T(8,128)S(1)}, u32[]{:S(2)}, u32[]{:S(2)}) async-start(f32[8,80,320]{2,1,0:T(8,128)} %shard_map.61), calls=%async_computation.2 | async-start | bytes 1966080 | tf_op jit(solution)/shard_map/all_to_all | solution.py:573
  183.4 4.0 %collective-permute-start.22 = (f32[64,320]{1,0:T(8,128)S(1)}, f32[64,320]{1,0:T(8,128)S(1)}, u32[]{:S(2)}, u32[]{:S(2)}) collective-permute-start(f32[64,320]{1,0:T(8,128)S(1)} %pad_maximum_fusion.5), channel_id=1, source_target_pairs={{0,8},{1,9},{2,10},{3,11},{4,12},{5,13},{6,14},{7,15},{8,0},{9,1},... | collective-permute-start | bytes 245768 | tf_op jit(solution)/shard_map/ppermute | solution.py:36
  189.1 5.9 %all-to-all-done.2 = f32[8,80,320]{2,1,0:T(8,128)S(1)} async-done(((f32[8,80,320]{2,1,0:T(8,128)}), f32[8,80,320]{2,1,0:T(8,128)S(1)}, u32[]{:S(2)}, u32[]{:S(2)}) %all-to-all-start.2) | async-done | bytes 819232 | tf_op jit(solution)/shard_map/all_to_all | solution.py:573
  195.0 2.6 %collective-permute-start.23 = (f32[320,320]{1,0:T(8,128)S(1)}, f32[320,320]{1,0:T(8,128)S(1)}, u32[]{:S(2)}, u32[]{:S(2)}) collective-permute-start(f32[320,320]{1,0:T(8,128)S(1)} %constant_dynamic-slice_fusion), channel_id=1, source_target_pairs={{0,8},{1,9},{2,10},{3,11},{4,12},{5,13},{6,14},{7,15},{8,0},{9,1},... | collective-permute-start | bytes 1228808 | tf_op jit(solution)/shard_map/ppermute | solution.py:36
  197.7 3.2 %add_sqrt_fusion.root = f32[320,640]{1,0:T(8,128)} fusion(f32[640]{0:T(1024)S(1)} %get-tuple-element.92, f32[640]{0:T(1024)S(1)} %get-tuple-element.93, f32[640]{0:T(1024)S(1)} %get-tuple-element.94, f32[640]{0:T(1024)S(1)} %get-tuple-element.95, f32[640]{0:T(1024)S(1)} %get-tuple-element.96, f32[640]{0:T(1024)S(1)} %get-tuple-element.97, ...), kind=kLoop, calls=%fused_computation.7 | loop fusion | flops 3686400 | bytes 857600 | tf_op jit(solution)/shard_map/sqrt | solution.py:592
  201.7 2.7 %shard_map.62 = f32[320,640]{1,0:T(8,128)} custom-call(s32[15]{0:T(128)} %stack.79.info.refs_0_, f32[640,320]{1,0:T(8,128)} %bitcast.33, f32[320,320]{1,0:T(8,128)} %copy-done.5, f32[320,640]{1,0:T(8,128)} %add_sqrt_fusion.root), custom_call_target="tpu_custom_call" | custom-call | tf_op jit(solution)/shard_map/pallas_call | solution.py:441
  (103 shorter events, 46.4 us)
Async XLA Ops:
  8.9 11.4 %collective-permute-start.3 = (bf16[320,4352]{1,0:T(8,128)(2,1)}, bf16[320,4352]{1,0:T(8,128)(2,1)}, u32[]{:S(2)}, u32[]{:S(2)}) collective-permute-start(bf16[320,4352]{1,0:T(8,128)(2,1)} %get-tuple-element.52.own.refs_2_.refs_5_.refs_1_), channel_id=1, source_target_pairs={{0,8},{1,9},{2,10},{3,11},{4,12},{5,13},{6,14},{7,15},{8,0},{9,1},... | collective-permute-start | bytes 8355848 | tf_op jit(solution)/shard_map/ppermute | solution.py:36
  10.3 37.7 %collective-permute-start = (bf16[320,2176]{1,0:T(8,128)(2,1)}, bf16[320,2176]{1,0:T(8,128)(2,1)}, u32[]{:S(2)}, u32[]{:S(2)}) collective-permute-start(bf16[320,2176]{1,0:T(8,128)(2,1)} %get-tuple-element.44), channel_id=1, source_target_pairs={{0,48},{1,49},{2,50},{3,51},{4,52},{5,53},{6,54},{7,55},{8,56},{9,... | collective-permute-start | bytes 4177928 | tf_op jit(solution)/shard_map/ppermute | solution.py:36
  14.2 33.9 %collective-permute-start.1 = (bf16[320,2176]{1,0:T(8,128)(2,1)}, bf16[320,2176]{1,0:T(8,128)(2,1)}, u32[]{:S(2)}, u32[]{:S(2)}) collective-permute-start(bf16[320,2176]{1,0:T(8,128)(2,1)} %get-tuple-element.45), channel_id=1, source_target_pairs={{0,64},{1,65},{2,66},{3,67},{4,68},{5,69},{6,70},{7,71},{8,72},{9,... | collective-permute-start | bytes 4177928 | tf_op jit(solution)/shard_map/ppermute | solution.py:36
  17.1 33.0 %collective-permute-start.2 = (bf16[320,2176]{1,0:T(8,128)(2,1)}, bf16[320,2176]{1,0:T(8,128)(2,1)}, u32[]{:S(2)}, u32[]{:S(2)}) collective-permute-start(bf16[320,2176]{1,0:T(8,128)(2,1)} %get-tuple-element.46), channel_id=1, source_target_pairs={{0,16},{1,17},{2,18},{3,19},{4,20},{5,21},{6,22},{7,23},{8,24},{9,... | collective-permute-start | bytes 4177928 | tf_op jit(solution)/shard_map/ppermute | solution.py:36
  28.1 18.7 %all-to-all-start = ((f32[4,2,80,320]{3,2,1,0:T(8,128)}), f32[4,2,80,320]{3,2,1,0:T(8,128)}, u32[]{:S(2)}, u32[]{:S(2)}) async-start(f32[4,2,80,320]{3,2,1,0:T(8,128)} %get-tuple-element.50), calls=%async_computation | async-start | bytes 1966080 | tf_op jit(solution)/shard_map/all_to_all | solution.py:41
  51.6 5.5 %collective-permute-start.8 = (bf16[320,2176]{1,0:T(8,128)(2,1)S(1)}, bf16[320,2176]{1,0:T(8,128)(2,1)}, u32[]{:S(2)}, u32[]{:S(2)}) collective-permute-start(bf16[320,2176]{1,0:T(8,128)(2,1)S(1)} %broadcast_select_fusion), channel_id=1, source_target_pairs={{0,8},{1,9},{2,10},{3,11},{4,12},{5,13},{6,14},{7,15},{8,0},{9,1},... | collective-permute-start | bytes 4177928 | tf_op jit(solution)/shard_map/ppermute | solution.py:36
  53.2 42.0 %collective-permute-start.4 = (bf16[320,2176]{1,0:T(8,128)(2,1)}, bf16[320,2176]{1,0:T(8,128)(2,1)S(1)}, u32[]{:S(2)}, u32[]{:S(2)}) collective-permute-start(bf16[320,2176]{1,0:T(8,128)(2,1)} %get-tuple-element.54), channel_id=1, source_target_pairs={{0,48},{1,49},{2,50},{3,51},{4,52},{5,53},{6,54},{7,55},{8,56},{9,... | collective-permute-start | bytes 4177928 | tf_op jit(solution)/shard_map/ppermute | solution.py:36
  53.5 41.8 %collective-permute-start.5 = (bf16[320,2176]{1,0:T(8,128)(2,1)}, bf16[320,2176]{1,0:T(8,128)(2,1)}, u32[]{:S(2)}, u32[]{:S(2)}) collective-permute-start(bf16[320,2176]{1,0:T(8,128)(2,1)} %get-tuple-element.55), channel_id=1, source_target_pairs={{0,64},{1,65},{2,66},{3,67},{4,68},{5,69},{6,70},{7,71},{8,72},{9,... | collective-permute-start | bytes 4177928 | tf_op jit(solution)/shard_map/ppermute | solution.py:36
  53.7 41.7 %collective-permute-start.6 = (bf16[320,2176]{1,0:T(8,128)(2,1)}, bf16[320,2176]{1,0:T(8,128)(2,1)S(1)}, u32[]{:S(2)}, u32[]{:S(2)}) collective-permute-start(bf16[320,2176]{1,0:T(8,128)(2,1)} %collective-permute-done.1.refs_1_.refs_6_.refs_3_), channel_id=1, source_target_pairs={{0,16},{1,17},{2,18},{3,19},{4,20},{5,21},{6,22},{7,23},{8,24},{9,... | collective-permute-start | bytes 4177928 | tf_op jit(solution)/shard_map/ppermute | solution.py:36
  66.4 14.3 %collective-permute-start.9 = (f32[2,168,320]{2,1,0:T(8,128)}, f32[2,168,320]{2,1,0:T(8,128)S(1)}, u32[]{:S(2)}, u32[]{:S(2)}) collective-permute-start(f32[2,168,320]{2,1,0:T(8,128)} %get-tuple-element.61), channel_id=1, source_target_pairs={{0,1},{1,2},{2,3},{3,0},{4,5},{5,6},{6,7},{7,4},{8,9},{9,10},{10,1... | collective-permute-start | bytes 1290248 | tf_op jit(solution)/shard_map/ppermute | solution.py:36
  67.7 25.0 %collective-permute-start.10 = (f32[2,168,320]{2,1,0:T(8,128)}, f32[2,168,320]{2,1,0:T(8,128)S(1)}, u32[]{:S(2)}, u32[]{:S(2)}) collective-permute-start(f32[2,168,320]{2,1,0:T(8,128)} %get-tuple-element.62), channel_id=1, source_target_pairs={{0,2},{1,3},{2,0},{3,1},{4,6},{5,7},{6,4},{7,5},{8,10},{9,11},{10,... | collective-permute-start | bytes 1290248 | tf_op jit(solution)/shard_map/ppermute | solution.py:36
  80.7 13.4 %collective-permute-start.11 = (f32[2,168,320]{2,1,0:T(8,128)}, f32[2,168,320]{2,1,0:T(8,128)S(1)}, u32[]{:S(2)}, u32[]{:S(2)}) collective-permute-start(f32[2,168,320]{2,1,0:T(8,128)} %get-tuple-element.63), channel_id=1, source_target_pairs={{0,3},{1,0},{2,1},{3,2},{4,7},{5,4},{6,5},{7,6},{8,11},{9,8},{10,9... | collective-permute-start | bytes 1290248 | tf_op jit(solution)/shard_map/ppermute | solution.py:36
  92.7 14.4 %collective-permute-start.12 = (bf16[320,2176]{1,0:T(8,128)(2,1)}, bf16[320,2176]{1,0:T(8,128)(2,1)}, u32[]{:S(2)}, u32[]{:S(2)}) collective-permute-start(bf16[320,2176]{1,0:T(8,128)(2,1)} %collective-permute-done.refs_7_.refs_12_.refs_5_), channel_id=1, source_target_pairs={{0,8},{1,9},{2,10},{3,11},{4,12},{5,13},{6,14},{7,15},{8,0},{9,1},... | collective-permute-start | bytes 4177928 | tf_op jit(solution)/shard_map/ppermute | solution.py:36
  95.3 11.8 %collective-permute-start.13 = (bf16[320,2176]{1,0:T(8,128)(2,1)S(1)}, bf16[320,2176]{1,0:T(8,128)(2,1)}, u32[]{:S(2)}, u32[]{:S(2)}) collective-permute-start(bf16[320,2176]{1,0:T(8,128)(2,1)S(1)} %collective-permute-done.4.refs_6_.refs_8_), channel_id=1, source_target_pairs={{0,8},{1,9},{2,10},{3,11},{4,12},{5,13},{6,14},{7,15},{8,0},{9,1},... | collective-permute-start | bytes 4177928 | tf_op jit(solution)/shard_map/ppermute | solution.py:36
  96.4 10.7 %collective-permute-start.14 = (bf16[320,2176]{1,0:T(8,128)(2,1)S(1)}, bf16[320,2176]{1,0:T(8,128)(2,1)}, u32[]{:S(2)}, u32[]{:S(2)}) collective-permute-start(bf16[320,2176]{1,0:T(8,128)(2,1)S(1)} %collective-permute-done.6.refs_9_.refs_10_), channel_id=1, source_target_pairs={{0,8},{1,9},{2,10},{3,11},{4,12},{5,13},{6,14},{7,15},{8,0},{9,1},... | collective-permute-start | bytes 4177928 | tf_op jit(solution)/shard_map/ppermute | solution.py:36
  98.0 18.4 %collective-permute-start.15 = (f32[248,320]{1,0:T(8,128)S(1)}, f32[248,320]{1,0:T(8,128)S(1)}, u32[]{:S(2)}, u32[]{:S(2)}) collective-permute-start(f32[248,320]{1,0:T(8,128)S(1)} %pad_maximum_fusion), channel_id=1, source_target_pairs={{0,4},{1,5},{2,6},{3,7},{4,0},{5,1},{6,2},{7,3},{8,12},{9,13},{10,... | collective-permute-start | bytes 952328 | tf_op jit(solution)/shard_map/ppermute | solution.py:36
  117.1 40.8 %all-to-all-start.1 = ((f32[8,3,80,320]{3,2,1,0:T(8,128)}), f32[8,3,80,320]{3,2,1,0:T(8,128)S(1)}, u32[]{:S(2)}, u32[]{:S(2)}) async-start(f32[8,3,80,320]{3,2,1,0:T(8,128)} %shard_map.60), calls=%async_computation.1 | async-start | bytes 5898240 | tf_op jit(solution)/shard_map/all_to_all | solution.py:555
  122.9 5.4 %collective-permute-start.18 = (f32[88,320]{1,0:T(8,128)S(1)}, f32[88,320]{1,0:T(8,128)S(1)}, u32[]{:S(2)}, u32[]{:S(2)}) collective-permute-start(f32[88,320]{1,0:T(8,128)S(1)} %pad_maximum_fusion.4), channel_id=1, source_target_pairs={{0,16},{1,17},{2,18},{3,19},{4,20},{5,21},{6,22},{7,23},{8,24},{9,... | collective-permute-start | bytes 337928 | tf_op jit(solution)/shard_map/ppermute | solution.py:36
  159.8 11.8 %collective-permute-start.19 = (f32[3,80,320]{2,1,0:T(8,128)}, f32[3,80,320]{2,1,0:T(8,128)}, u32[]{:S(2)}, u32[]{:S(2)}) collective-permute-start(f32[3,80,320]{2,1,0:T(8,128)} %reduce_sum.28.late), channel_id=1, source_target_pairs={{0,16},{1,17},{2,18},{3,19},{4,20},{5,21},{6,22},{7,23},{8,24},{9,... | collective-permute-start | bytes 921608 | tf_op jit(solution)/shard_map/ppermute | solution.py:36
  160.6 11.0 %collective-permute-start.20 = (f32[192,320]{1,0:T(8,128)}, f32[192,320]{1,0:T(8,128)S(1)}, u32[]{:S(2)}, u32[]{:S(2)}) collective-permute-start(f32[192,320]{1,0:T(8,128)} %pad_maximum_fusion.2), channel_id=1, source_target_pairs={{0,64},{1,65},{2,66},{3,67},{4,68},{5,69},{6,70},{7,71},{8,72},{9,... | collective-permute-start | bytes 737288 | tf_op jit(solution)/shard_map/ppermute | solution.py:36
  162.3 9.2 %collective-permute-start.21 = (f32[80,320]{1,0:T(8,128)}, f32[80,320]{1,0:T(8,128)S(1)}, u32[]{:S(2)}, u32[]{:S(2)}) collective-permute-start(f32[80,320]{1,0:T(8,128)} %slice_reduce_fusion), channel_id=1, source_target_pairs={{0,112},{1,113},{2,114},{3,115},{4,116},{5,117},{6,118},{7,119},{8... | collective-permute-start | bytes 307208 | tf_op jit(solution)/shard_map/ppermute | solution.py:36
  174.8 20.2 %all-to-all-start.2 = ((f32[8,80,320]{2,1,0:T(8,128)}), f32[8,80,320]{2,1,0:T(8,128)S(1)}, u32[]{:S(2)}, u32[]{:S(2)}) async-start(f32[8,80,320]{2,1,0:T(8,128)} %shard_map.61), calls=%async_computation.2 | async-start | bytes 1966080 | tf_op jit(solution)/shard_map/all_to_all | solution.py:573
  183.4 5.6 %collective-permute-start.22 = (f32[64,320]{1,0:T(8,128)S(1)}, f32[64,320]{1,0:T(8,128)S(1)}, u32[]{:S(2)}, u32[]{:S(2)}) collective-permute-start(f32[64,320]{1,0:T(8,128)S(1)} %pad_maximum_fusion.5), channel_id=1, source_target_pairs={{0,8},{1,9},{2,10},{3,11},{4,12},{5,13},{6,14},{7,15},{8,0},{9,1},... | collective-permute-start | bytes 245768 | tf_op jit(solution)/shard_map/ppermute | solution.py:36
  195.0 5.8 %collective-permute-start.23 = (f32[320,320]{1,0:T(8,128)S(1)}, f32[320,320]{1,0:T(8,128)S(1)}, u32[]{:S(2)}, u32[]{:S(2)}) collective-permute-start(f32[320,320]{1,0:T(8,128)S(1)} %constant_dynamic-slice_fusion), channel_id=1, source_target_pairs={{0,8},{1,9},{2,10},{3,11},{4,12},{5,13},{6,14},{7,15},{8,0},{9,1},... | collective-permute-start | bytes 1228808 | tf_op jit(solution)/shard_map/ppermute | solution.py:36
  (16 other events, 99.5 us)

commit v5 on v4

--- a/solution.py
+++ b/solution.py
@@ -525,8 +525,22 @@
         ((LOWER, ONE, CORE, YH), (LOW, ON_B3, ON_B3, HIGH)), info, partner_a, own, partner_s, sibling, own, partner_a,
         following_a, previous, third_a_s, third_a_s, previous, following_a, weight, partial_energy,
     )
-    half_pair = half_pair[0] + send(half_pair[1], dx=1) + send(half_pair[2], dx=2) + send(half_pair[3], dx=-1)
-    following_b, partner_b, diagonal, half_pair = together(following_b, partner_b, diagonal, half_pair)
+    half_parts = [send(half_pair[1], dx=1), send(half_pair[2], dx=2), send(half_pair[3], dx=-1)]
+    following_b, partner_b, diagonal, kept, half_parts[0], half_parts[2] = together(
+        following_b, partner_b, diagonal, half_pair[0], half_parts[0], half_parts[2]
+    )
+
+    following_as = send(following_a, dc=1)
+    following_bs = send(following_b, dc=1)
+    diagonal_s = send(diagonal, dc=1)
+    late = late_tiles(
+        True, info, own, own_w, partner_a, partner_b, following_a, following_b, following_a, following_b,
+        diagonal, diagonal, weight,
+    )
+    late, following_as, following_bs, diagonal_s, *half_pair = together(
+        late, following_as, following_bs, diagonal_s, kept, *half_parts
+    )
+    half_pair = half_pair[0] + half_pair[1] + half_pair[2] + half_pair[3]
 
     own_yl = freq // 4
 
@@ -538,15 +552,7 @@
             half_pair[0, 2 * slices :],
         ]
 
-    following_as = send(following_a, dc=1)
-    following_bs = send(following_b, dc=1)
-    diagonal_s = send(diagonal, dc=1)
     early = send(jnp.concatenate(halves(1 - own_yl)), dyl=1)
-    late = late_tiles(
-        True, info, own, own_w, partner_a, partner_b, following_a, following_b, following_a, following_b,
-        diagonal, diagonal, weight,
-    )
-    late, following_as, following_bs, diagonal_s = together(late, following_as, following_bs, diagonal_s)
     late = late_tiles(
         False, info, own, own_w, partner_a, partner_b, following_as, following_bs, following_a, following_b,
         diagonal, diagonal_s, weight, late,

time: 206 us -> 204 us (level)
  starting transfers between devices: 50.1 us -> 47.2 us
    all_to_all x1, starting transfers between devices: 6.73 us -> 3.55 us  [per_device(): lax.all_to_all(pieces, 'freq', 0, 0, tiled=True).reshape(2 * rows, rows)]
  transfers between devices with their start and end apart: 27 -> 27, of which waited for: 11 -> 12; matrix products, arithmetic and copies ran while one was open for 10% -> 9% of each run, Pallas kernels for 17% -> 18%
where the time goes in v5:
time: 204 us; the launch traced here: 202 us
  waiting for transfers between devices  77.6 us (38%)
  Pallas kernels  47.7 us (23%)
  starting transfers between devices  47.2 us (23%)
  other arithmetic  14 us (7%)
  local copies, waits for them, and re-layouts  11.4 us (6%)
  matrix products  3.51 us (2%)
    ppermute x24, starting transfers between devices, send(): return lax.ppermute(block, BOTH, route(dyh, dz, dc, dyl, dx))  35.3 us
    ppermute x24, waiting for transfers between devices, send(): return lax.ppermute(block, BOTH, route(dyh, dz, dc, dyl, dx))  35.2 us
    all_to_all x1, waiting for transfers between devices, per_device(): late = lax.all_to_all(late, 'freq', 0, 0, tiled=True)  27.1 us
    pallas_call x2, Pallas kernels, late_tiles(): pl.pallas_call(kernel, in_specs=specs, out_specs=ANY, out_shape=jax.Shape...  18.1 us
    all_to_all x1, waiting for transfers between devices, summed_along_x(): lax.all_to_all(tiles, 'freq', 0, 0, axis_index_groups=groups, tiled=True)  9.03 us
    pallas_call x1, Pallas kernels, half_tiles(): pl.pallas_call(kernel, in_specs=[SMEM] + [ANY] * (len(operands) - 2) + [V...  8.15 us
    pallas_call x1, Pallas kernels, first_tiles(): pl.pallas_call(first_kernel, in_specs=[SMEM, ANY, ANY, VMEM], out_specs=[...  7.67 us
    pallas_call x1, Pallas kernels, masked_blocks(): pl.pallas_call(mask_kernel, grid_spec=pltpu.PrefetchScalarGridSpec(num_sc...  6.72 us
  transfers between devices with their start and end apart: 27, of which 12 were waited for; matrix products, arithmetic and copies ran while one was open for 9% of the time, Pallas kernels for 18%

profile of v5, /device:TPU:1, one launch (start us, length us, event | category | flops | bytes accessed | tf_op | source)
XLA Modules:
  0.0 201.8 jit_solution(4781817853647119707)
XLA Ops:
  2.2 6.7 %shard_map.55 = (bf16[320,4352]{1,0:T(8,128)(2,1)}, bf16[320,2176]{1,0:T(8,128)(2,1)}, bf16[320,2176]{1,0:T(8,128)(2,1)}, bf16[320,2176]{1,0:T(8,128)(2,1)}, bf16[8,4352]{1,0:T(8,128)(2,1)}) custom-call(s32[15]{0:T(128)} %stack.79.info.refs_0_, bf16[320,8]{1,0:T(8,128)(2,1)} %fusion.6.hot, bf16[320,4352]{1,0:T(8,128)(2,1)} %spectra.1, s32[8,2176]{1,0:T(8,128)} %wedges.1), custom_call_target="tpu_custom_call" | custom-call | flops 1024 | bytes 1024 | tf_op jit(solution)/shard_map/pallas_call | solution.py:93
  10.4 3.8 %collective-permute-start = (bf16[320,2176]{1,0:T(8,128)(2,1)}, bf16[320,2176]{1,0:T(8,128)(2,1)}, u32[]{:S(2)}, u32[]{:S(2)}) collective-permute-start(bf16[320,2176]{1,0:T(8,128)(2,1)} %get-tuple-element.50), channel_id=1, source_target_pairs={{0,48},{1,49},{2,50},{3,51},{4,52},{5,53},{6,54},{7,55},{8,56},{9,... | collective-permute-start | bytes 4177928 | tf_op jit(solution)/shard_map/ppermute | solution.py:36
  14.2 2.9 %collective-permute-start.1 = (bf16[320,2176]{1,0:T(8,128)(2,1)}, bf16[320,2176]{1,0:T(8,128)(2,1)}, u32[]{:S(2)}, u32[]{:S(2)}) collective-permute-start(bf16[320,2176]{1,0:T(8,128)(2,1)} %get-tuple-element.51), channel_id=1, source_target_pairs={{0,64},{1,65},{2,66},{3,67},{4,68},{5,69},{6,70},{7,71},{8,72},{9,... | collective-permute-start | bytes 4177928 | tf_op jit(solution)/shard_map/ppermute | solution.py:36
  20.4 7.7 %shard_map.57 = (f32[4,2,80,320]{3,2,1,0:T(8,128)}, bf16[320,4352]{1,0:T(8,128)(2,1)}) custom-call(s32[15]{0:T(128)} %stack.79.info.refs_0_, bf16[320,4352]{1,0:T(8,128)(2,1)} %get-tuple-element.58.own.refs_2_.refs_5_.refs_1_, bf16[320,4352]{1,0:T(8,128)(2,1)} %collective-permute-done.3.sibling.refs_4_, f32[1,4352]{1,0:T(1,128)} %shard_map.56.weight.refs_13_.refs_11_), custom_call_target="tpu_custom_call" | custom-call | flops 1024 | bytes 1024 | tf_op jit(solution)/shard_map/pallas_call | solution.py:177
  28.1 4.4 %all-to-all-start = ((f32[4,2,80,320]{3,2,1,0:T(8,128)}), f32[4,2,80,320]{3,2,1,0:T(8,128)}, u32[]{:S(2)}, u32[]{:S(2)}) async-start(f32[4,2,80,320]{3,2,1,0:T(8,128)} %get-tuple-element.56), calls=%async_computation | async-start | bytes 1966080 | tf_op jit(solution)/shard_map/all_to_all | solution.py:41
  32.5 3.5 %fusion.refs_14_ = f32[8,320]{1,0:T(8,128)} fusion(bf16[8,4352]{1,0:T(8,128)(2,1)S(1)} %copy-done.14, bf16[320,4352]{1,0:T(8,128)(2,1)S(1)} %copy-done, f32[4352]{0:T(1024)S(1)} %reduce.1), kind=kOutput, calls=%fused_computation | convolution fusion | flops 137871360 | bytes 2882560 | tf_op jit(solution)/shard_map/dot_general | solution.py:512
  37.7 9.0 %all-to-all-done = f32[4,2,80,320]{3,2,1,0:T(8,128)} async-done(((f32[4,2,80,320]{3,2,1,0:T(8,128)}), f32[4,2,80,320]{3,2,1,0:T(8,128)}, u32[]{:S(2)}, u32[]{:S(2)}) %all-to-all-start) | async-done | bytes 819232 | tf_op jit(solution)/shard_map/all_to_all | solution.py:41
  58.3 8.2 %shard_map.58 = (f32[2,168,320]{2,1,0:T(8,128)}, f32[2,168,320]{2,1,0:T(8,128)}, f32[2,168,320]{2,1,0:T(8,128)}, f32[2,168,320]{2,1,0:T(8,128)}) custom-call(s32[15]{0:T(128)} %stack.79.info.refs_0_, bf16[320,2176]{1,0:T(8,128)(2,1)} %collective-permute-done.1.refs_1_.refs_6_.refs_3_, bf16[320,4352]{1,0:T(8,128)(2,1)} %get-tuple-element.58.own.refs_2_.refs_5_.refs_1_, ...), custom_call_target="tpu_custom_call" | custom-call | flops 1024 | bytes 1024 | tf_op jit(solution)/shard_map/pallas_call | solution.py:257
  66.4 2.5 %collective-permute-start.10 = (f32[2,168,320]{2,1,0:T(8,128)}, f32[2,168,320]{2,1,0:T(8,128)S(1)}, u32[]{:S(2)}, u32[]{:S(2)}) collective-permute-start(f32[2,168,320]{2,1,0:T(8,128)} %get-tuple-element.69), channel_id=1, source_target_pairs={{0,3},{1,0},{2,1},{3,2},{4,7},{5,4},{6,5},{7,6},{8,11},{9,8},{10,9... | collective-permute-start | bytes 1290248 | tf_op jit(solution)/shard_map/ppermute | solution.py:36
  69.0 16.3 %collective-permute-done.4.refs_6_.refs_8_ = bf16[320,2176]{1,0:T(8,128)(2,1)S(1)} collective-permute-done((bf16[320,2176]{1,0:T(8,128)(2,1)}, bf16[320,2176]{1,0:T(8,128)(2,1)S(1)}, u32[]{:S(2)}, u32[]{:S(2)}) %collective-permute-start.4) | collective-permute-done | bytes 1392672 | tf_op jit(solution)/shard_map/ppermute | solution.py:36
  92.4 8.7 %shard_map.59.refs_12_ = f32[8,3,80,320]{3,2,1,0:T(8,128)} custom-call(s32[15]{0:T(128)} %stack.79.info.refs_0_, bf16[320,4352]{1,0:T(8,128)(2,1)} %get-tuple-element.58.own.refs_2_.refs_5_.refs_1_, bf16[320,4352]{1,0:T(8,128)(2,1)} %get-tuple-element.60.refs_2_, bf16[320,2176]{1,0:T(8,128)(2,1)} %collective-permute-done.1.refs_1_.refs_6_.refs_3_, ...), custom_call_target="tpu_custom_call" | custom-call | flops 1024 | bytes 1024 | tf_op jit(solution)/shard_map/pallas_call | solution.py:375
  101.2 2.6 %collective-permute-done.14 = f32[2,168,320]{2,1,0:T(8,128)} collective-permute-done((f32[2,168,320]{2,1,0:T(8,128)}, f32[2,168,320]{2,1,0:T(8,128)}, u32[]{:S(2)}, u32[]{:S(2)}) %collective-permute-start.14) | collective-permute-done | bytes 430112 | tf_op jit(solution)/shard_map/ppermute | solution.py:36
  107.1 9.3 %shard_map.60 = f32[8,3,80,320]{3,2,1,0:T(8,128)} custom-call(s32[15]{0:T(128)} %stack.79.info.refs_0_, bf16[320,4352]{1,0:T(8,128)(2,1)} %get-tuple-element.58.own.refs_2_.refs_5_.refs_1_, bf16[320,4352]{1,0:T(8,128)(2,1)} %get-tuple-element.60.refs_2_, ...), custom_call_target="tpu_custom_call", output_to_operand_aliasing={{}: (12, {})} | custom-call | flops 1024 | bytes 1024 | tf_op jit(solution)/shard_map/pallas_call | solution.py:375
  116.4 4.0 %all-to-all-start.1 = ((f32[8,3,80,320]{3,2,1,0:T(8,128)}), f32[8,3,80,320]{3,2,1,0:T(8,128)S(1)}, u32[]{:S(2)}, u32[]{:S(2)}) async-start(f32[8,3,80,320]{3,2,1,0:T(8,128)} %shard_map.60), calls=%async_computation.1 | async-start | bytes 5898240 | tf_op jit(solution)/shard_map/all_to_all | solution.py:561
  125.9 3.0 %collective-permute-done.18.third_back = f32[88,320]{1,0:T(8,128)S(1)} collective-permute-done((f32[88,320]{1,0:T(8,128)S(1)}, f32[88,320]{1,0:T(8,128)S(1)}, u32[]{:S(2)}, u32[]{:S(2)}) %collective-permute-start.18) | collective-permute-done | bytes 112672 | tf_op jit(solution)/shard_map/ppermute | solution.py:36
  129.5 27.1 %all-to-all-done.1 = f32[8,3,80,320]{3,2,1,0:T(8,128)S(1)} async-done(((f32[8,3,80,320]{3,2,1,0:T(8,128)}), f32[8,3,80,320]{3,2,1,0:T(8,128)S(1)}, u32[]{:S(2)}, u32[]{:S(2)}) %all-to-all-start.1) | async-done | bytes 2457632 | tf_op jit(solution)/shard_map/all_to_all | solution.py:561
  162.1 3.3 %collective-permute-start.21 = (f32[80,320]{1,0:T(8,128)}, f32[80,320]{1,0:T(8,128)S(1)}, u32[]{:S(2)}, u32[]{:S(2)}) collective-permute-start(f32[80,320]{1,0:T(8,128)} %slice_reduce_fusion), channel_id=1, source_target_pairs={{0,112},{1,113},{2,114},{3,115},{4,116},{5,117},{6,118},{7,119},{8... | collective-permute-start | bytes 307208 | tf_op jit(solution)/shard_map/ppermute | solution.py:36
  165.4 6.8 %collective-permute-done.21.from_diagonal = f32[80,320]{1,0:T(8,128)S(1)} collective-permute-done((f32[80,320]{1,0:T(8,128)}, f32[80,320]{1,0:T(8,128)S(1)}, u32[]{:S(2)}, u32[]{:S(2)}) %collective-permute-start.21) | collective-permute-done | bytes 102432 | tf_op jit(solution)/shard_map/ppermute | solution.py:36
  173.0 2.5 %shard_map.61 = f32[8,80,320]{2,1,0:T(8,128)} custom-call(s32[15]{0:T(128)} %stack.79.info.refs_0_, f32[248,320]{1,0:T(8,128)} %copy-done.4, f32[3,80,320]{2,1,0:T(8,128)} %reduce_sum.28.late, f32[3,80,320]{2,1,0:T(8,128)} %collective-permute-done.19.from_previous, f32[88,320]{1,0:T(8,128)} %copy-done.11, f32[88,320]{1,0:T(8,128)} %copy-done.10, ...), custom_call_target="tpu_custom_call" | custom-call | tf_op jit(solution)/shard_map/pallas_call | solution.py:415
  175.5 3.6 %all-to-all-start.2 = ((f32[8,80,320]{2,1,0:T(8,128)}), f32[8,80,320]{2,1,0:T(8,128)S(1)}, u32[]{:S(2)}, u32[]{:S(2)}) async-start(f32[8,80,320]{2,1,0:T(8,128)} %shard_map.61), calls=%async_computation.2 | async-start | bytes 1966080 | tf_op jit(solution)/shard_map/all_to_all | solution.py:579
  180.9 3.8 %collective-permute-start.22 = (f32[64,320]{1,0:T(8,128)S(1)}, f32[64,320]{1,0:T(8,128)S(1)}, u32[]{:S(2)}, u32[]{:S(2)}) collective-permute-start(f32[64,320]{1,0:T(8,128)S(1)} %pad_maximum_fusion.5), channel_id=1, source_target_pairs={{0,8},{1,9},{2,10},{3,11},{4,12},{5,13},{6,14},{7,15},{8,0},{9,1},... | collective-permute-start | bytes 245768 | tf_op jit(solution)/shard_map/ppermute | solution.py:36
  186.4 6.3 %all-to-all-done.2 = f32[8,80,320]{2,1,0:T(8,128)S(1)} async-done(((f32[8,80,320]{2,1,0:T(8,128)}), f32[8,80,320]{2,1,0:T(8,128)S(1)}, u32[]{:S(2)}, u32[]{:S(2)}) %all-to-all-start.2) | async-done | bytes 819232 | tf_op jit(solution)/shard_map/all_to_all | solution.py:579
  195.1 3.2 %add_sqrt_fusion.root = f32[320,640]{1,0:T(8,128)} fusion(f32[640]{0:T(1024)S(1)} %get-tuple-element.104, f32[640]{0:T(1024)S(1)} %get-tuple-element.105, f32[640]{0:T(1024)S(1)} %get-tuple-element.106, f32[640]{0:T(1024)S(1)} %get-tuple-element.107, f32[640]{0:T(1024)S(1)} %get-tuple-element.108, f32[640]{0:T(1024)S(1)} %get-tuple-element.109, ...), kind=kLoop, calls=%fused_computation.7 | loop fusion | flops 3686400 | bytes 857600 | tf_op jit(solution)/shard_map/sqrt | solution.py:598
  199.1 2.7 %shard_map.62 = f32[320,640]{1,0:T(8,128)} custom-call(s32[15]{0:T(128)} %stack.79.info.refs_0_, f32[640,320]{1,0:T(8,128)} %bitcast.33, f32[320,320]{1,0:T(8,128)} %copy-done.7, f32[320,640]{1,0:T(8,128)} %add_sqrt_fusion.root), custom_call_target="tpu_custom_call" | custom-call | tf_op jit(solution)/shard_map/pallas_call | solution.py:441
  (107 shorter events, 49.5 us)
Async XLA Ops:
  8.9 11.4 %collective-permute-start.3 = (bf16[320,4352]{1,0:T(8,128)(2,1)}, bf16[320,4352]{1,0:T(8,128)(2,1)}, u32[]{:S(2)}, u32[]{:S(2)}) collective-permute-start(bf16[320,4352]{1,0:T(8,128)(2,1)} %get-tuple-element.58.own.refs_2_.refs_5_.refs_1_), channel_id=1, source_target_pairs={{0,8},{1,9},{2,10},{3,11},{4,12},{5,13},{6,14},{7,15},{8,0},{9,1},... | collective-permute-start | bytes 8355848 | tf_op jit(solution)/shard_map/ppermute | solution.py:36
  10.4 37.7 %collective-permute-start = (bf16[320,2176]{1,0:T(8,128)(2,1)}, bf16[320,2176]{1,0:T(8,128)(2,1)}, u32[]{:S(2)}, u32[]{:S(2)}) collective-permute-start(bf16[320,2176]{1,0:T(8,128)(2,1)} %get-tuple-element.50), channel_id=1, source_target_pairs={{0,48},{1,49},{2,50},{3,51},{4,52},{5,53},{6,54},{7,55},{8,56},{9,... | collective-permute-start | bytes 4177928 | tf_op jit(solution)/shard_map/ppermute | solution.py:36
  14.2 33.9 %collective-permute-start.1 = (bf16[320,2176]{1,0:T(8,128)(2,1)}, bf16[320,2176]{1,0:T(8,128)(2,1)}, u32[]{:S(2)}, u32[]{:S(2)}) collective-permute-start(bf16[320,2176]{1,0:T(8,128)(2,1)} %get-tuple-element.51), channel_id=1, source_target_pairs={{0,64},{1,65},{2,66},{3,67},{4,68},{5,69},{6,70},{7,71},{8,72},{9,... | collective-permute-start | bytes 4177928 | tf_op jit(solution)/shard_map/ppermute | solution.py:36
  17.1 33.0 %collective-permute-start.2 = (bf16[320,2176]{1,0:T(8,128)(2,1)}, bf16[320,2176]{1,0:T(8,128)(2,1)}, u32[]{:S(2)}, u32[]{:S(2)}) collective-permute-start(bf16[320,2176]{1,0:T(8,128)(2,1)} %get-tuple-element.52), channel_id=1, source_target_pairs={{0,16},{1,17},{2,18},{3,19},{4,20},{5,21},{6,22},{7,23},{8,24},{9,... | collective-permute-start | bytes 4177928 | tf_op jit(solution)/shard_map/ppermute | solution.py:36
  28.1 18.7 %all-to-all-start = ((f32[4,2,80,320]{3,2,1,0:T(8,128)}), f32[4,2,80,320]{3,2,1,0:T(8,128)}, u32[]{:S(2)}, u32[]{:S(2)}) async-start(f32[4,2,80,320]{3,2,1,0:T(8,128)} %get-tuple-element.56), calls=%async_computation | async-start | bytes 1966080 | tf_op jit(solution)/shard_map/all_to_all | solution.py:41
  51.6 5.5 %collective-permute-start.8 = (bf16[320,2176]{1,0:T(8,128)(2,1)S(1)}, bf16[320,2176]{1,0:T(8,128)(2,1)}, u32[]{:S(2)}, u32[]{:S(2)}) collective-permute-start(bf16[320,2176]{1,0:T(8,128)(2,1)S(1)} %broadcast_select_fusion), channel_id=1, source_target_pairs={{0,8},{1,9},{2,10},{3,11},{4,12},{5,13},{6,14},{7,15},{8,0},{9,1},... | collective-permute-start | bytes 4177928 | tf_op jit(solution)/shard_map/ppermute | solution.py:36
  53.3 32.0 %collective-permute-start.4 = (bf16[320,2176]{1,0:T(8,128)(2,1)}, bf16[320,2176]{1,0:T(8,128)(2,1)S(1)}, u32[]{:S(2)}, u32[]{:S(2)}) collective-permute-start(bf16[320,2176]{1,0:T(8,128)(2,1)} %get-tuple-element.62), channel_id=1, source_target_pairs={{0,48},{1,49},{2,50},{3,51},{4,52},{5,53},{6,54},{7,55},{8,56},{9,... | collective-permute-start | bytes 4177928 | tf_op jit(solution)/shard_map/ppermute | solution.py:36
  53.5 33.2 %collective-permute-start.5 = (bf16[320,2176]{1,0:T(8,128)(2,1)}, bf16[320,2176]{1,0:T(8,128)(2,1)}, u32[]{:S(2)}, u32[]{:S(2)}) collective-permute-start(bf16[320,2176]{1,0:T(8,128)(2,1)} %get-tuple-element.63), channel_id=1, source_target_pairs={{0,64},{1,65},{2,66},{3,67},{4,68},{5,69},{6,70},{7,71},{8,72},{9,... | collective-permute-start | bytes 4177928 | tf_op jit(solution)/shard_map/ppermute | solution.py:36
  53.7 33.0 %collective-permute-start.6 = (bf16[320,2176]{1,0:T(8,128)(2,1)}, bf16[320,2176]{1,0:T(8,128)(2,1)S(1)}, u32[]{:S(2)}, u32[]{:S(2)}) collective-permute-start(bf16[320,2176]{1,0:T(8,128)(2,1)} %collective-permute-done.1.refs_1_.refs_6_.refs_3_), channel_id=1, source_target_pairs={{0,16},{1,17},{2,18},{3,19},{4,20},{5,21},{6,22},{7,23},{8,24},{9,... | collective-permute-start | bytes 4177928 | tf_op jit(solution)/shard_map/ppermute | solution.py:36
  66.4 20.3 %collective-permute-start.10 = (f32[2,168,320]{2,1,0:T(8,128)}, f32[2,168,320]{2,1,0:T(8,128)S(1)}, u32[]{:S(2)}, u32[]{:S(2)}) collective-permute-start(f32[2,168,320]{2,1,0:T(8,128)} %get-tuple-element.69), channel_id=1, source_target_pairs={{0,3},{1,0},{2,1},{3,2},{4,7},{5,4},{6,5},{7,6},{8,11},{9,8},{10,9... | collective-permute-start | bytes 1290248 | tf_op jit(solution)/shard_map/ppermute | solution.py:36
  69.0 17.8 %collective-permute-start.9 = (f32[2,168,320]{2,1,0:T(8,128)}, f32[2,168,320]{2,1,0:T(8,128)S(1)}, u32[]{:S(2)}, u32[]{:S(2)}) collective-permute-start(f32[2,168,320]{2,1,0:T(8,128)} %get-tuple-element.68), channel_id=1, source_target_pairs={{0,1},{1,2},{2,3},{3,0},{4,5},{5,6},{6,7},{7,4},{8,9},{9,10},{10,1... | collective-permute-start | bytes 1290248 | tf_op jit(solution)/shard_map/ppermute | solution.py:36
  85.3 15.9 %collective-permute-start.11 = (bf16[320,2176]{1,0:T(8,128)(2,1)}, bf16[320,2176]{1,0:T(8,128)(2,1)}, u32[]{:S(2)}, u32[]{:S(2)}) collective-permute-start(bf16[320,2176]{1,0:T(8,128)(2,1)} %collective-permute-done.refs_7_.refs_12_.refs_5_), channel_id=1, source_target_pairs={{0,8},{1,9},{2,10},{3,11},{4,12},{5,13},{6,14},{7,15},{8,0},{9,1},... | collective-permute-start | bytes 4177928 | tf_op jit(solution)/shard_map/ppermute | solution.py:36
  87.6 16.2 %collective-permute-start.12 = (bf16[320,2176]{1,0:T(8,128)(2,1)S(1)}, bf16[320,2176]{1,0:T(8,128)(2,1)}, u32[]{:S(2)}, u32[]{:S(2)}) collective-permute-start(bf16[320,2176]{1,0:T(8,128)(2,1)S(1)} %collective-permute-done.4.refs_6_.refs_8_), channel_id=1, source_target_pairs={{0,8},{1,9},{2,10},{3,11},{4,12},{5,13},{6,14},{7,15},{8,0},{9,1},... | collective-permute-start | bytes 4177928 | tf_op jit(solution)/shard_map/ppermute | solution.py:36
  89.2 14.6 %collective-permute-start.13 = (bf16[320,2176]{1,0:T(8,128)(2,1)S(1)}, bf16[320,2176]{1,0:T(8,128)(2,1)}, u32[]{:S(2)}, u32[]{:S(2)}) collective-permute-start(bf16[320,2176]{1,0:T(8,128)(2,1)S(1)} %collective-permute-done.6.refs_9_.refs_10_), channel_id=1, source_target_pairs={{0,8},{1,9},{2,10},{3,11},{4,12},{5,13},{6,14},{7,15},{8,0},{9,1},... | collective-permute-start | bytes 4177928 | tf_op jit(solution)/shard_map/ppermute | solution.py:36
  89.2 14.6 %collective-permute-start.14 = (f32[2,168,320]{2,1,0:T(8,128)}, f32[2,168,320]{2,1,0:T(8,128)}, u32[]{:S(2)}, u32[]{:S(2)}) collective-permute-start(f32[2,168,320]{2,1,0:T(8,128)} %get-tuple-element.75), channel_id=1, source_target_pairs={{0,2},{1,3},{2,0},{3,1},{4,6},{5,7},{6,4},{7,5},{8,10},{9,11},{10,... | collective-permute-start | bytes 1290248 | tf_op jit(solution)/shard_map/ppermute | solution.py:36
  106.0 10.4 %collective-permute-start.15 = (f32[248,320]{1,0:T(8,128)S(1)}, f32[248,320]{1,0:T(8,128)}, u32[]{:S(2)}, u32[]{:S(2)}) collective-permute-start(f32[248,320]{1,0:T(8,128)S(1)} %pad_maximum_fusion), channel_id=1, source_target_pairs={{0,4},{1,5},{2,6},{3,7},{4,0},{5,1},{6,2},{7,3},{8,12},{9,13},{10,... | collective-permute-start | bytes 952328 | tf_op jit(solution)/shard_map/ppermute | solution.py:36
  116.4 40.2 %all-to-all-start.1 = ((f32[8,3,80,320]{3,2,1,0:T(8,128)}), f32[8,3,80,320]{3,2,1,0:T(8,128)S(1)}, u32[]{:S(2)}, u32[]{:S(2)}) async-start(f32[8,3,80,320]{3,2,1,0:T(8,128)} %shard_map.60), calls=%async_computation.1 | async-start | bytes 5898240 | tf_op jit(solution)/shard_map/all_to_all | solution.py:561
  123.3 5.5 %collective-permute-start.18 = (f32[88,320]{1,0:T(8,128)S(1)}, f32[88,320]{1,0:T(8,128)S(1)}, u32[]{:S(2)}, u32[]{:S(2)}) collective-permute-start(f32[88,320]{1,0:T(8,128)S(1)} %pad_maximum_fusion.4), channel_id=1, source_target_pairs={{0,16},{1,17},{2,18},{3,19},{4,20},{5,21},{6,22},{7,23},{8,24},{9,... | collective-permute-start | bytes 337928 | tf_op jit(solution)/shard_map/ppermute | solution.py:36
  123.3 5.5 %collective-permute-start.17 = (f32[8,320]{1,0:T(8,128)S(1)}, f32[8,320]{1,0:T(8,128)S(1)}, u32[]{:S(2)}, u32[]{:S(2)}) collective-permute-start(f32[8,320]{1,0:T(8,128)S(1)} %slice.129), channel_id=1, source_target_pairs={{0,32},{1,33},{2,34},{3,35},{4,36},{5,37},{6,38},{7,39},{8,40},{9,... | collective-permute-start | bytes 30728 | tf_op jit(solution)/shard_map/ppermute | solution.py:36
  158.5 13.7 %collective-permute-start.19 = (f32[3,80,320]{2,1,0:T(8,128)}, f32[3,80,320]{2,1,0:T(8,128)}, u32[]{:S(2)}, u32[]{:S(2)}) collective-permute-start(f32[3,80,320]{2,1,0:T(8,128)} %reduce_sum.28.late), channel_id=1, source_target_pairs={{0,16},{1,17},{2,18},{3,19},{4,20},{5,21},{6,22},{7,23},{8,24},{9,... | collective-permute-start | bytes 921608 | tf_op jit(solution)/shard_map/ppermute | solution.py:36
  160.8 11.5 %collective-permute-start.20 = (f32[192,320]{1,0:T(8,128)}, f32[192,320]{1,0:T(8,128)S(1)}, u32[]{:S(2)}, u32[]{:S(2)}) collective-permute-start(f32[192,320]{1,0:T(8,128)} %pad_maximum_fusion.2), channel_id=1, source_target_pairs={{0,64},{1,65},{2,66},{3,67},{4,68},{5,69},{6,70},{7,71},{8,72},{9,... | collective-permute-start | bytes 737288 | tf_op jit(solution)/shard_map/ppermute | solution.py:36
  162.1 10.2 %collective-permute-start.21 = (f32[80,320]{1,0:T(8,128)}, f32[80,320]{1,0:T(8,128)S(1)}, u32[]{:S(2)}, u32[]{:S(2)}) collective-permute-start(f32[80,320]{1,0:T(8,128)} %slice_reduce_fusion), channel_id=1, source_target_pairs={{0,112},{1,113},{2,114},{3,115},{4,116},{5,117},{6,118},{7,119},{8... | collective-permute-start | bytes 307208 | tf_op jit(solution)/shard_map/ppermute | solution.py:36
  175.5 17.1 %all-to-all-start.2 = ((f32[8,80,320]{2,1,0:T(8,128)}), f32[8,80,320]{2,1,0:T(8,128)S(1)}, u32[]{:S(2)}, u32[]{:S(2)}) async-start(f32[8,80,320]{2,1,0:T(8,128)} %shard_map.61), calls=%async_computation.2 | async-start | bytes 1966080 | tf_op jit(solution)/shard_map/all_to_all | solution.py:579
  192.6 5.6 %collective-permute-start.23 = (f32[320,320]{1,0:T(8,128)S(1)}, f32[320,320]{1,0:T(8,128)S(1)}, u32[]{:S(2)}, u32[]{:S(2)}) collective-permute-start(f32[320,320]{1,0:T(8,128)S(1)} %constant_dynamic-slice_fusion), channel_id=1, source_target_pairs={{0,8},{1,9},{2,10},{3,11},{4,12},{5,13},{6,14},{7,15},{8,0},{9,1},... | collective-permute-start | bytes 1228808 | tf_op jit(solution)/shard_map/ppermute | solution.py:36
  (18 other events, 119.5 us)

commit v6 on v5

--- a/solution.py
+++ b/solution.py
@@ -6,7 +6,7 @@
 from jax.sharding import PartitionSpec as P
 
 BOTH = ("blk", "freq")
-VMEM_BYTES = 60 * 1024 * 1024
+VMEM_BYTES = 54 * 1024 * 1024
 LANES = 128
 PARAMS = pltpu.CompilerParams(vmem_limit_bytes=VMEM_BYTES)
 COST = pl.CostEstimate(flops=1024, bytes_accessed=1024, transcendentals=0)

time: 204 us -> 203 us (level)
  no operation moved by 1% of the time
where the time goes in v6:
time: 203 us; the launch traced here: 202 us
  waiting for transfers between devices  76.5 us (38%)
  starting transfers between devices  48.8 us (24%)
  Pallas kernels  47.6 us (23%)
  other arithmetic  14 us (7%)
  local copies, waits for them, and re-layouts  11.3 us (6%)
  matrix products  3.51 us (2%)
    ppermute x24, starting transfers between devices, send(): return lax.ppermute(block, BOTH, route(dyh, dz, dc, dyl, dx))  36.4 us
    ppermute x24, waiting for transfers between devices, send(): return lax.ppermute(block, BOTH, route(dyh, dz, dc, dyl, dx))  34.3 us
    all_to_all x1, waiting for transfers between devices, per_device(): late = lax.all_to_all(late, 'freq', 0, 0, tiled=True)  27.7 us
    pallas_call x2, Pallas kernels, late_tiles(): pl.pallas_call(kernel, in_specs=specs, out_specs=ANY, out_shape=jax.Shape...  18 us
    all_to_all x1, waiting for transfers between devices, summed_along_x(): lax.all_to_all(tiles, 'freq', 0, 0, axis_index_groups=groups, tiled=True)  9.05 us
    pallas_call x1, Pallas kernels, half_tiles(): pl.pallas_call(kernel, in_specs=[SMEM] + [ANY] * (len(operands) - 2) + [V...  8.16 us
    pallas_call x1, Pallas kernels, first_tiles(): pl.pallas_call(first_kernel, in_specs=[SMEM, ANY, ANY, VMEM], out_specs=[...  7.74 us
    pallas_call x1, Pallas kernels, masked_blocks(): pl.pallas_call(mask_kernel, grid_spec=pltpu.PrefetchScalarGridSpec(num_sc...  6.64 us
  transfers between devices with their start and end apart: 27, of which 12 were waited for; matrix products, arithmetic and copies ran while one was open for 9% of the time, Pallas kernels for 18%

profile of v6, /device:TPU:1, one launch (start us, length us, event | category | flops | bytes accessed | tf_op | source)
XLA Modules:
  0.0 202.0 jit_solution(10594682620129100212)
XLA Ops:
  2.1 6.6 %shard_map.55 = (bf16[320,4352]{1,0:T(8,128)(2,1)}, bf16[320,2176]{1,0:T(8,128)(2,1)}, bf16[320,2176]{1,0:T(8,128)(2,1)}, bf16[320,2176]{1,0:T(8,128)(2,1)}, bf16[8,4352]{1,0:T(8,128)(2,1)}) custom-call(s32[15]{0:T(128)} %stack.79.info.refs_0_, bf16[320,8]{1,0:T(8,128)(2,1)} %fusion.6.hot, bf16[320,4352]{1,0:T(8,128)(2,1)} %spectra.1, s32[8,2176]{1,0:T(8,128)} %wedges.1), custom_call_target="tpu_custom_call" | custom-call | flops 1024 | bytes 1024 | tf_op jit(solution)/shard_map/pallas_call | solution.py:93
  10.2 3.8 %collective-permute-start = (bf16[320,2176]{1,0:T(8,128)(2,1)}, bf16[320,2176]{1,0:T(8,128)(2,1)}, u32[]{:S(2)}, u32[]{:S(2)}) collective-permute-start(bf16[320,2176]{1,0:T(8,128)(2,1)} %get-tuple-element.50), channel_id=1, source_target_pairs={{0,48},{1,49},{2,50},{3,51},{4,52},{5,53},{6,54},{7,55},{8,56},{9,... | collective-permute-start | bytes 4177928 | tf_op jit(solution)/shard_map/ppermute | solution.py:36
  14.0 2.9 %collective-permute-start.1 = (bf16[320,2176]{1,0:T(8,128)(2,1)}, bf16[320,2176]{1,0:T(8,128)(2,1)}, u32[]{:S(2)}, u32[]{:S(2)}) collective-permute-start(bf16[320,2176]{1,0:T(8,128)(2,1)} %get-tuple-element.51), channel_id=1, source_target_pairs={{0,64},{1,65},{2,66},{3,67},{4,68},{5,69},{6,70},{7,71},{8,72},{9,... | collective-permute-start | bytes 4177928 | tf_op jit(solution)/shard_map/ppermute | solution.py:36
  20.2 7.7 %shard_map.57 = (f32[4,2,80,320]{3,2,1,0:T(8,128)}, bf16[320,4352]{1,0:T(8,128)(2,1)}) custom-call(s32[15]{0:T(128)} %stack.79.info.refs_0_, bf16[320,4352]{1,0:T(8,128)(2,1)} %get-tuple-element.58.own.refs_2_.refs_5_.refs_1_, bf16[320,4352]{1,0:T(8,128)(2,1)} %collective-permute-done.3.sibling.refs_4_, f32[1,4352]{1,0:T(1,128)} %shard_map.56.weight.refs_13_.refs_11_), custom_call_target="tpu_custom_call" | custom-call | flops 1024 | bytes 1024 | tf_op jit(solution)/shard_map/pallas_call | solution.py:177
  28.0 4.4 %all-to-all-start = ((f32[4,2,80,320]{3,2,1,0:T(8,128)}), f32[4,2,80,320]{3,2,1,0:T(8,128)}, u32[]{:S(2)}, u32[]{:S(2)}) async-start(f32[4,2,80,320]{3,2,1,0:T(8,128)} %get-tuple-element.56), calls=%async_computation | async-start | bytes 1966080 | tf_op jit(solution)/shard_map/all_to_all | solution.py:41
  32.4 3.5 %fusion.refs_14_ = f32[8,320]{1,0:T(8,128)} fusion(bf16[8,4352]{1,0:T(8,128)(2,1)S(1)} %copy-done.18, bf16[320,4352]{1,0:T(8,128)(2,1)S(1)} %copy-done, f32[4352]{0:T(1024)S(1)} %reduce.1), kind=kOutput, calls=%fused_computation | convolution fusion | flops 137871360 | bytes 2882560 | tf_op jit(solution)/shard_map/dot_general | solution.py:512
  37.6 9.1 %all-to-all-done = f32[4,2,80,320]{3,2,1,0:T(8,128)} async-done(((f32[4,2,80,320]{3,2,1,0:T(8,128)}), f32[4,2,80,320]{3,2,1,0:T(8,128)}, u32[]{:S(2)}, u32[]{:S(2)}) %all-to-all-start) | async-done | bytes 819232 | tf_op jit(solution)/shard_map/all_to_all | solution.py:41
  58.3 8.2 %shard_map.58 = (f32[2,168,320]{2,1,0:T(8,128)}, f32[2,168,320]{2,1,0:T(8,128)}, f32[2,168,320]{2,1,0:T(8,128)}, f32[2,168,320]{2,1,0:T(8,128)}) custom-call(s32[15]{0:T(128)} %stack.79.info.refs_0_, bf16[320,2176]{1,0:T(8,128)(2,1)} %collective-permute-done.1.refs_1_.refs_6_.refs_3_, bf16[320,4352]{1,0:T(8,128)(2,1)} %get-tuple-element.58.own.refs_2_.refs_5_.refs_1_, ...), custom_call_target="tpu_custom_call" | custom-call | flops 1024 | bytes 1024 | tf_op jit(solution)/shard_map/pallas_call | solution.py:257
  66.4 2.5 %collective-permute-start.10 = (f32[2,168,320]{2,1,0:T(8,128)}, f32[2,168,320]{2,1,0:T(8,128)S(1)}, u32[]{:S(2)}, u32[]{:S(2)}) collective-permute-start(f32[2,168,320]{2,1,0:T(8,128)} %get-tuple-element.69), channel_id=1, source_target_pairs={{0,3},{1,0},{2,1},{3,2},{4,7},{5,4},{6,5},{7,6},{8,11},{9,8},{10,9... | collective-permute-start | bytes 1290248 | tf_op jit(solution)/shard_map/ppermute | solution.py:36
  69.0 16.0 %collective-permute-done.4.refs_6_.refs_8_ = bf16[320,2176]{1,0:T(8,128)(2,1)S(1)} collective-permute-done((bf16[320,2176]{1,0:T(8,128)(2,1)S(1)}, bf16[320,2176]{1,0:T(8,128)(2,1)S(1)}, u32[]{:S(2)}, u32[]{:S(2)}) %collective-permute-start.4) | collective-permute-done | bytes 1392672 | tf_op jit(solution)/shard_map/ppermute | solution.py:36
  89.3 2.5 %collective-permute-start.14 = (f32[2,168,320]{2,1,0:T(8,128)}, f32[2,168,320]{2,1,0:T(8,128)}, u32[]{:S(2)}, u32[]{:S(2)}) collective-permute-start(f32[2,168,320]{2,1,0:T(8,128)} %get-tuple-element.75), channel_id=1, source_target_pairs={{0,2},{1,3},{2,0},{3,1},{4,6},{5,7},{6,4},{7,5},{8,10},{9,11},{10,... | collective-permute-start | bytes 1290248 | tf_op jit(solution)/shard_map/ppermute | solution.py:36
  92.5 8.8 %shard_map.59.refs_12_ = f32[8,3,80,320]{3,2,1,0:T(8,128)} custom-call(s32[15]{0:T(128)} %stack.79.info.refs_0_, bf16[320,4352]{1,0:T(8,128)(2,1)} %get-tuple-element.58.own.refs_2_.refs_5_.refs_1_, bf16[320,4352]{1,0:T(8,128)(2,1)} %get-tuple-element.60.refs_2_, bf16[320,2176]{1,0:T(8,128)(2,1)} %collective-permute-done.1.refs_1_.refs_6_.refs_3_, ...), custom_call_target="tpu_custom_call" | custom-call | flops 1024 | bytes 1024 | tf_op jit(solution)/shard_map/pallas_call | solution.py:375
  101.3 2.8 %collective-permute-done.14 = f32[2,168,320]{2,1,0:T(8,128)} collective-permute-done((f32[2,168,320]{2,1,0:T(8,128)}, f32[2,168,320]{2,1,0:T(8,128)}, u32[]{:S(2)}, u32[]{:S(2)}) %collective-permute-start.14) | collective-permute-done | bytes 430112 | tf_op jit(solution)/shard_map/ppermute | solution.py:36
  107.4 9.2 %shard_map.60 = f32[8,3,80,320]{3,2,1,0:T(8,128)} custom-call(s32[15]{0:T(128)} %stack.79.info.refs_0_, bf16[320,4352]{1,0:T(8,128)(2,1)} %get-tuple-element.58.own.refs_2_.refs_5_.refs_1_, bf16[320,4352]{1,0:T(8,128)(2,1)} %get-tuple-element.60.refs_2_, ...), custom_call_target="tpu_custom_call", output_to_operand_aliasing={{}: (12, {})} | custom-call | flops 1024 | bytes 1024 | tf_op jit(solution)/shard_map/pallas_call | solution.py:375
  116.6 3.9 %all-to-all-start.1 = ((f32[8,3,80,320]{3,2,1,0:T(8,128)}), f32[8,3,80,320]{3,2,1,0:T(8,128)S(1)}, u32[]{:S(2)}, u32[]{:S(2)}) async-start(f32[8,3,80,320]{3,2,1,0:T(8,128)} %shard_map.60), calls=%async_computation.1 | async-start | bytes 5898240 | tf_op jit(solution)/shard_map/all_to_all | solution.py:561
  129.0 27.7 %all-to-all-done.1 = f32[8,3,80,320]{3,2,1,0:T(8,128)S(1)} async-done(((f32[8,3,80,320]{3,2,1,0:T(8,128)}), f32[8,3,80,320]{3,2,1,0:T(8,128)S(1)}, u32[]{:S(2)}, u32[]{:S(2)}) %all-to-all-start.1) | async-done | bytes 2457632 | tf_op jit(solution)/shard_map/all_to_all | solution.py:561
  162.7 2.7 %collective-permute-start.21 = (f32[80,320]{1,0:T(8,128)}, f32[80,320]{1,0:T(8,128)S(1)}, u32[]{:S(2)}, u32[]{:S(2)}) collective-permute-start(f32[80,320]{1,0:T(8,128)} %slice_reduce_fusion), channel_id=1, source_target_pairs={{0,112},{1,113},{2,114},{3,115},{4,116},{5,117},{6,118},{7,119},{8... | collective-permute-start | bytes 307208 | tf_op jit(solution)/shard_map/ppermute | solution.py:36
  165.5 6.4 %collective-permute-done.21.from_diagonal = f32[80,320]{1,0:T(8,128)S(1)} collective-permute-done((f32[80,320]{1,0:T(8,128)}, f32[80,320]{1,0:T(8,128)S(1)}, u32[]{:S(2)}, u32[]{:S(2)}) %collective-permute-start.21) | collective-permute-done | bytes 102432 | tf_op jit(solution)/shard_map/ppermute | solution.py:36
  175.1 4.0 %all-to-all-start.2 = ((f32[8,80,320]{2,1,0:T(8,128)}), f32[8,80,320]{2,1,0:T(8,128)S(1)}, u32[]{:S(2)}, u32[]{:S(2)}) async-start(f32[8,80,320]{2,1,0:T(8,128)} %shard_map.61), calls=%async_computation.2 | async-start | bytes 1966080 | tf_op jit(solution)/shard_map/all_to_all | solution.py:579
  181.0 4.3 %collective-permute-start.22 = (f32[64,320]{1,0:T(8,128)S(1)}, f32[64,320]{1,0:T(8,128)S(1)}, u32[]{:S(2)}, u32[]{:S(2)}) collective-permute-start(f32[64,320]{1,0:T(8,128)S(1)} %pad_maximum_fusion.5), channel_id=1, source_target_pairs={{0,8},{1,9},{2,10},{3,11},{4,12},{5,13},{6,14},{7,15},{8,0},{9,1},... | collective-permute-start | bytes 245768 | tf_op jit(solution)/shard_map/ppermute | solution.py:36
  187.1 5.4 %all-to-all-done.2 = f32[8,80,320]{2,1,0:T(8,128)S(1)} async-done(((f32[8,80,320]{2,1,0:T(8,128)}), f32[8,80,320]{2,1,0:T(8,128)S(1)}, u32[]{:S(2)}, u32[]{:S(2)}) %all-to-all-start.2) | async-done | bytes 819232 | tf_op jit(solution)/shard_map/all_to_all | solution.py:579
  192.5 2.7 %collective-permute-start.23 = (f32[320,320]{1,0:T(8,128)S(1)}, f32[320,320]{1,0:T(8,128)S(1)}, u32[]{:S(2)}, u32[]{:S(2)}) collective-permute-start(f32[320,320]{1,0:T(8,128)S(1)} %constant_dynamic-slice_fusion), channel_id=1, source_target_pairs={{0,8},{1,9},{2,10},{3,11},{4,12},{5,13},{6,14},{7,15},{8,0},{9,1},... | collective-permute-start | bytes 1228808 | tf_op jit(solution)/shard_map/ppermute | solution.py:36
  195.3 3.2 %add_sqrt_fusion.root = f32[320,640]{1,0:T(8,128)} fusion(f32[640]{0:T(1024)S(1)} %get-tuple-element.104, f32[640]{0:T(1024)S(1)} %get-tuple-element.105, f32[640]{0:T(1024)S(1)} %get-tuple-element.106, f32[640]{0:T(1024)S(1)} %get-tuple-element.107, f32[640]{0:T(1024)S(1)} %get-tuple-element.108, f32[640]{0:T(1024)S(1)} %get-tuple-element.109, ...), kind=kLoop, calls=%fused_computation.7 | loop fusion | flops 3686400 | bytes 857600 | tf_op jit(solution)/shard_map/sqrt | solution.py:598
  199.3 2.7 %shard_map.62 = f32[320,640]{1,0:T(8,128)} custom-call(s32[15]{0:T(128)} %stack.79.info.refs_0_, f32[640,320]{1,0:T(8,128)} %bitcast.33, f32[320,320]{1,0:T(8,128)} %copy-done.12, f32[320,640]{1,0:T(8,128)} %add_sqrt_fusion.root), custom_call_target="tpu_custom_call" | custom-call | tf_op jit(solution)/shard_map/pallas_call | solution.py:441
  (115 shorter events, 50.5 us)
Async XLA Ops:
  8.7 11.4 %collective-permute-start.3 = (bf16[320,4352]{1,0:T(8,128)(2,1)}, bf16[320,4352]{1,0:T(8,128)(2,1)}, u32[]{:S(2)}, u32[]{:S(2)}) collective-permute-start(bf16[320,4352]{1,0:T(8,128)(2,1)} %get-tuple-element.58.own.refs_2_.refs_5_.refs_1_), channel_id=1, source_target_pairs={{0,8},{1,9},{2,10},{3,11},{4,12},{5,13},{6,14},{7,15},{8,0},{9,1},... | collective-permute-start | bytes 8355848 | tf_op jit(solution)/shard_map/ppermute | solution.py:36
  10.2 37.8 %collective-permute-start = (bf16[320,2176]{1,0:T(8,128)(2,1)}, bf16[320,2176]{1,0:T(8,128)(2,1)}, u32[]{:S(2)}, u32[]{:S(2)}) collective-permute-start(bf16[320,2176]{1,0:T(8,128)(2,1)} %get-tuple-element.50), channel_id=1, source_target_pairs={{0,48},{1,49},{2,50},{3,51},{4,52},{5,53},{6,54},{7,55},{8,56},{9,... | collective-permute-start | bytes 4177928 | tf_op jit(solution)/shard_map/ppermute | solution.py:36
  14.0 34.0 %collective-permute-start.1 = (bf16[320,2176]{1,0:T(8,128)(2,1)}, bf16[320,2176]{1,0:T(8,128)(2,1)}, u32[]{:S(2)}, u32[]{:S(2)}) collective-permute-start(bf16[320,2176]{1,0:T(8,128)(2,1)} %get-tuple-element.51), channel_id=1, source_target_pairs={{0,64},{1,65},{2,66},{3,67},{4,68},{5,69},{6,70},{7,71},{8,72},{9,... | collective-permute-start | bytes 4177928 | tf_op jit(solution)/shard_map/ppermute | solution.py:36
  16.9 33.0 %collective-permute-start.2 = (bf16[320,2176]{1,0:T(8,128)(2,1)}, bf16[320,2176]{1,0:T(8,128)(2,1)}, u32[]{:S(2)}, u32[]{:S(2)}) collective-permute-start(bf16[320,2176]{1,0:T(8,128)(2,1)} %get-tuple-element.52), channel_id=1, source_target_pairs={{0,16},{1,17},{2,18},{3,19},{4,20},{5,21},{6,22},{7,23},{8,24},{9,... | collective-permute-start | bytes 4177928 | tf_op jit(solution)/shard_map/ppermute | solution.py:36
  28.0 18.7 %all-to-all-start = ((f32[4,2,80,320]{3,2,1,0:T(8,128)}), f32[4,2,80,320]{3,2,1,0:T(8,128)}, u32[]{:S(2)}, u32[]{:S(2)}) async-start(f32[4,2,80,320]{3,2,1,0:T(8,128)} %get-tuple-element.56), calls=%async_computation | async-start | bytes 1966080 | tf_op jit(solution)/shard_map/all_to_all | solution.py:41
  51.6 5.4 %collective-permute-start.8 = (bf16[320,2176]{1,0:T(8,128)(2,1)S(1)}, bf16[320,2176]{1,0:T(8,128)(2,1)S(1)}, u32[]{:S(2)}, u32[]{:S(2)}) collective-permute-start(bf16[320,2176]{1,0:T(8,128)(2,1)S(1)} %broadcast_select_fusion), channel_id=1, source_target_pairs={{0,8},{1,9},{2,10},{3,11},{4,12},{5,13},{6,14},{7,15},{8,0},{9,1},... | collective-permute-start | bytes 4177928 | tf_op jit(solution)/shard_map/ppermute | solution.py:36
  53.2 31.7 %collective-permute-start.4 = (bf16[320,2176]{1,0:T(8,128)(2,1)S(1)}, bf16[320,2176]{1,0:T(8,128)(2,1)S(1)}, u32[]{:S(2)}, u32[]{:S(2)}) collective-permute-start(bf16[320,2176]{1,0:T(8,128)(2,1)S(1)} %copy-done.8), channel_id=1, source_target_pairs={{0,48},{1,49},{2,50},{3,51},{4,52},{5,53},{6,54},{7,55},{8,56},{9,... | collective-permute-start | bytes 4177928 | tf_op jit(solution)/shard_map/ppermute | solution.py:36
  53.6 32.9 %collective-permute-start.5 = (bf16[320,2176]{1,0:T(8,128)(2,1)S(1)}, bf16[320,2176]{1,0:T(8,128)(2,1)S(1)}, u32[]{:S(2)}, u32[]{:S(2)}) collective-permute-start(bf16[320,2176]{1,0:T(8,128)(2,1)S(1)} %copy-done.7), channel_id=1, source_target_pairs={{0,64},{1,65},{2,66},{3,67},{4,68},{5,69},{6,70},{7,71},{8,72},{9,... | collective-permute-start | bytes 4177928 | tf_op jit(solution)/shard_map/ppermute | solution.py:36
  53.7 32.8 %collective-permute-start.6 = (bf16[320,2176]{1,0:T(8,128)(2,1)}, bf16[320,2176]{1,0:T(8,128)(2,1)S(1)}, u32[]{:S(2)}, u32[]{:S(2)}) collective-permute-start(bf16[320,2176]{1,0:T(8,128)(2,1)} %collective-permute-done.1.refs_1_.refs_6_.refs_3_), channel_id=1, source_target_pairs={{0,16},{1,17},{2,18},{3,19},{4,20},{5,21},{6,22},{7,23},{8,24},{9,... | collective-permute-start | bytes 4177928 | tf_op jit(solution)/shard_map/ppermute | solution.py:36
  66.4 20.1 %collective-permute-start.10 = (f32[2,168,320]{2,1,0:T(8,128)}, f32[2,168,320]{2,1,0:T(8,128)S(1)}, u32[]{:S(2)}, u32[]{:S(2)}) collective-permute-start(f32[2,168,320]{2,1,0:T(8,128)} %get-tuple-element.69), channel_id=1, source_target_pairs={{0,3},{1,0},{2,1},{3,2},{4,7},{5,4},{6,5},{7,6},{8,11},{9,8},{10,9... | collective-permute-start | bytes 1290248 | tf_op jit(solution)/shard_map/ppermute | solution.py:36
  69.0 17.5 %collective-permute-start.9 = (f32[2,168,320]{2,1,0:T(8,128)}, f32[2,168,320]{2,1,0:T(8,128)S(1)}, u32[]{:S(2)}, u32[]{:S(2)}) collective-permute-start(f32[2,168,320]{2,1,0:T(8,128)} %get-tuple-element.68), channel_id=1, source_target_pairs={{0,1},{1,2},{2,3},{3,0},{4,5},{5,6},{6,7},{7,4},{8,9},{9,10},{10,1... | collective-permute-start | bytes 1290248 | tf_op jit(solution)/shard_map/ppermute | solution.py:36
  84.9 16.4 %collective-permute-start.11 = (bf16[320,2176]{1,0:T(8,128)(2,1)}, bf16[320,2176]{1,0:T(8,128)(2,1)}, u32[]{:S(2)}, u32[]{:S(2)}) collective-permute-start(bf16[320,2176]{1,0:T(8,128)(2,1)} %collective-permute-done.refs_7_.refs_12_.refs_5_), channel_id=1, source_target_pairs={{0,8},{1,9},{2,10},{3,11},{4,12},{5,13},{6,14},{7,15},{8,0},{9,1},... | collective-permute-start | bytes 4177928 | tf_op jit(solution)/shard_map/ppermute | solution.py:36
  87.6 16.5 %collective-permute-start.12 = (bf16[320,2176]{1,0:T(8,128)(2,1)S(1)}, bf16[320,2176]{1,0:T(8,128)(2,1)}, u32[]{:S(2)}, u32[]{:S(2)}) collective-permute-start(bf16[320,2176]{1,0:T(8,128)(2,1)S(1)} %collective-permute-done.4.refs_6_.refs_8_), channel_id=1, source_target_pairs={{0,8},{1,9},{2,10},{3,11},{4,12},{5,13},{6,14},{7,15},{8,0},{9,1},... | collective-permute-start | bytes 4177928 | tf_op jit(solution)/shard_map/ppermute | solution.py:36
  89.2 14.9 %collective-permute-start.13 = (bf16[320,2176]{1,0:T(8,128)(2,1)S(1)}, bf16[320,2176]{1,0:T(8,128)(2,1)}, u32[]{:S(2)}, u32[]{:S(2)}) collective-permute-start(bf16[320,2176]{1,0:T(8,128)(2,1)S(1)} %collective-permute-done.6.refs_9_.refs_10_), channel_id=1, source_target_pairs={{0,8},{1,9},{2,10},{3,11},{4,12},{5,13},{6,14},{7,15},{8,0},{9,1},... | collective-permute-start | bytes 4177928 | tf_op jit(solution)/shard_map/ppermute | solution.py:36
  89.3 14.8 %collective-permute-start.14 = (f32[2,168,320]{2,1,0:T(8,128)}, f32[2,168,320]{2,1,0:T(8,128)}, u32[]{:S(2)}, u32[]{:S(2)}) collective-permute-start(f32[2,168,320]{2,1,0:T(8,128)} %get-tuple-element.75), channel_id=1, source_target_pairs={{0,2},{1,3},{2,0},{3,1},{4,6},{5,7},{6,4},{7,5},{8,10},{9,11},{10,... | collective-permute-start | bytes 1290248 | tf_op jit(solution)/shard_map/ppermute | solution.py:36
  106.1 10.6 %collective-permute-start.15 = (f32[248,320]{1,0:T(8,128)S(1)}, f32[248,320]{1,0:T(8,128)}, u32[]{:S(2)}, u32[]{:S(2)}) collective-permute-start(f32[248,320]{1,0:T(8,128)S(1)} %pad_maximum_fusion), channel_id=1, source_target_pairs={{0,4},{1,5},{2,6},{3,7},{4,0},{5,1},{6,2},{7,3},{8,12},{9,13},{10,... | collective-permute-start | bytes 952328 | tf_op jit(solution)/shard_map/ppermute | solution.py:36
  116.6 40.1 %all-to-all-start.1 = ((f32[8,3,80,320]{3,2,1,0:T(8,128)}), f32[8,3,80,320]{3,2,1,0:T(8,128)S(1)}, u32[]{:S(2)}, u32[]{:S(2)}) async-start(f32[8,3,80,320]{3,2,1,0:T(8,128)} %shard_map.60), calls=%async_computation.1 | async-start | bytes 5898240 | tf_op jit(solution)/shard_map/all_to_all | solution.py:561
  122.8 5.5 %collective-permute-start.18 = (f32[88,320]{1,0:T(8,128)S(1)}, f32[88,320]{1,0:T(8,128)S(1)}, u32[]{:S(2)}, u32[]{:S(2)}) collective-permute-start(f32[88,320]{1,0:T(8,128)S(1)} %pad_maximum_fusion.4), channel_id=1, source_target_pairs={{0,16},{1,17},{2,18},{3,19},{4,20},{5,21},{6,22},{7,23},{8,24},{9,... | collective-permute-start | bytes 337928 | tf_op jit(solution)/shard_map/ppermute | solution.py:36
  158.6 13.3 %collective-permute-start.19 = (f32[3,80,320]{2,1,0:T(8,128)}, f32[3,80,320]{2,1,0:T(8,128)}, u32[]{:S(2)}, u32[]{:S(2)}) collective-permute-start(f32[3,80,320]{2,1,0:T(8,128)} %reduce_sum.28.late), channel_id=1, source_target_pairs={{0,16},{1,17},{2,18},{3,19},{4,20},{5,21},{6,22},{7,23},{8,24},{9,... | collective-permute-start | bytes 921608 | tf_op jit(solution)/shard_map/ppermute | solution.py:36
  160.4 11.5 %collective-permute-start.20 = (f32[192,320]{1,0:T(8,128)}, f32[192,320]{1,0:T(8,128)S(1)}, u32[]{:S(2)}, u32[]{:S(2)}) collective-permute-start(f32[192,320]{1,0:T(8,128)} %pad_maximum_fusion.2), channel_id=1, source_target_pairs={{0,64},{1,65},{2,66},{3,67},{4,68},{5,69},{6,70},{7,71},{8,72},{9,... | collective-permute-start | bytes 737288 | tf_op jit(solution)/shard_map/ppermute | solution.py:36
  162.7 9.2 %collective-permute-start.21 = (f32[80,320]{1,0:T(8,128)}, f32[80,320]{1,0:T(8,128)S(1)}, u32[]{:S(2)}, u32[]{:S(2)}) collective-permute-start(f32[80,320]{1,0:T(8,128)} %slice_reduce_fusion), channel_id=1, source_target_pairs={{0,112},{1,113},{2,114},{3,115},{4,116},{5,117},{6,118},{7,119},{8... | collective-permute-start | bytes 307208 | tf_op jit(solution)/shard_map/ppermute | solution.py:36
  175.1 17.3 %all-to-all-start.2 = ((f32[8,80,320]{2,1,0:T(8,128)}), f32[8,80,320]{2,1,0:T(8,128)S(1)}, u32[]{:S(2)}, u32[]{:S(2)}) async-start(f32[8,80,320]{2,1,0:T(8,128)} %shard_map.61), calls=%async_computation.2 | async-start | bytes 1966080 | tf_op jit(solution)/shard_map/all_to_all | solution.py:579
  181.0 5.9 %collective-permute-start.22 = (f32[64,320]{1,0:T(8,128)S(1)}, f32[64,320]{1,0:T(8,128)S(1)}, u32[]{:S(2)}, u32[]{:S(2)}) collective-permute-start(f32[64,320]{1,0:T(8,128)S(1)} %pad_maximum_fusion.5), channel_id=1, source_target_pairs={{0,8},{1,9},{2,10},{3,11},{4,12},{5,13},{6,14},{7,15},{8,0},{9,1},... | collective-permute-start | bytes 245768 | tf_op jit(solution)/shard_map/ppermute | solution.py:36
  192.5 5.9 %collective-permute-start.23 = (f32[320,320]{1,0:T(8,128)S(1)}, f32[320,320]{1,0:T(8,128)S(1)}, u32[]{:S(2)}, u32[]{:S(2)}) collective-permute-start(f32[320,320]{1,0:T(8,128)S(1)} %constant_dynamic-slice_fusion), channel_id=1, source_target_pairs={{0,8},{1,9},{2,10},{3,11},{4,12},{5,13},{6,14},{7,15},{8,0},{9,1},... | collective-permute-start | bytes 1228808 | tf_op jit(solution)/shard_map/ppermute | solution.py:36
  (22 other events, 141.9 us)

commit v7 on v6

--- a/solution.py
+++ b/solution.py
@@ -526,8 +526,8 @@
         following_a, previous, third_a_s, third_a_s, previous, following_a, weight, partial_energy,
     )
     half_parts = [send(half_pair[1], dx=1), send(half_pair[2], dx=2), send(half_pair[3], dx=-1)]
-    following_b, partner_b, diagonal, kept, half_parts[0], half_parts[2] = together(
-        following_b, partner_b, diagonal, half_pair[0], half_parts[0], half_parts[2]
+    following_b, partner_b, diagonal, kept, half_parts[0], half_parts[1] = together(
+        following_b, partner_b, diagonal, half_pair[0], half_parts[0], half_parts[1]
     )
 
     following_as = send(following_a, dc=1)

time: 203 us -> 206 us (1.015)
  waiting for transfers between devices: 76.5 us -> 82.4 us
  starting transfers between devices: 48.8 us -> 46.7 us
    ppermute x24, waiting for transfers between devices: 34.3 us -> 39.5 us  [send(): return lax.ppermute(block, BOTH, route(dyh, dz, dc, dyl, dx))]
    ppermute x24, starting transfers between devices: 36.4 us -> 32 us  [send(): return lax.ppermute(block, BOTH, route(dyh, dz, dc, dyl, dx))]
    all_to_all x1, starting transfers between devices: 4.03 us -> 6.51 us  [per_device(): lax.all_to_all(pieces, 'freq', 0, 0, tiled=True).reshape(2 * rows, rows)]
  transfers between devices with their start and end apart: 27 -> 27, of which waited for: 12 -> 14; matrix products, arithmetic and copies ran while one was open for 9% -> 9% of each run, Pallas kernels for 18% -> 17%
where the time goes in v7:
time: 206 us; the launch traced here: 205 us
  waiting for transfers between devices  82.4 us (40%)
  Pallas kernels  47.6 us (23%)
  starting transfers between devices  46.7 us (23%)
  other arithmetic  14 us (7%)
  local copies, waits for them, and re-layouts  10.5 us (5%)
  matrix products  3.51 us (2%)
    ppermute x24, waiting for transfers between devices, send(): return lax.ppermute(block, BOTH, route(dyh, dz, dc, dyl, dx))  39.5 us
    ppermute x24, starting transfers between devices, send(): return lax.ppermute(block, BOTH, route(dyh, dz, dc, dyl, dx))  32 us
    all_to_all x1, waiting for transfers between devices, per_device(): late = lax.all_to_all(late, 'freq', 0, 0, tiled=True)  28 us
    pallas_call x2, Pallas kernels, late_tiles(): pl.pallas_call(kernel, in_specs=specs, out_specs=ANY, out_shape=jax.Shape...  18 us
    all_to_all x1, waiting for transfers between devices, summed_along_x(): lax.all_to_all(tiles, 'freq', 0, 0, axis_index_groups=groups, tiled=True)  9.05 us
    pallas_call x1, Pallas kernels, half_tiles(): pl.pallas_call(kernel, in_specs=[SMEM] + [ANY] * (len(operands) - 2) + [V...  8.16 us
    pallas_call x1, Pallas kernels, first_tiles(): pl.pallas_call(first_kernel, in_specs=[SMEM, ANY, ANY, VMEM], out_specs=[...  7.74 us
    pallas_call x1, Pallas kernels, masked_blocks(): pl.pallas_call(mask_kernel, grid_spec=pltpu.PrefetchScalarGridSpec(num_sc...  6.64 us
  transfers between devices with their start and end apart: 27, of which 14 were waited for; matrix products, arithmetic and copies ran while one was open for 9% of the time, Pallas kernels for 17%

profile of v7, /device:TPU:1, one launch (start us, length us, event | category | flops | bytes accessed | tf_op | source)
XLA Modules:
  0.0 205.0 jit_solution(3757862887510951091)
XLA Ops:
  2.1 6.6 %shard_map.55 = (bf16[320,4352]{1,0:T(8,128)(2,1)}, bf16[320,2176]{1,0:T(8,128)(2,1)}, bf16[320,2176]{1,0:T(8,128)(2,1)}, bf16[320,2176]{1,0:T(8,128)(2,1)}, bf16[8,4352]{1,0:T(8,128)(2,1)}) custom-call(s32[15]{0:T(128)} %stack.79.info.refs_0_, bf16[320,8]{1,0:T(8,128)(2,1)} %fusion.6.hot, bf16[320,4352]{1,0:T(8,128)(2,1)} %spectra.1, s32[8,2176]{1,0:T(8,128)} %wedges.1), custom_call_target="tpu_custom_call" | custom-call | flops 1024 | bytes 1024 | tf_op jit(solution)/shard_map/pallas_call | solution.py:93
  10.2 3.8 %collective-permute-start = (bf16[320,2176]{1,0:T(8,128)(2,1)}, bf16[320,2176]{1,0:T(8,128)(2,1)}, u32[]{:S(2)}, u32[]{:S(2)}) collective-permute-start(bf16[320,2176]{1,0:T(8,128)(2,1)} %get-tuple-element.50), channel_id=1, source_target_pairs={{0,48},{1,49},{2,50},{3,51},{4,52},{5,53},{6,54},{7,55},{8,56},{9,... | collective-permute-start | bytes 4177928 | tf_op jit(solution)/shard_map/ppermute | solution.py:36
  14.0 2.9 %collective-permute-start.1 = (bf16[320,2176]{1,0:T(8,128)(2,1)}, bf16[320,2176]{1,0:T(8,128)(2,1)}, u32[]{:S(2)}, u32[]{:S(2)}) collective-permute-start(bf16[320,2176]{1,0:T(8,128)(2,1)} %get-tuple-element.51), channel_id=1, source_target_pairs={{0,64},{1,65},{2,66},{3,67},{4,68},{5,69},{6,70},{7,71},{8,72},{9,... | collective-permute-start | bytes 4177928 | tf_op jit(solution)/shard_map/ppermute | solution.py:36
  20.2 7.7 %shard_map.57 = (f32[4,2,80,320]{3,2,1,0:T(8,128)}, bf16[320,4352]{1,0:T(8,128)(2,1)}) custom-call(s32[15]{0:T(128)} %stack.79.info.refs_0_, bf16[320,4352]{1,0:T(8,128)(2,1)} %get-tuple-element.58.own.refs_2_.refs_5_.refs_1_, bf16[320,4352]{1,0:T(8,128)(2,1)} %collective-permute-done.3.sibling.refs_4_, f32[1,4352]{1,0:T(1,128)} %shard_map.56.weight.refs_13_.refs_11_), custom_call_target="tpu_custom_call" | custom-call | flops 1024 | bytes 1024 | tf_op jit(solution)/shard_map/pallas_call | solution.py:177
  28.0 4.4 %all-to-all-start = ((f32[4,2,80,320]{3,2,1,0:T(8,128)}), f32[4,2,80,320]{3,2,1,0:T(8,128)}, u32[]{:S(2)}, u32[]{:S(2)}) async-start(f32[4,2,80,320]{3,2,1,0:T(8,128)} %get-tuple-element.56), calls=%async_computation | async-start | bytes 1966080 | tf_op jit(solution)/shard_map/all_to_all | solution.py:41
  32.4 3.5 %fusion.refs_14_ = f32[8,320]{1,0:T(8,128)} fusion(bf16[8,4352]{1,0:T(8,128)(2,1)S(1)} %copy-done.18, bf16[320,4352]{1,0:T(8,128)(2,1)S(1)} %copy-done, f32[4352]{0:T(1024)S(1)} %reduce.1), kind=kOutput, calls=%fused_computation | convolution fusion | flops 137871360 | bytes 2882560 | tf_op jit(solution)/shard_map/dot_general | solution.py:512
  37.6 9.1 %all-to-all-done = f32[4,2,80,320]{3,2,1,0:T(8,128)} async-done(((f32[4,2,80,320]{3,2,1,0:T(8,128)}), f32[4,2,80,320]{3,2,1,0:T(8,128)}, u32[]{:S(2)}, u32[]{:S(2)}) %all-to-all-start) | async-done | bytes 819232 | tf_op jit(solution)/shard_map/all_to_all | solution.py:41
  58.3 8.2 %shard_map.58 = (f32[2,168,320]{2,1,0:T(8,128)}, f32[2,168,320]{2,1,0:T(8,128)}, f32[2,168,320]{2,1,0:T(8,128)}, f32[2,168,320]{2,1,0:T(8,128)}) custom-call(s32[15]{0:T(128)} %stack.79.info.refs_0_, bf16[320,2176]{1,0:T(8,128)(2,1)} %collective-permute-done.1.refs_1_.refs_6_.refs_3_, bf16[320,4352]{1,0:T(8,128)(2,1)} %get-tuple-element.58.own.refs_2_.refs_5_.refs_1_, ...), custom_call_target="tpu_custom_call" | custom-call | flops 1024 | bytes 1024 | tf_op jit(solution)/shard_map/pallas_call | solution.py:257
  66.4 2.8 %collective-permute-start.10 = (f32[2,168,320]{2,1,0:T(8,128)}, f32[2,168,320]{2,1,0:T(8,128)S(1)}, u32[]{:S(2)}, u32[]{:S(2)}) collective-permute-start(f32[2,168,320]{2,1,0:T(8,128)} %get-tuple-element.69), channel_id=1, source_target_pairs={{0,2},{1,3},{2,0},{3,1},{4,6},{5,7},{6,4},{7,5},{8,10},{9,11},{10,... | collective-permute-start | bytes 1290248 | tf_op jit(solution)/shard_map/ppermute | solution.py:36
  69.6 15.4 %collective-permute-done.4.refs_6_.refs_8_ = bf16[320,2176]{1,0:T(8,128)(2,1)S(1)} collective-permute-done((bf16[320,2176]{1,0:T(8,128)(2,1)S(1)}, bf16[320,2176]{1,0:T(8,128)(2,1)S(1)}, u32[]{:S(2)}, u32[]{:S(2)}) %collective-permute-start.4) | collective-permute-done | bytes 1392672 | tf_op jit(solution)/shard_map/ppermute | solution.py:36
  86.5 6.4 %collective-permute-done.9 = f32[2,168,320]{2,1,0:T(8,128)S(1)} collective-permute-done((f32[2,168,320]{2,1,0:T(8,128)}, f32[2,168,320]{2,1,0:T(8,128)S(1)}, u32[]{:S(2)}, u32[]{:S(2)}) %collective-permute-start.9) | collective-permute-done | bytes 430112 | tf_op jit(solution)/shard_map/ppermute | solution.py:36
  95.2 8.8 %shard_map.59.refs_12_ = f32[8,3,80,320]{3,2,1,0:T(8,128)} custom-call(s32[15]{0:T(128)} %stack.79.info.refs_0_, bf16[320,4352]{1,0:T(8,128)(2,1)} %get-tuple-element.58.own.refs_2_.refs_5_.refs_1_, bf16[320,4352]{1,0:T(8,128)(2,1)} %get-tuple-element.60.refs_2_, bf16[320,2176]{1,0:T(8,128)(2,1)} %collective-permute-done.1.refs_1_.refs_6_.refs_3_, ...), custom_call_target="tpu_custom_call" | custom-call | flops 1024 | bytes 1024 | tf_op jit(solution)/shard_map/pallas_call | solution.py:375
  104.1 3.8 %collective-permute-done.14 = f32[2,168,320]{2,1,0:T(8,128)} collective-permute-done((f32[2,168,320]{2,1,0:T(8,128)}, f32[2,168,320]{2,1,0:T(8,128)}, u32[]{:S(2)}, u32[]{:S(2)}) %collective-permute-start.14) | collective-permute-done | bytes 430112 | tf_op jit(solution)/shard_map/ppermute | solution.py:36
  110.4 9.2 %shard_map.60 = f32[8,3,80,320]{3,2,1,0:T(8,128)} custom-call(s32[15]{0:T(128)} %stack.79.info.refs_0_, bf16[320,4352]{1,0:T(8,128)(2,1)} %get-tuple-element.58.own.refs_2_.refs_5_.refs_1_, bf16[320,4352]{1,0:T(8,128)(2,1)} %get-tuple-element.60.refs_2_, ...), custom_call_target="tpu_custom_call", output_to_operand_aliasing={{}: (12, {})} | custom-call | flops 1024 | bytes 1024 | tf_op jit(solution)/shard_map/pallas_call | solution.py:375
  119.7 3.9 %all-to-all-start.1 = ((f32[8,3,80,320]{3,2,1,0:T(8,128)}), f32[8,3,80,320]{3,2,1,0:T(8,128)S(1)}, u32[]{:S(2)}, u32[]{:S(2)}) async-start(f32[8,3,80,320]{3,2,1,0:T(8,128)} %shard_map.60), calls=%async_computation.1 | async-start | bytes 5898240 | tf_op jit(solution)/shard_map/all_to_all | solution.py:561
  131.6 28.0 %all-to-all-done.1 = f32[8,3,80,320]{3,2,1,0:T(8,128)S(1)} async-done(((f32[8,3,80,320]{3,2,1,0:T(8,128)}), f32[8,3,80,320]{3,2,1,0:T(8,128)S(1)}, u32[]{:S(2)}, u32[]{:S(2)}) %all-to-all-start.1) | async-done | bytes 2457632 | tf_op jit(solution)/shard_map/all_to_all | solution.py:561
  164.1 4.4 %collective-permute-start.21 = (f32[80,320]{1,0:T(8,128)}, f32[80,320]{1,0:T(8,128)S(1)}, u32[]{:S(2)}, u32[]{:S(2)}) collective-permute-start(f32[80,320]{1,0:T(8,128)} %slice_reduce_fusion), channel_id=1, source_target_pairs={{0,112},{1,113},{2,114},{3,115},{4,116},{5,117},{6,118},{7,119},{8... | collective-permute-start | bytes 307208 | tf_op jit(solution)/shard_map/ppermute | solution.py:36
  168.4 4.1 %collective-permute-done.21.from_diagonal = f32[80,320]{1,0:T(8,128)S(1)} collective-permute-done((f32[80,320]{1,0:T(8,128)}, f32[80,320]{1,0:T(8,128)S(1)}, u32[]{:S(2)}, u32[]{:S(2)}) %collective-permute-start.21) | collective-permute-done | bytes 102432 | tf_op jit(solution)/shard_map/ppermute | solution.py:36
  175.7 6.5 %all-to-all-start.2 = ((f32[8,80,320]{2,1,0:T(8,128)}), f32[8,80,320]{2,1,0:T(8,128)S(1)}, u32[]{:S(2)}, u32[]{:S(2)}) async-start(f32[8,80,320]{2,1,0:T(8,128)} %shard_map.61), calls=%async_computation.2 | async-start | bytes 1966080 | tf_op jit(solution)/shard_map/all_to_all | solution.py:579
  184.1 4.1 %collective-permute-start.22 = (f32[64,320]{1,0:T(8,128)S(1)}, f32[64,320]{1,0:T(8,128)S(1)}, u32[]{:S(2)}, u32[]{:S(2)}) collective-permute-start(f32[64,320]{1,0:T(8,128)S(1)} %pad_maximum_fusion.5), channel_id=1, source_target_pairs={{0,8},{1,9},{2,10},{3,11},{4,12},{5,13},{6,14},{7,15},{8,0},{9,1},... | collective-permute-start | bytes 245768 | tf_op jit(solution)/shard_map/ppermute | solution.py:36
  189.8 5.8 %all-to-all-done.2 = f32[8,80,320]{2,1,0:T(8,128)S(1)} async-done(((f32[8,80,320]{2,1,0:T(8,128)}), f32[8,80,320]{2,1,0:T(8,128)S(1)}, u32[]{:S(2)}, u32[]{:S(2)}) %all-to-all-start.2) | async-done | bytes 819232 | tf_op jit(solution)/shard_map/all_to_all | solution.py:579
  195.7 2.6 %collective-permute-start.23 = (f32[320,320]{1,0:T(8,128)S(1)}, f32[320,320]{1,0:T(8,128)S(1)}, u32[]{:S(2)}, u32[]{:S(2)}) collective-permute-start(f32[320,320]{1,0:T(8,128)S(1)} %constant_dynamic-slice_fusion), channel_id=1, source_target_pairs={{0,8},{1,9},{2,10},{3,11},{4,12},{5,13},{6,14},{7,15},{8,0},{9,1},... | collective-permute-start | bytes 1228808 | tf_op jit(solution)/shard_map/ppermute | solution.py:36
  198.4 3.2 %add_sqrt_fusion.root = f32[320,640]{1,0:T(8,128)} fusion(f32[640]{0:T(1024)S(1)} %get-tuple-element.104, f32[640]{0:T(1024)S(1)} %get-tuple-element.105, f32[640]{0:T(1024)S(1)} %get-tuple-element.106, f32[640]{0:T(1024)S(1)} %get-tuple-element.107, f32[640]{0:T(1024)S(1)} %get-tuple-element.108, f32[640]{0:T(1024)S(1)} %get-tuple-element.109, ...), kind=kLoop, calls=%fused_computation.7 | loop fusion | flops 3686400 | bytes 857600 | tf_op jit(solution)/shard_map/sqrt | solution.py:598
  202.3 2.7 %shard_map.62 = f32[320,640]{1,0:T(8,128)} custom-call(s32[15]{0:T(128)} %stack.79.info.refs_0_, f32[640,320]{1,0:T(8,128)} %bitcast.33, f32[320,320]{1,0:T(8,128)} %copy-done.12, f32[320,640]{1,0:T(8,128)} %add_sqrt_fusion.root), custom_call_target="tpu_custom_call" | custom-call | tf_op jit(solution)/shard_map/pallas_call | solution.py:441
  (115 shorter events, 46.9 us)
Async XLA Ops:
  8.7 11.4 %collective-permute-start.3 = (bf16[320,4352]{1,0:T(8,128)(2,1)}, bf16[320,4352]{1,0:T(8,128)(2,1)}, u32[]{:S(2)}, u32[]{:S(2)}) collective-permute-start(bf16[320,4352]{1,0:T(8,128)(2,1)} %get-tuple-element.58.own.refs_2_.refs_5_.refs_1_), channel_id=1, source_target_pairs={{0,8},{1,9},{2,10},{3,11},{4,12},{5,13},{6,14},{7,15},{8,0},{9,1},... | collective-permute-start | bytes 8355848 | tf_op jit(solution)/shard_map/ppermute | solution.py:36
  10.2 37.8 %collective-permute-start = (bf16[320,2176]{1,0:T(8,128)(2,1)}, bf16[320,2176]{1,0:T(8,128)(2,1)}, u32[]{:S(2)}, u32[]{:S(2)}) collective-permute-start(bf16[320,2176]{1,0:T(8,128)(2,1)} %get-tuple-element.50), channel_id=1, source_target_pairs={{0,48},{1,49},{2,50},{3,51},{4,52},{5,53},{6,54},{7,55},{8,56},{9,... | collective-permute-start | bytes 4177928 | tf_op jit(solution)/shard_map/ppermute | solution.py:36
  14.0 34.0 %collective-permute-start.1 = (bf16[320,2176]{1,0:T(8,128)(2,1)}, bf16[320,2176]{1,0:T(8,128)(2,1)}, u32[]{:S(2)}, u32[]{:S(2)}) collective-permute-start(bf16[320,2176]{1,0:T(8,128)(2,1)} %get-tuple-element.51), channel_id=1, source_target_pairs={{0,64},{1,65},{2,66},{3,67},{4,68},{5,69},{6,70},{7,71},{8,72},{9,... | collective-permute-start | bytes 4177928 | tf_op jit(solution)/shard_map/ppermute | solution.py:36
  16.9 33.0 %collective-permute-start.2 = (bf16[320,2176]{1,0:T(8,128)(2,1)}, bf16[320,2176]{1,0:T(8,128)(2,1)}, u32[]{:S(2)}, u32[]{:S(2)}) collective-permute-start(bf16[320,2176]{1,0:T(8,128)(2,1)} %get-tuple-element.52), channel_id=1, source_target_pairs={{0,16},{1,17},{2,18},{3,19},{4,20},{5,21},{6,22},{7,23},{8,24},{9,... | collective-permute-start | bytes 4177928 | tf_op jit(solution)/shard_map/ppermute | solution.py:36
  28.0 18.7 %all-to-all-start = ((f32[4,2,80,320]{3,2,1,0:T(8,128)}), f32[4,2,80,320]{3,2,1,0:T(8,128)}, u32[]{:S(2)}, u32[]{:S(2)}) async-start(f32[4,2,80,320]{3,2,1,0:T(8,128)} %get-tuple-element.56), calls=%async_computation | async-start | bytes 1966080 | tf_op jit(solution)/shard_map/all_to_all | solution.py:41
  51.6 5.4 %collective-permute-start.8 = (bf16[320,2176]{1,0:T(8,128)(2,1)S(1)}, bf16[320,2176]{1,0:T(8,128)(2,1)S(1)}, u32[]{:S(2)}, u32[]{:S(2)}) collective-permute-start(bf16[320,2176]{1,0:T(8,128)(2,1)S(1)} %broadcast_select_fusion), channel_id=1, source_target_pairs={{0,8},{1,9},{2,10},{3,11},{4,12},{5,13},{6,14},{7,15},{8,0},{9,1},... | collective-permute-start | bytes 4177928 | tf_op jit(solution)/shard_map/ppermute | solution.py:36
  53.2 31.7 %collective-permute-start.4 = (bf16[320,2176]{1,0:T(8,128)(2,1)S(1)}, bf16[320,2176]{1,0:T(8,128)(2,1)S(1)}, u32[]{:S(2)}, u32[]{:S(2)}) collective-permute-start(bf16[320,2176]{1,0:T(8,128)(2,1)S(1)} %copy-done.8), channel_id=1, source_target_pairs={{0,48},{1,49},{2,50},{3,51},{4,52},{5,53},{6,54},{7,55},{8,56},{9,... | collective-permute-start | bytes 4177928 | tf_op jit(solution)/shard_map/ppermute | solution.py:36
  53.6 32.9 %collective-permute-start.5 = (bf16[320,2176]{1,0:T(8,128)(2,1)S(1)}, bf16[320,2176]{1,0:T(8,128)(2,1)S(1)}, u32[]{:S(2)}, u32[]{:S(2)}) collective-permute-start(bf16[320,2176]{1,0:T(8,128)(2,1)S(1)} %copy-done.7), channel_id=1, source_target_pairs={{0,64},{1,65},{2,66},{3,67},{4,68},{5,69},{6,70},{7,71},{8,72},{9,... | collective-permute-start | bytes 4177928 | tf_op jit(solution)/shard_map/ppermute | solution.py:36
  53.7 32.8 %collective-permute-start.6 = (bf16[320,2176]{1,0:T(8,128)(2,1)}, bf16[320,2176]{1,0:T(8,128)(2,1)S(1)}, u32[]{:S(2)}, u32[]{:S(2)}) collective-permute-start(bf16[320,2176]{1,0:T(8,128)(2,1)} %collective-permute-done.1.refs_1_.refs_6_.refs_3_), channel_id=1, source_target_pairs={{0,16},{1,17},{2,18},{3,19},{4,20},{5,21},{6,22},{7,23},{8,24},{9,... | collective-permute-start | bytes 4177928 | tf_op jit(solution)/shard_map/ppermute | solution.py:36
  66.4 20.1 %collective-permute-start.10 = (f32[2,168,320]{2,1,0:T(8,128)}, f32[2,168,320]{2,1,0:T(8,128)S(1)}, u32[]{:S(2)}, u32[]{:S(2)}) collective-permute-start(f32[2,168,320]{2,1,0:T(8,128)} %get-tuple-element.69), channel_id=1, source_target_pairs={{0,2},{1,3},{2,0},{3,1},{4,6},{5,7},{6,4},{7,5},{8,10},{9,11},{10,... | collective-permute-start | bytes 1290248 | tf_op jit(solution)/shard_map/ppermute | solution.py:36
  69.2 23.7 %collective-permute-start.9 = (f32[2,168,320]{2,1,0:T(8,128)}, f32[2,168,320]{2,1,0:T(8,128)S(1)}, u32[]{:S(2)}, u32[]{:S(2)}) collective-permute-start(f32[2,168,320]{2,1,0:T(8,128)} %get-tuple-element.68), channel_id=1, source_target_pairs={{0,1},{1,2},{2,3},{3,0},{4,5},{5,6},{6,7},{7,4},{8,9},{9,10},{10,1... | collective-permute-start | bytes 1290248 | tf_op jit(solution)/shard_map/ppermute | solution.py:36
  84.9 19.1 %collective-permute-start.11 = (bf16[320,2176]{1,0:T(8,128)(2,1)}, bf16[320,2176]{1,0:T(8,128)(2,1)}, u32[]{:S(2)}, u32[]{:S(2)}) collective-permute-start(bf16[320,2176]{1,0:T(8,128)(2,1)} %collective-permute-done.refs_7_.refs_12_.refs_5_), channel_id=1, source_target_pairs={{0,8},{1,9},{2,10},{3,11},{4,12},{5,13},{6,14},{7,15},{8,0},{9,1},... | collective-permute-start | bytes 4177928 | tf_op jit(solution)/shard_map/ppermute | solution.py:36
  93.0 15.0 %collective-permute-start.12 = (bf16[320,2176]{1,0:T(8,128)(2,1)S(1)}, bf16[320,2176]{1,0:T(8,128)(2,1)}, u32[]{:S(2)}, u32[]{:S(2)}) collective-permute-start(bf16[320,2176]{1,0:T(8,128)(2,1)S(1)} %collective-permute-done.4.refs_6_.refs_8_), channel_id=1, source_target_pairs={{0,8},{1,9},{2,10},{3,11},{4,12},{5,13},{6,14},{7,15},{8,0},{9,1},... | collective-permute-start | bytes 4177928 | tf_op jit(solution)/shard_map/ppermute | solution.py:36
  93.7 14.2 %collective-permute-start.13 = (bf16[320,2176]{1,0:T(8,128)(2,1)S(1)}, bf16[320,2176]{1,0:T(8,128)(2,1)}, u32[]{:S(2)}, u32[]{:S(2)}) collective-permute-start(bf16[320,2176]{1,0:T(8,128)(2,1)S(1)} %collective-permute-done.6.refs_9_.refs_10_), channel_id=1, source_target_pairs={{0,8},{1,9},{2,10},{3,11},{4,12},{5,13},{6,14},{7,15},{8,0},{9,1},... | collective-permute-start | bytes 4177928 | tf_op jit(solution)/shard_map/ppermute | solution.py:36
  94.2 13.7 %collective-permute-start.14 = (f32[2,168,320]{2,1,0:T(8,128)}, f32[2,168,320]{2,1,0:T(8,128)}, u32[]{:S(2)}, u32[]{:S(2)}) collective-permute-start(f32[2,168,320]{2,1,0:T(8,128)} %get-tuple-element.76), channel_id=1, source_target_pairs={{0,3},{1,0},{2,1},{3,2},{4,7},{5,4},{6,5},{7,6},{8,11},{9,8},{10,9... | collective-permute-start | bytes 1290248 | tf_op jit(solution)/shard_map/ppermute | solution.py:36
  109.9 9.8 %collective-permute-start.15 = (f32[248,320]{1,0:T(8,128)S(1)}, f32[248,320]{1,0:T(8,128)}, u32[]{:S(2)}, u32[]{:S(2)}) collective-permute-start(f32[248,320]{1,0:T(8,128)S(1)} %pad_maximum_fusion), channel_id=1, source_target_pairs={{0,4},{1,5},{2,6},{3,7},{4,0},{5,1},{6,2},{7,3},{8,12},{9,13},{10,... | collective-permute-start | bytes 952328 | tf_op jit(solution)/shard_map/ppermute | solution.py:36
  119.7 40.0 %all-to-all-start.1 = ((f32[8,3,80,320]{3,2,1,0:T(8,128)}), f32[8,3,80,320]{3,2,1,0:T(8,128)S(1)}, u32[]{:S(2)}, u32[]{:S(2)}) async-start(f32[8,3,80,320]{3,2,1,0:T(8,128)} %shard_map.60), calls=%async_computation.1 | async-start | bytes 5898240 | tf_op jit(solution)/shard_map/all_to_all | solution.py:561
  125.5 5.5 %collective-permute-start.18 = (f32[88,320]{1,0:T(8,128)S(1)}, f32[88,320]{1,0:T(8,128)S(1)}, u32[]{:S(2)}, u32[]{:S(2)}) collective-permute-start(f32[88,320]{1,0:T(8,128)S(1)} %pad_maximum_fusion.4), channel_id=1, source_target_pairs={{0,16},{1,17},{2,18},{3,19},{4,20},{5,21},{6,22},{7,23},{8,24},{9,... | collective-permute-start | bytes 337928 | tf_op jit(solution)/shard_map/ppermute | solution.py:36
  161.5 10.9 %collective-permute-start.19 = (f32[3,80,320]{2,1,0:T(8,128)}, f32[3,80,320]{2,1,0:T(8,128)}, u32[]{:S(2)}, u32[]{:S(2)}) collective-permute-start(f32[3,80,320]{2,1,0:T(8,128)} %reduce_sum.28.late), channel_id=1, source_target_pairs={{0,16},{1,17},{2,18},{3,19},{4,20},{5,21},{6,22},{7,23},{8,24},{9,... | collective-permute-start | bytes 921608 | tf_op jit(solution)/shard_map/ppermute | solution.py:36
  162.4 10.1 %collective-permute-start.20 = (f32[192,320]{1,0:T(8,128)}, f32[192,320]{1,0:T(8,128)S(1)}, u32[]{:S(2)}, u32[]{:S(2)}) collective-permute-start(f32[192,320]{1,0:T(8,128)} %pad_maximum_fusion.2), channel_id=1, source_target_pairs={{0,64},{1,65},{2,66},{3,67},{4,68},{5,69},{6,70},{7,71},{8,72},{9,... | collective-permute-start | bytes 737288 | tf_op jit(solution)/shard_map/ppermute | solution.py:36
  164.1 8.4 %collective-permute-start.21 = (f32[80,320]{1,0:T(8,128)}, f32[80,320]{1,0:T(8,128)S(1)}, u32[]{:S(2)}, u32[]{:S(2)}) collective-permute-start(f32[80,320]{1,0:T(8,128)} %slice_reduce_fusion), channel_id=1, source_target_pairs={{0,112},{1,113},{2,114},{3,115},{4,116},{5,117},{6,118},{7,119},{8... | collective-permute-start | bytes 307208 | tf_op jit(solution)/shard_map/ppermute | solution.py:36
  175.7 19.9 %all-to-all-start.2 = ((f32[8,80,320]{2,1,0:T(8,128)}), f32[8,80,320]{2,1,0:T(8,128)S(1)}, u32[]{:S(2)}, u32[]{:S(2)}) async-start(f32[8,80,320]{2,1,0:T(8,128)} %shard_map.61), calls=%async_computation.2 | async-start | bytes 1966080 | tf_op jit(solution)/shard_map/all_to_all | solution.py:579
  184.1 5.6 %collective-permute-start.22 = (f32[64,320]{1,0:T(8,128)S(1)}, f32[64,320]{1,0:T(8,128)S(1)}, u32[]{:S(2)}, u32[]{:S(2)}) collective-permute-start(f32[64,320]{1,0:T(8,128)S(1)} %pad_maximum_fusion.5), channel_id=1, source_target_pairs={{0,8},{1,9},{2,10},{3,11},{4,12},{5,13},{6,14},{7,15},{8,0},{9,1},... | collective-permute-start | bytes 245768 | tf_op jit(solution)/shard_map/ppermute | solution.py:36
  195.7 5.9 %collective-permute-start.23 = (f32[320,320]{1,0:T(8,128)S(1)}, f32[320,320]{1,0:T(8,128)S(1)}, u32[]{:S(2)}, u32[]{:S(2)}) collective-permute-start(f32[320,320]{1,0:T(8,128)S(1)} %constant_dynamic-slice_fusion), channel_id=1, source_target_pairs={{0,8},{1,9},{2,10},{3,11},{4,12},{5,13},{6,14},{7,15},{8,0},{9,1},... | collective-permute-start | bytes 1228808 | tf_op jit(solution)/shard_map/ppermute | solution.py:36
  (22 other events, 152.3 us)
